TPU v7x, 128 devices: a whole 4x4x4 slice. The times are simulated.
128 devices in a mesh: tmpl: 16 (over x, z_lo, core), seg: 8 (over z_hi, y).
Axes of the slice: x: 4, y: 4, z: 4 (z_hi: 2, z_lo: 2; z = z_hi * 2 + z_lo), core: 2. Of those that a mesh axis runs over, the one named last changes fastest.
Arguments:
- strain: float32 [2, 1024, 1024], P(None, 'seg'), may hold values from -6 to 6
- gate_start: int32 [2, 8, 2], P(None, 'seg'), may hold values from 0 to 131071
- gate_span: int32 [2, 8, 2], P(None, 'seg'), may hold values from 1 to 4096
- asd: float32 [1024, 1024], P(None, 'seg'), may hold values from 0.5 to 2
- bank: float32 [2, 32, 1024, 1024], P(None, None, 'tmpl', 'seg'), may hold values from -6 to 6
- assign: int32 [32], replicated, may hold values from 0 to 31, each once
Outputs:
- snr: float32 [2, 32, 1024, 1024], P(None, 'tmpl', None, 'seg')
Inputs may be any that keep to these rules, and one draw needn't show every extreme that they name: `assign`: every template number appears exactly once.
All inputs are finite; a program needn't handle non-finite values.
Results may differ from a plain program's by a relative error of at most 0.0037.
Values may be sent and summed in bfloat16 or wider, within the bound.
No kernel may reach another device: no remote copies, remote signals or barrier semaphores. Data moves between devices by JAX's collectives and lax.ppermute only.
A program may use at most 128 MiB of HBM per device.

v0:
```python
import functools
import math

import jax
import jax.numpy as jnp
import numpy as np
from jax import lax
from jax.experimental import pallas as pl
from jax.experimental.pallas import tpu as pltpu
from jax.sharding import PartitionSpec as P

BF = jnp.bfloat16
F32 = jnp.float32
NSAMP = 1048576
VMEM = pl.BlockSpec(memory_space=pltpu.VMEM)
SMEM = pl.BlockSpec(memory_space=pltpu.SMEM)
ANY = pl.BlockSpec(memory_space=pl.ANY)
MIB = 1 << 20


def phases(product, count):
    angle = 2.0 * math.pi / count * (product % count).astype(np.float64)
    return np.cos(angle), np.sin(angle)


def split_hi_lo(table):
    table = table.astype(np.float32)
    hi = table.astype(jnp.bfloat16)
    lo = (table - hi.astype(np.float32)).astype(jnp.bfloat16)
    return hi, lo


@functools.cache
def tables():
    q = np.arange(256)
    select = np.zeros((2, 256, 128), np.float32)
    for core in range(2):
        for seg in range(2):
            for j in range(64):
                select[core, seg * 128 + core * 64 + j, seg * 64 + (j % 4) * 16 + j // 4] = 1.0
    order = np.zeros((128, 128), np.float32)
    for m in range(128):
        order[(m % 4) * 32 + m // 4, m] = 1.0
    first = []
    for r in range(4):
        c, s = phases((4 * q[:, None] + r) * q[None, :], 1024)
        first.append(np.stack([np.stack(split_hi_lo(c)), np.stack(split_hi_lo(-s))]))
    rows = np.array([4 * (i % 16) + i // 16 for i in range(64)])
    k2 = np.arange(1024)
    c, s = phases(rows[:, None] * k2[None, :], NSAMP)
    fine = np.stack([c, -s]).astype(np.float32)
    c, s = phases(64 * np.arange(16)[:, None] * k2[None, :], NSAMP)
    base = np.stack([c, -s]).astype(np.float32)
    n1 = np.array([128 * s + 64 * c + 4 * j for c in range(2) for s in range(8) for j in range(16)])
    second = []
    for r in range(4):
        c, s = phases(q[:, None] * (n1 + r)[None, :], 1024)
        (ch, cl), (sh, sl) = split_hi_lo(c), split_hi_lo(s)
        second.append(np.concatenate([ch, sh, cl, sl], axis=1))
    third = []
    for p in range(4):
        c, s = phases(q[:, None] * (4 * q[None, :] + p), 1024)
        c, s = c.astype(np.float32), s.astype(np.float32)
        third.append(np.stack([np.concatenate([c, -s], 1), np.concatenate([s, c], 1)]))
    c, s = phases(np.arange(1024)[:, None] * k2[None, :], NSAMP)
    back = np.stack([c, s]).astype(np.float32).reshape(2, 1024, 8, 128).transpose(2, 0, 1, 3)
    last = []
    for p in range(4):
        c, s = phases((4 * q[:, None] + p) * q[None, :], 1024)
        last.append(np.stack([c, s]).astype(np.float32))
    return dict(
        select=select.astype(jnp.bfloat16),
        order=order.astype(jnp.bfloat16),
        first=np.stack(first),
        fine=fine,
        base=base,
        second=np.stack(second),
        third=np.stack(third).astype(jnp.bfloat16),
        back=np.ascontiguousarray(back),
        last=np.stack(last).astype(jnp.bfloat16),
    )


def dot(a, b):
    return jnp.dot(a, b, preferred_element_type=F32)


def dot_nt(a, b):
    return lax.dot_general(a, b, (((1,), (1,)), ((), ())), preferred_element_type=F32)


def place():
    t = lax.axis_index("tmpl")
    return t // 4, (t // 2) % 2, t % 2


def gate_kernel(strain_ref, start_ref, span_ref, select_ref, order_ref, out_ref):
    _, _, core = place()
    pick = select_ref[core]
    order = order_ref[...]
    lane = lax.broadcasted_iota(jnp.int32, (128, 128), 1)
    row = lax.broadcasted_iota(jnp.int32, (128, 128), 0)
    for dest in range(8):
        cols = slice(128 * dest, 128 * dest + 128)
        sample = row * 1024 + lane + 128 * dest
        both = []
        for seg in range(2):
            value = strain_ref[seg, :, cols]
            for g in range(2):
                first = start_ref[seg, 0, g]
                inside = (sample >= first) & (sample < first + span_ref[seg, 0, g])
                value = jnp.where(inside, 0.0, value)
            both.append(value.astype(BF))
        picked = dot(jnp.concatenate(both, axis=1), pick).astype(BF)
        out_ref[dest] = dot(order, picked).astype(BF)


def pick_kernel(assign_ref, bank_ref, near_ref, cross_ref):
    x, z, core = place()

    def body(i, carry):
        rz, rx = i // 4, i % 4
        for rc in range(2):
            dest = ((x + rx) % 4) * 4 + (z + rz) % 2 * 2 + (core + rc) % 2
            for slot in range(2):
                chosen = assign_ref[2 * dest + slot]
                for part in range(2):
                    for p in range(4):
                        value = bank_ref[part, chosen, pl.ds(p, 16, stride=4), :].astype(BF)
                        if rc == 1:
                            cross_ref[rz, rx, slot, part, p] = value
                        else:
                            near_ref[rz, rx, slot, part, p] = value
        return carry

    lax.fori_loop(0, 8, body, 0)


def four_way(sign, parts):
    (ar, ai), (br, bi), (cr, ci), (dr, di) = parts
    sr, si = ar + cr, ai + ci
    tr, ti = ar - cr, ai - ci
    ur, ui = br + dr, bi + di
    vr, vi = br - dr, bi - di
    if sign > 0:
        wr, wi = -vi, vr
    else:
        wr, wi = vi, -vr
    return ((sr + ur, si + ui), (tr + wr, ti + wi), (sr - ur, si - ui), (tr - wr, ti - wi))


def first_kernel(cols_ref, table_ref, fine_ref, base_ref, out_ref, z_ref):
    _, _, core = place()
    group = 2 * lax.axis_index("seg") + core
    for r in range(4):
        piece = cols_ref[:, 32 * r : 32 * r + 32, :].reshape(256, 128)
        turned = piece.T
        for part in range(2):
            z_ref[r, part] = dot(turned, table_ref[r, part, 0]) + dot(turned, table_ref[r, part, 1])
    base_re = base_ref[0, pl.ds(group, 1), :]
    base_im = base_ref[1, pl.ds(group, 1), :]
    for r1 in range(4):
        rows = slice(16 * r1, 16 * r1 + 16)
        fr, fi = fine_ref[0, rows, :], fine_ref[1, rows, :]
        tr = fr * base_re - fi * base_im
        ti = fr * base_im + fi * base_re
        for seg in range(2):
            here = slice(64 * seg + 16 * r1, 64 * seg + 16 * r1 + 16)
            outs = four_way(-1, [(z_ref[r, 0, here, :], z_ref[r, 1, here, :]) for r in range(4)])
            for k, (re, im) in enumerate(outs):
                wr, wi = tr[:, 256 * k : 256 * k + 256], ti[:, 256 * k : 256 * k + 256]
                done = ((re * wr - im * wi).astype(BF), (re * wi + im * wr).astype(BF))
                for half in range(2):
                    for part in range(2):
                        out_ref[2 * k + half, part, seg, r1] = done[part][:, 128 * half : 128 * half + 128]


def filter_kernel(
    own_ref, other_ref, near_ref, cross_ref, side_ref, x1_ref, x2_ref, x3_ref, asd_ref, second_ref, third_ref, back_ref,
    out_ref,
    bank, twist, z_ref, spec, v_ref, sems,
):
    x, z, core = place()
    copies = []
    for rz in range(2):
        for rc in range(2):
            own = ((near_ref, cross_ref)[rc].at[0, 0]) if rz == 0 else side_ref.at[rc, 0]
            for dx, src in enumerate((own, x1_ref.at[rz, rc], x2_ref.at[rz, rc], x3_ref.at[rz, rc])):
                origin = ((x + 4 - dx) % 4) * 4 + (z + rz) % 2 * 2 + (core + rc) % 2
                copies.append(pltpu.make_async_copy(src, bank.at[origin], sems.at[len(copies)]))
    copies.append(pltpu.make_async_copy(back_ref.at[lax.axis_index("seg")], twist, sems.at[16]))
    for copy in copies:
        copy.start()
    low = core == 0
    for r in range(4):
        parts = []
        for part in range(2):
            lanes = []
            for seg in range(2):
                mine = own_ref[:, part, seg, r].reshape(128, 128)
                theirs = other_ref[:, part, seg, r].reshape(128, 128)
                lanes.append(
                    jnp.concatenate([jnp.where(low, mine, theirs), jnp.where(low, theirs, mine)], axis=0)
                )
            parts.append(jnp.concatenate(lanes, axis=1))
        re, im = parts
        table = second_ref[r]
        for part, stack in enumerate(([re, im], [im, -re])):
            right = jnp.concatenate(stack, axis=0)
            z_ref[r, part] = dot(table[:, :512], right) + dot(table[:, 512:], right)
    for i in range(8):
        rows = slice(32 * i, 32 * i + 32)
        outs = four_way(-1, [(z_ref[r, 0, rows, :], z_ref[r, 1, rows, :]) for r in range(4)])
        for k, (re, im) in enumerate(outs):
            here = slice(256 * k + 32 * i, 256 * k + 32 * i + 32)
            for seg in range(2):
                cols = slice(128 * seg, 128 * seg + 128)
                spec[0, seg, here, :] = re[:, cols]
                spec[1, seg, here, :] = im[:, cols]
    for copy in copies:
        copy.wait()
    norms = [jnp.zeros((8, 128), F32), jnp.zeros((8, 128), F32)]
    for p in range(4):
        asd = asd_ref[pl.ds(p, 256, stride=4), :]
        weight = 1.0 / (asd * asd)
        lanes_re, lanes_im = [], []
        heard = []
        for seg in range(2):
            heard.append([spec[part, seg, pl.ds(p, 256, stride=4), :] * weight for part in range(2)])
        for slot in range(2):
            hr = bank[:, slot, 0, p].reshape(256, 128).astype(F32)
            hi = bank[:, slot, 1, p].reshape(256, 128).astype(F32)
            power = (hr * hr + hi * hi) * weight
            norms[slot] = norms[slot] + power.reshape(32, 8, 128).sum(axis=0)
            for seg in range(2):
                sr, si = heard[seg]
                lanes_re.append((sr * hr + si * hi).astype(BF))
                lanes_im.append((si * hr - sr * hi).astype(BF))
        right = jnp.concatenate([jnp.concatenate(lanes_re, axis=1), jnp.concatenate(lanes_im, axis=1)], axis=0)
        v_ref[p, 0] = dot(third_ref[p, 0], right)
        v_ref[p, 1] = dot(third_ref[p, 1], right)
    for i in range(8):
        rows = slice(32 * i, 32 * i + 32)
        half, inside = i // 4, (i % 4) * 32
        for pair in range(4):
            slot, seg = pair // 2, pair % 2
            cols = slice(128 * pair, 128 * pair + 128)
            outs = four_way(1, [(v_ref[p, 0, rows, cols], v_ref[p, 1, rows, cols]) for p in range(4)])
            for k, (re, im) in enumerate(outs):
                wr = twist[0, 256 * k + 32 * i : 256 * k + 32 * i + 32, :]
                wi = twist[1, 256 * k + 32 * i : 256 * k + 32 * i + 32, :]
                at = (seg * 2 + slot) * 256 + inside
                out_ref[2 * k + half, at : at + 32, :] = (re * wr - im * wi).astype(BF)
                out_ref[2 * k + half, at + 128 : at + 160, :] = (re * wi + im * wr).astype(BF)
    row = lax.broadcasted_iota(jnp.int32, (16, 128), 0)
    tail = jnp.zeros((16, 128), F32)
    for slot in range(2):
        left = jnp.broadcast_to(norms[slot].sum(axis=0, keepdims=True), (16, 128))
        for piece in range(3):
            rounded = left.astype(BF).astype(F32)
            tail = jnp.where(row == 3 * slot + piece, rounded, tail)
            left = left - rounded
    for dest in range(8):
        out_ref[dest, 1024:1040, :] = tail.astype(BF)


def last_kernel(in_ref, table_ref, out_ref):
    total = jnp.zeros((16, 128), F32)
    for s in range(8):
        total = total + in_ref[s, 1024:1040, :].astype(F32)
    row = lax.broadcasted_iota(jnp.int32, (16, 128), 0)
    scales = []
    for slot in range(2):
        mine = (row >= 3 * slot) & (row < 3 * slot + 3)
        sigma2 = jnp.sum(jnp.where(mine, total, 0.0), axis=(0, 1), keepdims=True)
        scales.append(1.0 / jnp.sqrt(NSAMP * sigma2))
    for pair in range(4):
        seg, slot = pair // 2, pair % 2
        at = 256 * pair
        parts = []
        for r in range(4):
            both = jnp.concatenate([in_ref[2 * r, at : at + 256, :], in_ref[2 * r + 1, at : at + 256, :]], axis=1)
            both = both.astype(F32)
            parts.append((both[:128], both[128:]))
        outs = four_way(1, parts)
        for p, (re, im) in enumerate(outs):
            right = jnp.concatenate([re, im], axis=0)
            hi = right.astype(BF)
            lo = (right - hi.astype(F32)).astype(BF)
            cos = dot_nt(table_ref[p, 0], hi) + dot_nt(table_ref[p, 0], lo)
            sin = dot_nt(table_ref[p, 1], hi) + dot_nt(table_ref[p, 1], lo)
            sr = cos[:, :128] - sin[:, 128:]
            si = sin[:, :128] + cos[:, 128:]
            out_ref[seg, slot, pl.ds(p, 256, stride=4), :] = jnp.sqrt(sr * sr + si * si) * scales[slot]


def call(kernel, ins, outs, specs, flops, moved, scratch=(), limit=32):
    return pl.pallas_call(
        kernel,
        out_shape=outs,
        in_specs=specs,
        out_specs=jax.tree.map(lambda _: VMEM, outs),
        scratch_shapes=list(scratch),
        compiler_params=pltpu.CompilerParams(vmem_limit_bytes=limit * MIB),
        cost_estimate=pl.CostEstimate(flops=flops, bytes_accessed=moved, transcendentals=0),
    )(*ins)


def shape(*dims, dtype=BF):
    return jax.ShapeDtypeStruct(dims, dtype)


def per_device(strain, gate_start, gate_span, asd, bank, assign):
    const = {name: jnp.asarray(value) for name, value in tables().items()}
    swap_core = [(i, i ^ 1) for i in range(16)]
    swap_z = [(i, i ^ 2) for i in range(16)]

    gated = call(
        gate_kernel, (strain, gate_start, gate_span, const["select"], const["order"]), shape(8, 128, 128),
        [VMEM, SMEM, SMEM, VMEM, VMEM], 10**8, 2 * MIB,
    )
    columns = lax.all_to_all(gated, "seg", 0, 0)

    blk = (2, 2, 4, 16, 128)
    near, cross = call(
        pick_kernel, (assign, bank),
        (shape(2, 4, *blk), shape(2, 4, *blk)), [SMEM, VMEM], 10**8, 3 * MIB,
    )
    cross = lax.ppermute(cross, "tmpl", swap_core)
    side = lax.ppermute(jnp.stack([near[1], cross[1]]), "tmpl", swap_z)
    rounds = []
    for dx in range(1, 4):
        send = jnp.stack([jnp.stack([near[0, dx], cross[0, dx]]), side[:, dx]])
        hop = [(i, (i // 4 + dx) % 4 * 4 + i % 4) for i in range(16)]
        rounds.append(lax.ppermute(send, "tmpl", hop))

    turned = call(
        first_kernel, (columns, const["first"], const["fine"], const["base"]), shape(8, 2, 2, 4, 16, 128),
        [VMEM] * 4, 3 * 10**8, 4 * MIB, [pltpu.VMEM((4, 2, 128, 256), F32)],
    )
    own = lax.all_to_all(turned, "seg", 0, 0)
    other = lax.ppermute(own, "tmpl", swap_core)

    inner = call(
        filter_kernel,
        (own, other, near, cross, side, *rounds, asd, const["second"], const["third"], const["back"]),
        shape(8, 1040, 128),
        [VMEM] * 2 + [ANY] * 6 + [VMEM] * 3 + [ANY],
        3 * 10**9, 10 * MIB,
        [
            pltpu.VMEM((16, *blk), BF),
            pltpu.VMEM((2, 1024, 128), F32),
            pltpu.VMEM((4, 2, 256, 256), F32),
            pltpu.VMEM((2, 2, 1024, 128), F32),
            pltpu.VMEM((4, 2, 256, 512), F32),
            pltpu.SemaphoreType.DMA((17,)),
        ],
    )
    series = lax.all_to_all(inner, "seg", 0, 0)
    return call(
        last_kernel, (series, const["last"]), shape(2, 2, 1024, 128, dtype=F32), [VMEM] * 2, 3 * 10**9, 6 * MIB
    )


def solution(mesh):
    placed = (
        P(None, "seg", None),
        P(None, "seg", None),
        P(None, "seg", None),
        P(None, "seg"),
        P(None, None, "tmpl", "seg"),
        P(),
    )
    return jax.shard_map(
        per_device,
        mesh=mesh,
        in_specs=placed,
        out_specs=P(None, "tmpl", None, "seg"),
        check_vma=False,
    )
```

profile of v0, /device:TPU:0, one launch (start us, length us, event | category | flops | bytes accessed | tf_op | source)
XLA Modules:
  0.0 117.5 jit_solution(8250410307648052858)
XLA Ops:
  0.0 1.7 %copy-done.4 = f32[2,32,64,128]{3,2,1,0:T(8,128)S(1)} copy-done((f32[2,32,64,128]{3,2,1,0:T(8,128)S(1)}, f32[2,32,64,128]{3,2,1,0:T(8,128)}, u32[]{:S(2)}) %copy-start.4) | copy-done | bytes 2097176
  1.7 0.7 copy-done.13
  2.4 1.7 %shard_map.147 = (bf16[2,4,2,2,4,16,128]{6,5,4,3,2,1,0:T(8,128)(2,1)S(1)}, bf16[2,4,2,2,4,16,128]{6,5,4,3,2,1,0:T(8,128)(2,1)}) custom-call(s32[32]{0:T(128)S(1)} %copy-done.13, f32[2,32,64,128]{3,2,1,0:T(8,128)S(1)} %copy-done.4), custom_call_target="tpu_custom_call" | custom-call | flops 100000000 | bytes 3145728 | tf_op jit(solution)/shard_map/pallas_call | solution.py:298
  4.1 1.2 %copy-done.5 = f32[2,128,1024]{2,1,0:T(8,128)S(1)} copy-done((f32[2,128,1024]{2,1,0:T(8,128)S(1)}, f32[2,128,1024]{2,1,0:T(8,128)}, u32[]{:S(2)}) %copy-start.5) | copy-done | bytes 1048600
  5.3 0.9 copy-done.9
  6.2 0.8 copy-done.10
  7.0 2.8 %shard_map.145 = bf16[8,128,128]{2,1,0:T(8,128)(2,1)} custom-call(f32[2,128,1024]{2,1,0:T(8,128)S(1)} %copy-done.5, s32[2,1,2]{2,1,0:T(1,128)S(1)} %copy-done.11, s32[2,1,2]{2,1,0:T(1,128)S(1)} %copy-done.12, bf16[2,256,128]{2,1,0:T(8,128)(2,1)S(1)} %copy-done.9, bf16[128,128]{1,0:T(8,128)(2,1)S(1)} %copy-done.10), custom_call_target="tpu_custom_call" | custom-call | flops 100000000 | bytes 2097152 | tf_op jit(solution)/shard_map/pallas_call | solution.py:298
  9.7 7.9 %all-to-all-start = ((bf16[8,128,128]{2,1,0:T(8,128)(2,1)}), bf16[8,128,128]{2,1,0:T(8,128)(2,1)S(1)}, u32[]{:S(2)}, u32[]{:S(2)}) async-start(bf16[8,128,128]{2,1,0:T(8,128)(2,1)} %shard_map.145), calls=%async_computation | async-start | bytes 524288 | tf_op jit(solution)/shard_map/all_to_all | solution.py:322
  17.6 0.6 slice_bitcast_fusion.6
  18.3 8.8 %all-to-all-done.cols_ref = bf16[8,128,128]{2,1,0:T(8,128)(2,1)S(1)} async-done(((bf16[8,128,128]{2,1,0:T(8,128)(2,1)}), bf16[8,128,128]{2,1,0:T(8,128)(2,1)S(1)}, u32[]{:S(2)}, u32[]{:S(2)}) %all-to-all-start) | async-done | bytes 262176 | tf_op jit(solution)/shard_map/all_to_all | solution.py:322
  27.1 1.0 copy-done.7
  28.1 1.4 %shard_map.146 = bf16[8,2,2,4,16,128]{5,4,3,2,1,0:T(8,128)(2,1)} custom-call(bf16[8,128,128]{2,1,0:T(8,128)(2,1)S(1)} %all-to-all-done.cols_ref, bf16[4,2,2,256,256]{4,3,2,1,0:T(8,128)(2,1)S(1)} %copy-done.3, f32[2,64,1024]{2,1,0:T(8,128)S(1)} %copy-done.7, f32[2,16,1024]{2,1,0:T(8,128)S(1)} %copy-done.8), custom_call_target="tpu_custom_call" | custom-call | flops 300000000 | bytes 4194304 | tf_op jit(solution)/shard_map/pallas_call | solution.py:298
  29.5 3.5 %all-to-all-start.1 = ((bf16[8,2,2,4,16,128]{5,4,3,2,1,0:T(8,128)(2,1)}), bf16[8,2,2,4,16,128]{5,4,3,2,1,0:T(8,128)(2,1)S(1)}, u32[]{:S(2)}, u32[]{:S(2)}) async-start(bf16[8,2,2,4,16,128]{5,4,3,2,1,0:T(8,128)(2,1)} %shard_map.146), calls=%async_computation.1 | async-start | bytes 1048576 | tf_op jit(solution)/shard_map/all_to_all | solution.py:341
  33.1 1.0 slice.44
  34.1 0.1 pad_maximum_fusion
  34.1 0.9 copy.16
  35.0 1.0 collective-permute-start.2
  36.0 0.9 slice_bitcast_fusion.3
  37.0 7.8 %all-to-all-done.1.own_ref = bf16[8,2,2,4,16,128]{5,4,3,2,1,0:T(8,128)(2,1)S(1)} async-done(((bf16[8,2,2,4,16,128]{5,4,3,2,1,0:T(8,128)(2,1)}), bf16[8,2,2,4,16,128]{5,4,3,2,1,0:T(8,128)(2,1)S(1)}, u32[]{:S(2)}, u32[]{:S(2)}) %all-to-all-start.1) | async-done | bytes 524320 | tf_op jit(solution)/shard_map/all_to_all | solution.py:341
  44.8 7.6 %collective-permute-done.2 = bf16[2,4,2,2,4,16,128]{6,5,4,3,2,0,1:T(8,128)(2,1)} collective-permute-done((bf16[2,4,2,2,4,16,128]{6,5,4,3,2,0,1:T(8,128)(2,1)}, bf16[2,4,2,2,4,16,128]{6,5,4,3,2,0,1:T(8,128)(2,1)}, u32[]{:S(2)}, u32[]{:S(2)}) %collective-permute-start.2) | collective-permute-done | bytes 524320 | tf_op jit(solution)/shard_map/ppermute | solution.py:330
  52.4 1.1 slice_bitcast_fusion
  53.4 1.6 %collective-permute-start.3 = (bf16[2,2,2,2,4,16,128]{6,5,4,3,2,1,0:T(8,128)(2,1)S(1)}, bf16[2,2,2,2,4,16,128]{6,5,4,3,2,1,0:T(8,128)(2,1)S(1)}, u32[]{:S(2)}, u32[]{:S(2)}) collective-permute-start(bf16[2,2,2,2,4,16,128]{6,5,4,3,2,1,0:T(8,128)(2,1)S(1)} %pad_maximum_fusion.1), channel_id=1, source_target_pairs={{0,32},{8,40},{16,48},{24,56},{32,64},{40,72},{48,80},{56,88},{64,... | collective-permute-start | bytes 786440 | tf_op jit(solution)/shard_map/ppermute | solution.py:335
  55.0 2.8 %collective-permute-start.4 = (bf16[2,2,2,2,4,16,128]{6,5,4,3,2,1,0:T(8,128)(2,1)S(1)}, bf16[2,2,2,2,4,16,128]{6,5,4,3,2,1,0:T(8,128)(2,1)S(1)}, u32[]{:S(2)}, u32[]{:S(2)}) collective-permute-start(bf16[2,2,2,2,4,16,128]{6,5,4,3,2,1,0:T(8,128)(2,1)S(1)} %pad_maximum_fusion.2), channel_id=1, source_target_pairs={{0,64},{8,72},{16,80},{24,88},{32,96},{40,104},{48,112},{56,120},{... | collective-permute-start | bytes 786440 | tf_op jit(solution)/shard_map/ppermute | solution.py:335
  57.9 1.5 %collective-permute-start.5 = (bf16[2,2,2,2,4,16,128]{6,5,4,3,2,1,0:T(8,128)(2,1)S(1)}, bf16[2,2,2,2,4,16,128]{6,5,4,3,2,1,0:T(8,128)(2,1)S(1)}, u32[]{:S(2)}, u32[]{:S(2)}) collective-permute-start(bf16[2,2,2,2,4,16,128]{6,5,4,3,2,1,0:T(8,128)(2,1)S(1)} %pad_maximum_fusion.3), channel_id=1, source_target_pairs={{0,96},{8,104},{16,112},{24,120},{32,0},{40,8},{48,16},{56,24},{64... | collective-permute-start | bytes 786440 | tf_op jit(solution)/shard_map/ppermute | solution.py:335
  59.4 1.1 copy.17.side_ref
  60.5 2.5 %collective-permute-done.3.x1_ref = bf16[2,2,2,2,4,16,128]{6,5,4,3,2,1,0:T(8,128)(2,1)S(1)} collective-permute-done((bf16[2,2,2,2,4,16,128]{6,5,4,3,2,1,0:T(8,128)(2,1)S(1)}, bf16[2,2,2,2,4,16,128]{6,5,4,3,2,1,0:T(8,128)(2,1)S(1)}, u32[]{:S(2)}, u32[]{:S(2)}) %collective-permute-start.3) | collective-permute-done | bytes 262176 | tf_op jit(solution)/shard_map/ppermute | solution.py:335
  63.0 5.8 %collective-permute-done.4.x2_ref = bf16[2,2,2,2,4,16,128]{6,5,4,3,2,1,0:T(8,128)(2,1)S(1)} collective-permute-done((bf16[2,2,2,2,4,16,128]{6,5,4,3,2,1,0:T(8,128)(2,1)S(1)}, bf16[2,2,2,2,4,16,128]{6,5,4,3,2,1,0:T(8,128)(2,1)S(1)}, u32[]{:S(2)}, u32[]{:S(2)}) %collective-permute-start.4) | collective-permute-done | bytes 262176 | tf_op jit(solution)/shard_map/ppermute | solution.py:335
  68.8 3.4 %copy-done = f32[8,2,1024,128]{3,2,1,0:T(8,128)S(1)} copy-done((f32[8,2,1024,128]{3,2,1,0:T(8,128)S(1)}, f32[8,2,1024,128]{3,2,1,0:T(8,128)}, u32[]{:S(2)}) %copy-start) | copy-done | bytes 8388632
  72.2 1.0 copy-done.6
  73.2 5.3 %shard_map.148 = bf16[8,1040,128]{2,1,0:T(8,128)(2,1)S(1)} custom-call(bf16[8,2,2,4,16,128]{5,4,3,2,1,0:T(8,128)(2,1)S(1)} %all-to-all-done.1.own_ref, bf16[8,2,2,4,16,128]{5,4,3,2,1,0:T(8,128)(2,1)S(1)} %collective-permute-done.other_ref, bf16[2,4,2,2,4,16,128]{6,5,4,3,2,1,0:T(8,128)(2,1)S(1)} %get-tuple-element.7.near_ref, ...), custom_call_target="tpu_custom_call" | custom-call | flops 3000000000 | bytes 10485760 | tf_op jit(solution)/shard_map/pallas_call | solution.py:298
  78.6 35.0 %all_to_all.15.in_ref = bf16[8,1040,128]{2,1,0:T(8,128)(2,1)S(1)} all-to-all(bf16[8,1040,128]{2,1,0:T(8,128)(2,1)S(1)} %shard_map.148), channel_id=1, replica_groups=mesh['tmpl'=16,'seg'=8] {'seg'}, dimensions={0} | all-to-all | bytes 4259840 | tf_op jit(solution)/shard_map/all_to_all | solution.py:359
  113.6 3.9 %shard_map.149 = f32[2,2,1024,128]{3,2,1,0:T(8,128)} custom-call(bf16[8,1040,128]{2,1,0:T(8,128)(2,1)S(1)} %all_to_all.15.in_ref, bf16[4,2,256,256]{3,2,1,0:T(8,128)(2,1)S(1)} %copy-done.14), custom_call_target="tpu_custom_call" | custom-call | flops 3000000000 | bytes 6291456 | tf_op jit(solution)/shard_map/pallas_call | solution.py:298
  (36 shorter events, 0.2 us)
Async XLA Ops:
  0.0 27.1 %copy-start.3 = (bf16[4,2,2,256,256]{4,3,2,1,0:T(8,128)(2,1)S(1)}, bf16[4,2,2,256,256]{4,3,2,1,0:T(8,128)(2,1)}, u32[]{:S(2)}) copy-start(bf16[4,2,2,256,256]{4,3,2,1,0:T(8,128)(2,1)} %constant.20.clone.table_ref) | copy-start | bytes 6291460
  0.0 1.7 %copy-start.4 = (f32[2,32,64,128]{3,2,1,0:T(8,128)S(1)}, f32[2,32,64,128]{3,2,1,0:T(8,128)}, u32[]{:S(2)}) copy-start(f32[2,32,64,128]{3,2,1,0:T(8,128)} %bank_ref.1) | copy-start | bytes 6291460
  1.7 0.7 copy-start.13
  2.4 1.7 %copy-start.11 = (s32[2,1,2]{2,1,0:T(1,128)S(1)}, s32[2,1,2]{2,1,0:T(1,128)}, u32[]{:S(2)}) copy-start(s32[2,1,2]{2,1,0:T(1,128)} %start_ref.1) | copy-start | bytes 52
  2.4 1.7 %copy-start.12 = (s32[2,1,2]{2,1,0:T(1,128)S(1)}, s32[2,1,2]{2,1,0:T(1,128)}, u32[]{:S(2)}) copy-start(s32[2,1,2]{2,1,0:T(1,128)} %span_ref.1) | copy-start | bytes 52
  4.1 29.0 %collective-permute-start.1 = (bf16[2,4,2,2,4,16,128]{6,5,4,3,2,1,0:T(8,128)(2,1)}, bf16[2,4,2,2,4,16,128]{6,5,4,3,2,1,0:T(8,128)(2,1)}, u32[]{:S(2)}, u32[]{:S(2)}) collective-permute-start(bf16[2,4,2,2,4,16,128]{6,5,4,3,2,1,0:T(8,128)(2,1)} %get-tuple-element.8), channel_id=1, source_target_pairs={{0,8},{8,0},{16,24},{24,16},{32,40},{40,32},{48,56},{56,48},{64,72... | collective-permute-start | bytes 1572872 | tf_op jit(solution)/shard_map/ppermute | solution.py:329
  4.1 1.2 %copy-start.5 = (f32[2,128,1024]{2,1,0:T(8,128)S(1)}, f32[2,128,1024]{2,1,0:T(8,128)}, u32[]{:S(2)}) copy-start(f32[2,128,1024]{2,1,0:T(8,128)} %strain_ref.1) | copy-start | bytes 3145732
  5.3 0.9 copy-start.9
  6.2 0.8 copy-start.10
  7.0 20.1 %copy-start.8 = (f32[2,16,1024]{2,1,0:T(8,128)S(1)}, f32[2,16,1024]{2,1,0:T(8,128)}, u32[]{:S(2)}) copy-start(f32[2,16,1024]{2,1,0:T(8,128)} %constant.22.clone.base_ref) | copy-start | bytes 393220
  9.7 17.3 %all-to-all-start = ((bf16[8,128,128]{2,1,0:T(8,128)(2,1)}), bf16[8,128,128]{2,1,0:T(8,128)(2,1)S(1)}, u32[]{:S(2)}, u32[]{:S(2)}) async-start(bf16[8,128,128]{2,1,0:T(8,128)(2,1)} %shard_map.145), calls=%async_computation | async-start | bytes 524288 | tf_op jit(solution)/shard_map/all_to_all | solution.py:322
  27.1 1.0 copy-start.7
  29.5 15.2 %all-to-all-start.1 = ((bf16[8,2,2,4,16,128]{5,4,3,2,1,0:T(8,128)(2,1)}), bf16[8,2,2,4,16,128]{5,4,3,2,1,0:T(8,128)(2,1)S(1)}, u32[]{:S(2)}, u32[]{:S(2)}) async-start(bf16[8,2,2,4,16,128]{5,4,3,2,1,0:T(8,128)(2,1)} %shard_map.146), calls=%async_computation.1 | async-start | bytes 1048576 | tf_op jit(solution)/shard_map/all_to_all | solution.py:341
  33.0 3.9 %copy-start.15 = (bf16[1,2,2,4,16,128]{5,4,3,2,1,0:T(8,128)(2,1)S(1)}, bf16[1,2,2,4,16,128]{5,4,3,2,1,0:T(8,128)(2,1)}, u32[]{:S(2)}) copy-start(bf16[1,2,2,4,16,128]{5,4,3,2,1,0:T(8,128)(2,1)} %get-tuple-element.11) | copy-start | bytes 196612
  35.0 17.4 %collective-permute-start.2 = (bf16[2,4,2,2,4,16,128]{6,5,4,3,2,0,1:T(8,128)(2,1)}, bf16[2,4,2,2,4,16,128]{6,5,4,3,2,0,1:T(8,128)(2,1)}, u32[]{:S(2)}, u32[]{:S(2)}) collective-permute-start(bf16[2,4,2,2,4,16,128]{6,5,4,3,2,0,1:T(8,128)(2,1)} %copy.16), channel_id=1, source_target_pairs={{0,16},{8,24},{16,0},{24,8},{32,48},{40,56},{48,32},{56,40},{64,80... | collective-permute-start | bytes 1572872 | tf_op jit(solution)/shard_map/ppermute | solution.py:330
  36.9 31.9 %copy-start.1 = (bf16[4,2,256,512]{3,2,1,0:T(8,128)(2,1)S(1)}, bf16[4,2,256,512]{3,2,1,0:T(8,128)(2,1)}, u32[]{:S(2)}) copy-start(bf16[4,2,256,512]{3,2,1,0:T(8,128)(2,1)} %constant.24.clone.third_ref) | copy-start | bytes 6291460
  44.8 24.0 %copy-start.2 = (bf16[4,256,1024]{2,1,0:T(8,128)(2,1)S(1)}, bf16[4,256,1024]{2,1,0:T(8,128)(2,1)}, u32[]{:S(2)}) copy-start(bf16[4,256,1024]{2,1,0:T(8,128)(2,1)} %constant.23.clone.second_ref) | copy-start | bytes 6291460
  44.8 15.7 %collective-permute-start = (bf16[8,2,2,4,16,128]{5,4,3,2,1,0:T(8,128)(2,1)S(1)}, bf16[8,2,2,4,16,128]{5,4,3,2,1,0:T(8,128)(2,1)S(1)}, u32[]{:S(2)}, u32[]{:S(2)}) collective-permute-start(bf16[8,2,2,4,16,128]{5,4,3,2,1,0:T(8,128)(2,1)S(1)} %all-to-all-done.1.own_ref), channel_id=1, source_target_pairs={{0,8},{8,0},{16,24},{24,16},{32,40},{40,32},{48,56},{56,48},{64,72... | collective-permute-start | bytes 1572872 | tf_op jit(solution)/shard_map/ppermute | solution.py:342
  53.4 9.5 %collective-permute-start.3 = (bf16[2,2,2,2,4,16,128]{6,5,4,3,2,1,0:T(8,128)(2,1)S(1)}, bf16[2,2,2,2,4,16,128]{6,5,4,3,2,1,0:T(8,128)(2,1)S(1)}, u32[]{:S(2)}, u32[]{:S(2)}) collective-permute-start(bf16[2,2,2,2,4,16,128]{6,5,4,3,2,1,0:T(8,128)(2,1)S(1)} %pad_maximum_fusion.1), channel_id=1, source_target_pairs={{0,32},{8,40},{16,48},{24,56},{32,64},{40,72},{48,80},{56,88},{64,... | collective-permute-start | bytes 786440 | tf_op jit(solution)/shard_map/ppermute | solution.py:335
  55.0 13.8 %collective-permute-start.4 = (bf16[2,2,2,2,4,16,128]{6,5,4,3,2,1,0:T(8,128)(2,1)S(1)}, bf16[2,2,2,2,4,16,128]{6,5,4,3,2,1,0:T(8,128)(2,1)S(1)}, u32[]{:S(2)}, u32[]{:S(2)}) collective-permute-start(bf16[2,2,2,2,4,16,128]{6,5,4,3,2,1,0:T(8,128)(2,1)S(1)} %pad_maximum_fusion.2), channel_id=1, source_target_pairs={{0,64},{8,72},{16,80},{24,88},{32,96},{40,104},{48,112},{56,120},{... | collective-permute-start | bytes 786440 | tf_op jit(solution)/shard_map/ppermute | solution.py:335
  57.9 10.9 %collective-permute-start.5 = (bf16[2,2,2,2,4,16,128]{6,5,4,3,2,1,0:T(8,128)(2,1)S(1)}, bf16[2,2,2,2,4,16,128]{6,5,4,3,2,1,0:T(8,128)(2,1)S(1)}, u32[]{:S(2)}, u32[]{:S(2)}) collective-permute-start(bf16[2,2,2,2,4,16,128]{6,5,4,3,2,1,0:T(8,128)(2,1)S(1)} %pad_maximum_fusion.3), channel_id=1, source_target_pairs={{0,96},{8,104},{16,112},{24,120},{32,0},{40,8},{48,16},{56,24},{64... | collective-permute-start | bytes 786440 | tf_op jit(solution)/shard_map/ppermute | solution.py:335
  68.8 3.4 %copy-start = (f32[8,2,1024,128]{3,2,1,0:T(8,128)S(1)}, f32[8,2,1024,128]{3,2,1,0:T(8,128)}, u32[]{:S(2)}) copy-start(f32[8,2,1024,128]{3,2,1,0:T(8,128)} %constant.25.clone.back_ref) | copy-start | bytes 25165828
  72.2 1.0 copy-start.6
  78.6 35.0 %copy-start.14 = (bf16[4,2,256,256]{3,2,1,0:T(8,128)(2,1)S(1)}, bf16[4,2,256,256]{3,2,1,0:T(8,128)(2,1)}, u32[]{:S(2)}) copy-start(bf16[4,2,256,256]{3,2,1,0:T(8,128)(2,1)} %constant.26.clone.table_ref) | copy-start | bytes 3145732
where the time goes:
time: 119 us; the launch traced here: 118 us
  blocking collectives  35 us (29%)
  waiting for transfers between devices  32.5 us (27%)
  starting transfers between devices  18.3 us (15%)
  local copies, waits for them, and re-layouts  16.3 us (14%)
  Pallas kernels  15.1 us (13%)
    all_to_all x1, blocking collectives, per_device(): series = lax.all_to_all(inner, 'seg', 0, 0)  35 us
    pallas_call x5, Pallas kernels, call(): pl.pallas_call(kernel, out_shape=outs, in_specs=specs, out_specs=jax.tree...  15.1 us
    unnamed x32, local copies, waits for them, and re-layouts  10.8 us
    all_to_all x1, waiting for transfers between devices, per_device(): columns = lax.all_to_all(gated, 'seg', 0, 0)  8.79 us
    ppermute x3, waiting for transfers between devices, per_device(): rounds.append(lax.ppermute(send, 'tmpl', hop))  8.33 us
    all_to_all x1, starting transfers between devices, per_device(): columns = lax.all_to_all(gated, 'seg', 0, 0)  7.87 us
    all_to_all x1, waiting for transfers between devices, per_device(): own = lax.all_to_all(turned, 'seg', 0, 0)  7.76 us
    ppermute x1, waiting for transfers between devices, per_device(): side = lax.ppermute(jnp.stack([near[1], cross[1]]), 'tmpl', swap_z)  7.57 us
  transfers between devices with their start and end apart: 8, of which 5 were waited for; matrix products, arithmetic and copies ran while one was open for 5% of the time, Pallas kernels for 4%

commit v1 on v0

v1 whole, which is shorter than its diff:
```python
import functools
import math

import jax
import jax.numpy as jnp
import numpy as np
from jax import lax
from jax.experimental import pallas as pl
from jax.experimental.pallas import tpu as pltpu
from jax.sharding import PartitionSpec as P

BF = jnp.bfloat16
F32 = jnp.float32
NSAMP = 1048576
VMEM = pl.BlockSpec(memory_space=pltpu.VMEM)
SMEM = pl.BlockSpec(memory_space=pltpu.SMEM)
ANY = pl.BlockSpec(memory_space=pl.ANY)
MIB = 1 << 20
OFFSETS = [(rz, rx) for rz in range(2) for rx in range(4)][1:]


def phases(product, count):
    angle = 2.0 * math.pi / count * (product % count).astype(np.float64)
    return np.cos(angle), np.sin(angle)


def split_hi_lo(table):
    table = table.astype(np.float32)
    hi = table.astype(jnp.bfloat16)
    lo = (table - hi.astype(np.float32)).astype(jnp.bfloat16)
    return hi, lo


@functools.cache
def tables():
    q = np.arange(256)
    first = []
    for r in range(4):
        c, s = phases((4 * q[:, None] + r) * q[None, :], 1024)
        first.append(np.stack([np.stack(split_hi_lo(c)), np.stack(split_hi_lo(-s))]))
    rows = np.array([4 * (i % 32) + i // 32 for i in range(128)])
    k2 = np.arange(1024)
    c, s = phases(rows[:, None] * k2[None, :], NSAMP)
    fine = np.stack([c, -s]).astype(np.float32)
    c, s = phases(128 * np.arange(8)[:, None] * k2[None, :], NSAMP)
    base = np.stack([c, -s]).astype(np.float32)
    second = []
    for r in range(4):
        c, s = phases(q[:, None] * (4 * q[None, :] + r), 1024)
        (ch, cl), (sh, sl) = split_hi_lo(c), split_hi_lo(s)
        second.append(np.concatenate([ch, sh, cl, sl], axis=1))
    third = []
    for p in range(4):
        c, s = phases(q[:, None] * (4 * q[None, :] + p), 1024)
        c, s = c.astype(np.float32), s.astype(np.float32)
        third.append(np.stack([np.concatenate([c, -s], 1), np.concatenate([s, c], 1)]))
    n1 = np.arange(1024)
    c, s = phases(n1[:, None] * np.arange(128)[None, :], NSAMP)
    back = np.stack([c, s]).astype(np.float32)
    c, s = phases(n1[:, None] * 128 * np.arange(128)[None, :], NSAMP)
    shift = np.stack([c, s]).astype(np.float32)
    last = []
    for p in range(4):
        c, s = phases((4 * q[:, None] + p) * q[None, :], 1024)
        last.append(np.stack([c, s]).astype(np.float32))
    return dict(
        first=np.stack(first),
        fine=fine,
        base=base,
        second=np.stack(second),
        third=np.stack(third).astype(jnp.bfloat16),
        back=back,
        shift=shift,
        last=np.stack(last).astype(jnp.bfloat16),
    )


def dot(a, b):
    return jnp.dot(a, b, preferred_element_type=F32)


def dot_nt(a, b):
    return lax.dot_general(a, b, (((1,), (1,)), ((), ())), preferred_element_type=F32)


def place():
    t = lax.axis_index("tmpl")
    return t // 4, (t // 2) % 2, t % 2


def gate_kernel(
    strain_ref, start_any, span_any, assign_any, bank_any, out_ref, near_ref, cross_ref,
    strain, bank_ref, start_ref, span_ref, assign_ref, sems,
):
    x, z, core = place()
    copies = [
        pltpu.make_async_copy(start_any, start_ref, sems.at[0]),
        pltpu.make_async_copy(span_any, span_ref, sems.at[1]),
        pltpu.make_async_copy(strain_ref.at[core], strain, sems.at[2]),
        pltpu.make_async_copy(assign_any, assign_ref, sems.at[3]),
        pltpu.make_async_copy(bank_any, bank_ref, sems.at[4]),
    ]
    for copy in copies:
        copy.start()
    row = lax.broadcasted_iota(jnp.int32, (128, 128), 0)
    lane = lax.broadcasted_iota(jnp.int32, (128, 128), 1)
    order = jnp.where(lane == row % 32 * 4 + row // 32, 1.0, 0.0).astype(BF)
    pick = jnp.where(row == lane % 32 * 4 + lane // 32, 1.0, 0.0).astype(BF)
    for copy in copies[:3]:
        copy.wait()
    blocks = []
    for dest in range(8):
        value = strain[:, 128 * dest : 128 * dest + 128]
        sample = row * 1024 + (lane + 128 * dest)
        for g in range(2):
            first = start_ref[core, 0, g]
            inside = (sample >= first) & (sample < first + span_ref[core, 0, g])
            value = jnp.where(inside, 0.0, value)
        blocks.append(value.astype(BF))
    picked = dot(jnp.concatenate(blocks, axis=0), pick).astype(BF)
    wide = jnp.concatenate([picked[128 * dest : 128 * dest + 128] for dest in range(8)], axis=1)
    ordered = dot(order, wide).astype(BF)
    for dest in range(8):
        out_ref[dest] = ordered[:, 128 * dest : 128 * dest + 128]

    for copy in copies[3:]:
        copy.wait()
    for i in range(16):
        rc, rz, rx = i // 8, i // 4 % 2, i % 4
        dest = ((x + rx) % 4) * 4 + (z + rz) % 2 * 2 + (core + rc) % 2
        for slot in range(2):
            chosen = assign_ref[2 * dest + slot]
            for part in range(2):
                for p in range(4):
                    value = bank_ref[part, chosen, pl.ds(p, 16, stride=4), :].astype(BF)
                    (near_ref, cross_ref)[rc][rz, rx, slot, part, p] = value


def prepare_kernel(asd_ref, back_ref, shift_ref, weight_ref, twist_ref):
    for p in range(4):
        asd = asd_ref[pl.ds(p, 256, stride=4), :]
        weight_ref[p] = 1.0 / (asd * asd)
    seg = lax.axis_index("seg")
    own = lax.broadcasted_iota(jnp.int32, (128, 128), 1) == seg
    for i in range(8):
        rows = slice(128 * i, 128 * i + 128)
        shift = [jnp.sum(jnp.where(own, shift_ref[part, rows, :], 0.0), axis=1, keepdims=True) for part in range(2)]
        re, im = back_ref[0, rows, :], back_ref[1, rows, :]
        twist_ref[0, rows, :] = re * shift[0] - im * shift[1]
        twist_ref[1, rows, :] = re * shift[1] + im * shift[0]


def pack_kernel(near_ref, cross_ref, *out_refs):
    for i, (rz, rx) in enumerate(OFFSETS):
        out_refs[i][0] = near_ref[rz, rx]
        out_refs[i][1] = cross_ref[rz, rx]


def four_way(sign, parts):
    (ar, ai), (br, bi), (cr, ci), (dr, di) = parts
    sr, si = ar + cr, ai + ci
    tr, ti = ar - cr, ai - ci
    ur, ui = br + dr, bi + di
    vr, vi = br - dr, bi - di
    if sign > 0:
        wr, wi = -vi, vr
    else:
        wr, wi = vi, -vr
    return ((sr + ur, si + ui), (tr + wr, ti + wi), (sr - ur, si - ui), (tr - wr, ti - wi))


def first_kernel(cols_ref, table_ref, fine_ref, base_ref, after_ref, also_ref, out_ref, z_ref):
    del after_ref, also_ref
    seg = lax.axis_index("seg")
    for r in range(4):
        turned = cols_ref[:, 32 * r : 32 * r + 32, :].reshape(256, 128).T
        for part in range(2):
            z_ref[r, part] = dot(turned, table_ref[r, part, 0]) + dot(turned, table_ref[r, part, 1])
    base_re = base_ref[0, pl.ds(seg, 1), :]
    base_im = base_ref[1, pl.ds(seg, 1), :]
    for i in range(8):
        rows = slice(16 * i, 16 * i + 16)
        at = slice(i % 2 * 16, i % 2 * 16 + 16)
        fr, fi = fine_ref[0, rows, :], fine_ref[1, rows, :]
        tr = fr * base_re - fi * base_im
        ti = fr * base_im + fi * base_re
        outs = four_way(-1, [(z_ref[r, 0, rows, :], z_ref[r, 1, rows, :]) for r in range(4)])
        for k, (re, im) in enumerate(outs):
            wr, wi = tr[:, 256 * k : 256 * k + 256], ti[:, 256 * k : 256 * k + 256]
            done = ((re * wr - im * wi).astype(BF), (re * wi + im * wr).astype(BF))
            for half in range(2):
                for part in range(2):
                    out_ref[2 * k + half, part, i // 2, at] = done[part][:, 128 * half : 128 * half + 128]


def second_kernel(own_ref, table_ref, after_ref, spec_ref, z_ref):
    del after_ref
    for r in range(4):
        re = own_ref[:, 0, r].reshape(256, 128)
        im = own_ref[:, 1, r].reshape(256, 128)
        right = jnp.concatenate([jnp.concatenate([re, im], axis=1), jnp.concatenate([im, -re], axis=1)], axis=0)
        z_ref[r] = dot(table_ref[r, :, :512], right) + dot(table_ref[r, :, 512:], right)
    for i in range(8):
        rows = slice(32 * i, 32 * i + 32)
        outs = four_way(-1, [(z_ref[r, rows, :128], z_ref[r, rows, 128:]) for r in range(4)])
        for k, parts in enumerate(outs):
            for part in range(2):
                spec_ref[part, 256 * k + 32 * i : 256 * k + 32 * i + 32, :] = parts[part]


def assemble_kernel(near_ref, cross_ref, *rest):
    moved_refs, bank, sems = rest[:7], rest[7], rest[8]
    x, z, core = place()
    copies = []
    for i, (rz, rx) in enumerate([(0, 0)] + OFFSETS):
        for rc in range(2):
            src = (near_ref, cross_ref)[rc].at[0, 0] if i == 0 else moved_refs[i - 1].at[rc]
            origin = ((x + 4 - rx) % 4) * 4 + (z + rz) % 2 * 2 + (core + rc) % 2
            copies.append(pltpu.make_async_copy(src, bank.at[origin], sems.at[len(copies)]))
    for copy in copies:
        copy.start()
    for copy in copies:
        copy.wait()


def filter_segment(spec, weight_ref, third_ref, twist, bank, out_ref, first_row, v_ref, norms):
    for p in range(4):
        weight = weight_ref[p]
        sr = spec[0, pl.ds(p, 256, stride=4), :] * weight
        si = spec[1, pl.ds(p, 256, stride=4), :] * weight
        lanes_re, lanes_im = [], []
        for slot in range(2):
            hr = bank[:, slot, 0, p].reshape(256, 128).astype(F32)
            hi = bank[:, slot, 1, p].reshape(256, 128).astype(F32)
            if norms is not None:
                power = (hr * hr + hi * hi) * weight
                norms[slot] = norms[slot] + power.reshape(32, 8, 128).sum(axis=0)
            lanes_re.append((sr * hr + si * hi).astype(BF))
            lanes_im.append((si * hr - sr * hi).astype(BF))
        right = jnp.concatenate([jnp.concatenate(lanes_re, axis=1), jnp.concatenate(lanes_im, axis=1)], axis=0)
        v_ref[p, 0] = dot(third_ref[p, 0], right)
        v_ref[p, 1] = dot(third_ref[p, 1], right)
    for i in range(8):
        rows = slice(32 * i, 32 * i + 32)
        half, inside = i // 4, (i % 4) * 32
        for slot in range(2):
            cols = slice(128 * slot, 128 * slot + 128)
            outs = four_way(1, [(v_ref[p, 0, rows, cols], v_ref[p, 1, rows, cols]) for p in range(4)])
            for k, (re, im) in enumerate(outs):
                wr = twist[0, 256 * k + 32 * i : 256 * k + 32 * i + 32, :]
                wi = twist[1, 256 * k + 32 * i : 256 * k + 32 * i + 32, :]
                at = first_row + slot * 256 + inside
                out_ref[2 * k + half, at : at + 32, :] = (re * wr - im * wi).astype(BF)
                out_ref[2 * k + half, at + 128 : at + 160, :] = (re * wi + im * wr).astype(BF)


def own_kernel(spec, weight_ref, third_ref, twist, bank, out_ref, v_ref):
    norms = [jnp.zeros((8, 128), F32), jnp.zeros((8, 128), F32)]
    filter_segment(spec, weight_ref, third_ref, twist, bank, out_ref, 0, v_ref, norms)
    row = lax.broadcasted_iota(jnp.int32, (16, 128), 0)
    tail = jnp.zeros((16, 128), F32)
    for slot in range(2):
        left = jnp.broadcast_to(norms[slot].sum(axis=0, keepdims=True), (16, 128))
        for piece in range(3):
            rounded = left.astype(BF).astype(F32)
            tail = jnp.where(row == 3 * slot + piece, rounded, tail)
            left = left - rounded
    for dest in range(8):
        out_ref[dest, 512:528, :] = tail.astype(BF)


def other_kernel(spec, weight_ref, third_ref, twist, bank, half_ref, out_ref, v_ref):
    out_ref[:, :528, :] = half_ref[...]
    filter_segment(spec, weight_ref, third_ref, twist, bank, out_ref, 528, v_ref, None)


def last_kernel(in_ref, table_ref, out_ref):
    total = jnp.zeros((16, 128), F32)
    for s in range(8):
        total = total + in_ref[s, 512:528, :].astype(F32)
    row = lax.broadcasted_iota(jnp.int32, (16, 128), 0)
    scales = []
    for slot in range(2):
        mine = (row >= 3 * slot) & (row < 3 * slot + 3)
        sigma2 = jnp.sum(jnp.where(mine, total, 0.0), axis=(0, 1), keepdims=True)
        scales.append(1.0 / jnp.sqrt(NSAMP * sigma2))
    _, _, core = place()
    for pair in range(4):
        other, slot = pair // 2, pair % 2
        seg = (core + other) % 2
        at = 528 * other + 256 * slot
        parts = []
        for r in range(4):
            both = jnp.concatenate([in_ref[2 * r, at : at + 256, :], in_ref[2 * r + 1, at : at + 256, :]], axis=1)
            both = both.astype(F32)
            parts.append((both[:128], both[128:]))
        outs = four_way(1, parts)
        for p, (re, im) in enumerate(outs):
            right = jnp.concatenate([re, im], axis=0)
            hi = right.astype(BF)
            lo = (right - hi.astype(F32)).astype(BF)
            cos = dot_nt(table_ref[p, 0], hi) + dot_nt(table_ref[p, 0], lo)
            sin = dot_nt(table_ref[p, 1], hi) + dot_nt(table_ref[p, 1], lo)
            sr = cos[:, :128] - sin[:, 128:]
            si = sin[:, :128] + cos[:, 128:]
            out_ref[seg, slot, pl.ds(p, 256, stride=4), :] = jnp.sqrt(sr * sr + si * si) * scales[slot]


def call(kernel, ins, outs, specs, flops, moved, scratch=(), limit=16):
    return pl.pallas_call(
        kernel,
        out_shape=outs,
        in_specs=specs,
        out_specs=jax.tree.map(lambda _: VMEM, outs),
        scratch_shapes=list(scratch),
        compiler_params=pltpu.CompilerParams(vmem_limit_bytes=limit * MIB),
        cost_estimate=pl.CostEstimate(flops=flops, bytes_accessed=moved, transcendentals=0),
    )(*ins)


def shape(*dims, dtype=BF):
    return jax.ShapeDtypeStruct(dims, dtype)


def per_device(strain, gate_start, gate_span, asd, bank, assign):
    const = {name: jnp.asarray(value) for name, value in tables().items()}
    swap_core = [(i, i ^ 1) for i in range(16)]

    blk = (2, 2, 4, 16, 128)
    gated, near, cross = call(
        gate_kernel, (strain, gate_start, gate_span, assign, bank),
        (shape(8, 128, 128), shape(2, 4, *blk), shape(2, 4, *blk)), [ANY] * 5, 10**8, 4 * MIB,
        [
            pltpu.VMEM((128, 1024), F32), pltpu.VMEM((2, 32, 64, 128), F32), pltpu.SMEM((2, 1, 2), jnp.int32),
            pltpu.SMEM((2, 1, 2), jnp.int32), pltpu.SMEM((32,), jnp.int32), pltpu.SemaphoreType.DMA((5,)),
        ],
        limit=63,
    )
    columns = lax.all_to_all(gated, "seg", 0, 0)

    cross = lax.ppermute(cross, "tmpl", swap_core)
    sends = call(pack_kernel, (near, cross), (shape(2, *blk),) * 7, [VMEM] * 2, 10**6, 2 * MIB)
    moved = []
    for (rz, rx), send in zip(OFFSETS, sends):
        hop = [(i, (i // 4 + rx) % 4 * 4 + i % 4 ^ 2 * rz) for i in range(16)]
        moved.append(lax.ppermute(send, "tmpl", hop))
    ordered = call(
        assemble_kernel, (near, cross, *moved), shape(16, *blk), [ANY] * 9, 1, 20 * MIB, [pltpu.SemaphoreType.DMA((16,))]
    )
    weight, twist = call(
        prepare_kernel, (asd, const["back"], const["shift"]),
        (shape(4, 256, 128, dtype=F32), shape(2, 1024, 128, dtype=F32)), [VMEM] * 3, 1, 40 * MIB,
    )
    turned = call(
        first_kernel, (columns, const["first"], const["fine"], const["base"], sends[0], weight),
        shape(8, 2, 4, 32, 128), [VMEM] * 4 + [ANY] * 2, 3 * 10**8, 4 * MIB, [pltpu.VMEM((4, 2, 128, 256), F32)],
    )
    own = lax.all_to_all(turned, "seg", 0, 0)
    spec = call(
        second_kernel, (own, const["second"], ordered), shape(2, 1024, 128, dtype=F32),
        [VMEM] * 2 + [ANY], 1, 1, [pltpu.VMEM((4, 256, 256), F32)],
    )
    other_spec = lax.ppermute(spec, "tmpl", swap_core)
    half = call(
        own_kernel,
        (spec, weight, const["third"], twist, ordered),
        shape(8, 528, 128), [VMEM] * 5, 2 * 10**9, 10 * MIB, [pltpu.VMEM((4, 2, 256, 256), F32)],
    )
    inner = call(
        other_kernel,
        (other_spec, weight, const["third"], twist, ordered, half),
        shape(8, 1040, 128), [VMEM] * 6, 2 * 10**9, 10 * MIB, [pltpu.VMEM((4, 2, 256, 256), F32)],
    )
    series = lax.all_to_all(inner, "seg", 0, 0)
    return call(
        last_kernel, (series, const["last"]), shape(2, 2, 1024, 128, dtype=F32), [VMEM] * 2, 3 * 10**9, 6 * MIB
    )


def solution(mesh):
    placed = (
        P(None, "seg", None),
        P(None, "seg", None),
        P(None, "seg", None),
        P(None, "seg"),
        P(None, None, "tmpl", "seg"),
        P(),
    )
    return jax.shard_map(
        per_device,
        mesh=mesh,
        in_specs=placed,
        out_specs=P(None, "tmpl", None, "seg"),
        check_vma=False,
    )
```

time: 119 us -> 101 us (0.85)
  waiting for transfers between devices: 32.5 us -> 9.78 us
  starting transfers between devices: 18.3 us -> 27 us
  local copies, waits for them, and re-layouts: 16.3 us -> 12.2 us
    all_to_all x1, waiting for transfers between devices: 8.79 us -> 0.01 us  [per_device(): columns = lax.all_to_all(gated, 'seg', 0, 0)]
    all_to_all x1, waiting for transfers between devices: 7.76 us -> 0.01 us  [per_device(): own = lax.all_to_all(turned, 'seg', 0, 0)]
    ppermute x5 -> x8, waiting for transfers between devices: 15.9 us -> 9.77 us  [the longest x7 8.31 us: per_device(): moved.append(lax.ppermute(send, 'tmpl', hop))]
    ppermute x5 -> x8, starting transfers between devices: 6.9 us -> 11.7 us  [the longest x7 11.6 us: per_device(): moved.append(lax.ppermute(send, 'tmpl', hop))]
    all_to_all x1, starting transfers between devices: 3.49 us -> 7.21 us  [per_device(): own = lax.all_to_all(turned, 'seg', 0, 0)]
    another operation x4 -> x0, local copies, waits for them, and re-layouts: 3.46 us -> none  [the longest x3 2.6 us: per_device(): send = jnp.stack([jnp.stack([near[0, dx], cross[0, dx]]), side[:, dx]])]
    unnamed x32 -> x40, local copies, waits for them, and re-layouts: 10.8 us -> 12.2 us
    pallas_call x5 -> x9, Pallas kernels: 15.1 us -> 15.9 us  [call(): pl.pallas_call(kernel, out_shape=outs, in_specs=specs, out_specs=jax.tree...]
  transfers between devices with their start and end apart: 8 -> 11, of which waited for: 5 -> 2; matrix products, arithmetic and copies ran while one was open for 5% -> 0% of each run, Pallas kernels for 4% -> 4%
where the time goes in v1:
time: 101 us; the launch traced here: 100 us
  blocking collectives  35.4 us (35%)
  starting transfers between devices  27 us (27%)
  Pallas kernels  15.9 us (16%)
  local copies, waits for them, and re-layouts  12.2 us (12%)
  waiting for transfers between devices  9.78 us (10%)
    all_to_all x1, blocking collectives, per_device(): series = lax.all_to_all(inner, 'seg', 0, 0)  35.4 us
    pallas_call x9, Pallas kernels, call(): pl.pallas_call(kernel, out_shape=outs, in_specs=specs, out_specs=jax.tree...  15.9 us
    unnamed x40, local copies, waits for them, and re-layouts  12.2 us
    ppermute x7, starting transfers between devices, per_device(): moved.append(lax.ppermute(send, 'tmpl', hop))  11.6 us
    ppermute x7, waiting for transfers between devices, per_device(): moved.append(lax.ppermute(send, 'tmpl', hop))  8.31 us
    all_to_all x1, starting transfers between devices, per_device(): columns = lax.all_to_all(gated, 'seg', 0, 0)  8.01 us
    all_to_all x1, starting transfers between devices, per_device(): own = lax.all_to_all(turned, 'seg', 0, 0)  7.21 us
  transfers between devices with their start and end apart: 11, of which 2 were waited for; matrix products, arithmetic and copies ran while one was open for 0% of the time, Pallas kernels for 4%

profile of v1, /device:TPU:0, one launch (start us, length us, event | category | flops | bytes accessed | tf_op | source)
XLA Modules:
  0.0 100.4 jit_solution(2589208242374905763)
XLA Ops:
  0.0 3.0 %shard_map.136 = (bf16[8,128,128]{2,1,0:T(8,128)(2,1)}, bf16[2,4,2,2,4,16,128]{6,5,4,3,2,1,0:T(8,128)(2,1)}, bf16[2,4,2,2,4,16,128]{6,5,4,3,2,1,0:T(8,128)(2,1)}) custom-call(f32[2,128,1024]{2,1,0:T(8,128)} %strain_ref.1, s32[2,1,2]{2,1,0:T(1,128)} %start_any.1, s32[2,1,2]{2,1,0:T(1,128)} %span_any.1, s32[32]{0:T(128)} %assign_any.1, f32[2,32,64,128]{3,2,1,0:T(8,128)} %bank_any.1), custom_call_target="tpu_custom_call" | custom-call | flops 100000000 | bytes 4194304 | tf_op jit(solution)/shard_map/pallas_call | solution.py:310
  3.1 8.0 %all-to-all-start = ((bf16[8,128,128]{2,1,0:T(8,128)(2,1)}), bf16[8,128,128]{2,1,0:T(8,128)(2,1)S(1)}, u32[]{:S(2)}, u32[]{:S(2)}) async-start(bf16[8,128,128]{2,1,0:T(8,128)(2,1)} %get-tuple-element.17), calls=%async_computation | async-start | bytes 524288 | tf_op jit(solution)/shard_map/all_to_all | solution.py:339
  11.1 1.2 %copy-done.8 = f32[2,1024,128]{2,1,0:T(8,128)S(1)} copy-done((f32[2,1024,128]{2,1,0:T(8,128)S(1)}, f32[2,1024,128]{2,1,0:T(8,128)}, u32[]{:S(2)}) %copy-start.8) | copy-done | bytes 1048600
  12.3 1.2 %copy-done.9 = f32[2,1024,128]{2,1,0:T(8,128)S(1)} copy-done((f32[2,1024,128]{2,1,0:T(8,128)S(1)}, f32[2,1024,128]{2,1,0:T(8,128)}, u32[]{:S(2)}) %copy-start.9) | copy-done | bytes 1048600
  13.6 1.0 %copy-done.11 = f32[1024,128]{1,0:T(8,128)S(1)} copy-done((f32[1024,128]{1,0:T(8,128)S(1)}, f32[1024,128]{1,0:T(8,128)}, u32[]{:S(2)}) %copy-start.11) | copy-done | bytes 524312
  15.0 1.0 copy-done.6
  15.9 1.3 %shard_map.137 = (bf16[2,2,2,4,16,128]{5,4,3,2,1,0:T(8,128)(2,1)S(1)}, bf16[2,2,2,4,16,128]{5,4,3,2,1,0:T(8,128)(2,1)S(1)}, bf16[2,2,2,4,16,128]{5,4,3,2,1,0:T(8...) custom-call(bf16[2,4,2,2,4,16,128]{6,5,4,3,2,1,0:T(8,128)(2,1)S(1)} , ...), custom_call_target="tpu_custom_call" | custom-call | flops 1000000 | bytes 2097152 | tf_op jit(solution)/shard_map/pallas_call | solution.py:310
  17.2 0.6 copy-done.13
  17.9 0.7 copy-done.14
  18.5 0.6 copy-done.15
  19.2 0.6 copy-done.16
  19.8 0.6 copy-done.17
  20.5 0.6 copy-done.18
  21.1 1.2 %copy-done.10 = f32[2,128,1024]{2,1,0:T(8,128)S(1)} copy-done((f32[2,128,1024]{2,1,0:T(8,128)S(1)}, f32[2,128,1024]{2,1,0:T(8,128)}, u32[]{:S(2)}) %copy-start.10) | copy-done | bytes 1048600
  22.4 0.8 copy-done.12
  23.2 1.5 %shard_map.139 = bf16[8,2,4,32,128]{4,3,2,1,0:T(8,128)(2,1)} custom-call(bf16[8,128,128]{2,1,0:T(8,128)(2,1)S(1)} %all-to-all-done.cols_ref, bf16[4,2,2,256,256]{4,3,2,1,0:T(8,128)(2,1)S(1)} %copy-done.4, f32[2,128,1024]{2,1,0:T(8,128)S(1)} %copy-done.10, f32[2,8,1024]{2,1,0:T(8,128)S(1)} %copy-done.12, ...), custom_call_target="tpu_custom_call" | custom-call | flops 300000000 | bytes 4194304 | tf_op jit(solution)/shard_map/pallas_call | solution.py:310
  24.7 7.2 %all-to-all-start.1 = ((bf16[8,2,4,32,128]{4,3,2,1,0:T(8,128)(2,1)}), bf16[8,2,4,32,128]{4,3,2,1,0:T(8,128)(2,1)}, u32[]{:S(2)}, u32[]{:S(2)}) async-start(bf16[8,2,4,32,128]{4,3,2,1,0:T(8,128)(2,1)} %shard_map.139), calls=%async_computation.1 | async-start | bytes 1048576 | tf_op jit(solution)/shard_map/all_to_all | solution.py:358
  31.9 3.0 %collective-permute-start.2 = (bf16[2,2,2,4,16,128]{5,4,3,2,1,0:T(8,128)(2,1)}, bf16[2,2,2,4,16,128]{5,4,3,2,1,0:T(8,128)(2,1)S(1)}, u32[]{:S(2)}, u32[]{:S(2)}) collective-permute-start(bf16[2,2,2,4,16,128]{5,4,3,2,1,0:T(8,128)(2,1)} %copy-done.18), channel_id=1, source_target_pairs={{0,64},{8,72},{16,80},{24,88},{32,96},{40,104},{48,112},{56,120},{... | collective-permute-start | bytes 393224 | tf_op jit(solution)/shard_map/ppermute | solution.py:346
  34.9 1.1 %collective-permute-start.3 = (bf16[2,2,2,4,16,128]{5,4,3,2,1,0:T(8,128)(2,1)}, bf16[2,2,2,4,16,128]{5,4,3,2,1,0:T(8,128)(2,1)S(1)}, u32[]{:S(2)}, u32[]{:S(2)}) collective-permute-start(bf16[2,2,2,4,16,128]{5,4,3,2,1,0:T(8,128)(2,1)} %copy-done.17), channel_id=1, source_target_pairs={{0,96},{8,104},{16,112},{24,120},{32,0},{40,8},{48,16},{56,24},{64... | collective-permute-start | bytes 393224 | tf_op jit(solution)/shard_map/ppermute | solution.py:346
  36.1 1.0 %collective-permute-start.4 = (bf16[2,2,2,4,16,128]{5,4,3,2,1,0:T(8,128)(2,1)}, bf16[2,2,2,4,16,128]{5,4,3,2,1,0:T(8,128)(2,1)S(1)}, u32[]{:S(2)}, u32[]{:S(2)}) collective-permute-start(bf16[2,2,2,4,16,128]{5,4,3,2,1,0:T(8,128)(2,1)} %copy-done.16), channel_id=1, source_target_pairs={{0,16},{8,24},{16,0},{24,8},{32,48},{40,56},{48,32},{56,40},{64,80... | collective-permute-start | bytes 393224 | tf_op jit(solution)/shard_map/ppermute | solution.py:346
  37.1 1.3 %collective-permute-start.5 = (bf16[2,2,2,4,16,128]{5,4,3,2,1,0:T(8,128)(2,1)}, bf16[2,2,2,4,16,128]{5,4,3,2,1,0:T(8,128)(2,1)S(1)}, u32[]{:S(2)}, u32[]{:S(2)}) collective-permute-start(bf16[2,2,2,4,16,128]{5,4,3,2,1,0:T(8,128)(2,1)} %copy-done.15), channel_id=1, source_target_pairs={{0,48},{8,56},{16,32},{24,40},{32,80},{40,88},{48,64},{56,72},{64,... | collective-permute-start | bytes 393224 | tf_op jit(solution)/shard_map/ppermute | solution.py:346
  38.4 1.0 %collective-permute-start.6 = (bf16[2,2,2,4,16,128]{5,4,3,2,1,0:T(8,128)(2,1)}, bf16[2,2,2,4,16,128]{5,4,3,2,1,0:T(8,128)(2,1)S(1)}, u32[]{:S(2)}, u32[]{:S(2)}) collective-permute-start(bf16[2,2,2,4,16,128]{5,4,3,2,1,0:T(8,128)(2,1)} %copy-done.14), channel_id=1, source_target_pairs={{0,80},{8,88},{16,64},{24,72},{32,112},{40,120},{48,96},{56,104},{... | collective-permute-start | bytes 393224 | tf_op jit(solution)/shard_map/ppermute | solution.py:346
  39.4 3.8 %collective-permute-start.7 = (bf16[2,2,2,4,16,128]{5,4,3,2,1,0:T(8,128)(2,1)}, bf16[2,2,2,4,16,128]{5,4,3,2,1,0:T(8,128)(2,1)S(1)}, u32[]{:S(2)}, u32[]{:S(2)}) collective-permute-start(bf16[2,2,2,4,16,128]{5,4,3,2,1,0:T(8,128)(2,1)} %copy-done.13), channel_id=1, source_target_pairs={{0,112},{8,120},{16,96},{24,104},{32,16},{40,24},{48,0},{56,8},{64... | collective-permute-start | bytes 393224 | tf_op jit(solution)/shard_map/ppermute | solution.py:346
  43.5 8.3 %collective-permute-done.4.rest_3_ = bf16[2,2,2,4,16,128]{5,4,3,2,1,0:T(8,128)(2,1)S(1)} collective-permute-done((bf16[2,2,2,4,16,128]{5,4,3,2,1,0:T(8,128)(2,1)}, bf16[2,2,2,4,16,128]{5,4,3,2,1,0:T(8,128)(2,1)S(1)}, u32[]{:S(2)}, u32[]{:S(2)}) %collective-permute-start.4) | collective-permute-done | bytes 131104 | tf_op jit(solution)/shard_map/ppermute | solution.py:346
  51.9 1.6 %shard_map.140.after_ref.bank = bf16[16,2,2,4,16,128]{5,4,3,2,1,0:T(8,128)(2,1)S(1)} custom-call(bf16[2,4,2,2,4,16,128]{6,5,4,3,2,1,0:T(8,128)(2,1)S(1)} %copy-done.5, bf16[2,4,2,2,4,16,128]{6,5,4,3,2,1,0:T(8,128)(2,1)} %collective-permute-done.cross_ref, bf16[2,2,2,4,16,128]{5,4,3,2,1,0:T(8,128)(2,1)S(1)} %collective-permute-done.1.rest_0_, ...), custom_call_target="tpu_custom_call" | custom-call | flops 1 | bytes 20971520 | tf_op jit(solution)/shard_map/pallas_call | solution.py:310
  53.5 1.7 %copy-done.3 = bf16[4,256,1024]{2,1,0:T(8,128)(2,1)S(1)} copy-done((bf16[4,256,1024]{2,1,0:T(8,128)(2,1)S(1)}, bf16[4,256,1024]{2,1,0:T(8,128)(2,1)}, u32[]{:S(2)}) %copy-start.3) | copy-done | bytes 2097176
  55.3 1.9 %shard_map.141.spec = f32[2,1024,128]{2,1,0:T(8,128)S(1)} custom-call(bf16[8,2,4,32,128]{4,3,2,1,0:T(8,128)(2,1)} %all-to-all-done.1.own_ref, bf16[4,256,1024]{2,1,0:T(8,128)(2,1)S(1)} %copy-done.3, bf16[16,2,2,4,16,128]{5,4,3,2,1,0:T(8,128)(2,1)S(1)} %shard_map.140.after_ref.bank), custom_call_target="tpu_custom_call" | custom-call | flops 1 | bytes 1 | tf_op jit(solution)/shard_map/pallas_call | solution.py:310
  57.3 1.1 %shard_map.142.half_ref = bf16[8,528,128]{2,1,0:T(8,128)(2,1)S(1)} custom-call(f32[2,1024,128]{2,1,0:T(8,128)S(1)} %shard_map.141.spec, f32[4,256,128]{2,1,0:T(8,128)S(1)} %copy-done.2, bf16[4,2,256,512]{3,2,1,0:T(8,128)(2,1)S(1)} %copy-done, f32[2,1024,128]{2,1,0:T(8,128)S(1)} %copy-done.7, bf16[16,2,2,4,16,128]{5,4,3,2,1,0:T(8,128)(2,1)S(1)} %shard_map.140.after_ref.bank), custom_call_target="tpu_custom_call" | custom-call | flops 2000000000 | bytes 10485760 | tf_op jit(solution)/shard_map/pallas_call | solution.py:310
  58.4 1.5 %collective-permute-done.8.spec = f32[2,1024,128]{2,1,0:T(8,128)S(1)} collective-permute-done((f32[2,1024,128]{2,1,0:T(8,128)S(1)}, f32[2,1024,128]{2,1,0:T(8,128)S(1)}, u32[]{:S(2)}, u32[]{:S(2)}) %collective-permute-start.8) | collective-permute-done | bytes 1048608 | tf_op jit(solution)/shard_map/ppermute | solution.py:363
  59.9 1.2 %shard_map.143 = bf16[8,1040,128]{2,1,0:T(8,128)(2,1)S(1)} custom-call(f32[2,1024,128]{2,1,0:T(8,128)S(1)} %collective-permute-done.8.spec, f32[4,256,128]{2,1,0:T(8,128)S(1)} %copy-done.2, bf16[4,2,256,512]{3,2,1,0:T(8,128)(2,1)S(1)} %copy-done, f32[2,1024,128]{2,1,0:T(8,128)S(1)} %copy-done.7, ...), custom_call_target="tpu_custom_call" | custom-call | flops 2000000000 | bytes 10485760 | tf_op jit(solution)/shard_map/pallas_call | solution.py:310
  61.1 35.4 %all_to_all.15.in_ref = bf16[8,1040,128]{2,1,0:T(8,128)(2,1)S(1)} all-to-all(bf16[8,1040,128]{2,1,0:T(8,128)(2,1)S(1)} %shard_map.143), channel_id=1, replica_groups=mesh['tmpl'=16,'seg'=8] {'seg'}, dimensions={0} | all-to-all | bytes 4259840 | tf_op jit(solution)/shard_map/all_to_all | solution.py:374
  96.5 3.9 %shard_map.144 = f32[2,2,1024,128]{3,2,1,0:T(8,128)} custom-call(bf16[8,1040,128]{2,1,0:T(8,128)(2,1)S(1)} %all_to_all.15.in_ref, bf16[4,2,256,256]{3,2,1,0:T(8,128)(2,1)S(1)} %copy-done.19), custom_call_target="tpu_custom_call" | custom-call | flops 3000000000 | bytes 6291456 | tf_op jit(solution)/shard_map/pallas_call | solution.py:310
  (40 shorter events, 0.9 us)
Async XLA Ops:
  3.0 13.0 %copy-start.5 = (bf16[2,4,2,2,4,16,128]{6,5,4,3,2,1,0:T(8,128)(2,1)S(1)}, bf16[2,4,2,2,4,16,128]{6,5,4,3,2,1,0:T(8,128)(2,1)}, u32[]{:S(2)}) copy-start(bf16[2,4,2,2,4,16,128]{6,5,4,3,2,1,0:T(8,128)(2,1)} %get-tuple-element.18.near_ref) | copy-start | bytes 1572868
  3.0 13.0 %collective-permute-start = (bf16[2,4,2,2,4,16,128]{6,5,4,3,2,1,0:T(8,128)(2,1)}, bf16[2,4,2,2,4,16,128]{6,5,4,3,2,1,0:T(8,128)(2,1)}, u32[]{:S(2)}, u32[]{:S(2)}) collective-permute-start(bf16[2,4,2,2,4,16,128]{6,5,4,3,2,1,0:T(8,128)(2,1)} %get-tuple-element.19), channel_id=1, source_target_pairs={{0,8},{8,0},{16,24},{24,16},{32,40},{40,32},{48,56},{56,48},{64,72... | collective-permute-start | bytes 1572872 | tf_op jit(solution)/shard_map/ppermute | solution.py:341
  3.1 18.1 %copy-start.4 = (bf16[4,2,2,256,256]{4,3,2,1,0:T(8,128)(2,1)S(1)}, bf16[4,2,2,256,256]{4,3,2,1,0:T(8,128)(2,1)}, u32[]{:S(2)}) copy-start(bf16[4,2,2,256,256]{4,3,2,1,0:T(8,128)(2,1)} %constant.16.clone.table_ref) | copy-start | bytes 6291460
  3.1 18.0 %all-to-all-start = ((bf16[8,128,128]{2,1,0:T(8,128)(2,1)}), bf16[8,128,128]{2,1,0:T(8,128)(2,1)S(1)}, u32[]{:S(2)}, u32[]{:S(2)}) async-start(bf16[8,128,128]{2,1,0:T(8,128)(2,1)} %get-tuple-element.17), calls=%async_computation | async-start | bytes 524288 | tf_op jit(solution)/shard_map/all_to_all | solution.py:339
  11.1 1.2 %copy-start.8 = (f32[2,1024,128]{2,1,0:T(8,128)S(1)}, f32[2,1024,128]{2,1,0:T(8,128)}, u32[]{:S(2)}) copy-start(f32[2,1024,128]{2,1,0:T(8,128)} %constant.22.clone.shift_ref) | copy-start | bytes 3145732
  12.3 1.2 %copy-start.9 = (f32[2,1024,128]{2,1,0:T(8,128)S(1)}, f32[2,1024,128]{2,1,0:T(8,128)}, u32[]{:S(2)}) copy-start(f32[2,1024,128]{2,1,0:T(8,128)} %constant.21.clone.back_ref) | copy-start | bytes 3145732
  13.6 1.0 %copy-start.11 = (f32[1024,128]{1,0:T(8,128)S(1)}, f32[1024,128]{1,0:T(8,128)}, u32[]{:S(2)}) copy-start(f32[1024,128]{1,0:T(8,128)} %asd_ref.1) | copy-start | bytes 1572868
  15.0 1.0 copy-start.6
  15.9 8.8 %copy-start.1 = (f32[4,256,128]{2,1,0:T(8,128)}, f32[4,256,128]{2,1,0:T(8,128)S(1)}, u32[]{:S(2)}) copy-start(f32[4,256,128]{2,1,0:T(8,128)S(1)} %get-tuple-element.21.also_ref.weight_ref) | copy-start | bytes 1572868
  17.2 0.7 copy-start.13
  17.9 0.7 copy-start.14
  18.5 0.6 copy-start.15
  19.2 0.6 copy-start.16
  19.8 0.7 copy-start.17
  20.5 0.6 copy-start.18
  21.1 1.2 %copy-start.10 = (f32[2,128,1024]{2,1,0:T(8,128)S(1)}, f32[2,128,1024]{2,1,0:T(8,128)}, u32[]{:S(2)}) copy-start(f32[2,128,1024]{2,1,0:T(8,128)} %constant.17.clone.fine_ref) | copy-start | bytes 3145732
  22.4 0.8 copy-start.12
  24.7 28.8 %all-to-all-start.1 = ((bf16[8,2,4,32,128]{4,3,2,1,0:T(8,128)(2,1)}), bf16[8,2,4,32,128]{4,3,2,1,0:T(8,128)(2,1)}, u32[]{:S(2)}, u32[]{:S(2)}) async-start(bf16[8,2,4,32,128]{4,3,2,1,0:T(8,128)(2,1)} %shard_map.139), calls=%async_computation.1 | async-start | bytes 1048576 | tf_op jit(solution)/shard_map/all_to_all | solution.py:358
  31.9 7.6 %collective-permute-start.2 = (bf16[2,2,2,4,16,128]{5,4,3,2,1,0:T(8,128)(2,1)}, bf16[2,2,2,4,16,128]{5,4,3,2,1,0:T(8,128)(2,1)S(1)}, u32[]{:S(2)}, u32[]{:S(2)}) collective-permute-start(bf16[2,2,2,4,16,128]{5,4,3,2,1,0:T(8,128)(2,1)} %copy-done.18), channel_id=1, source_target_pairs={{0,64},{8,72},{16,80},{24,88},{32,96},{40,104},{48,112},{56,120},{... | collective-permute-start | bytes 393224 | tf_op jit(solution)/shard_map/ppermute | solution.py:346
  34.9 8.3 %collective-permute-start.3 = (bf16[2,2,2,4,16,128]{5,4,3,2,1,0:T(8,128)(2,1)}, bf16[2,2,2,4,16,128]{5,4,3,2,1,0:T(8,128)(2,1)S(1)}, u32[]{:S(2)}, u32[]{:S(2)}) collective-permute-start(bf16[2,2,2,4,16,128]{5,4,3,2,1,0:T(8,128)(2,1)} %copy-done.17), channel_id=1, source_target_pairs={{0,96},{8,104},{16,112},{24,120},{32,0},{40,8},{48,16},{56,24},{64... | collective-permute-start | bytes 393224 | tf_op jit(solution)/shard_map/ppermute | solution.py:346
  36.1 15.8 %collective-permute-start.4 = (bf16[2,2,2,4,16,128]{5,4,3,2,1,0:T(8,128)(2,1)}, bf16[2,2,2,4,16,128]{5,4,3,2,1,0:T(8,128)(2,1)S(1)}, u32[]{:S(2)}, u32[]{:S(2)}) collective-permute-start(bf16[2,2,2,4,16,128]{5,4,3,2,1,0:T(8,128)(2,1)} %copy-done.16), channel_id=1, source_target_pairs={{0,16},{8,24},{16,0},{24,8},{32,48},{40,56},{48,32},{56,40},{64,80... | collective-permute-start | bytes 393224 | tf_op jit(solution)/shard_map/ppermute | solution.py:346
  37.1 14.8 %collective-permute-start.5 = (bf16[2,2,2,4,16,128]{5,4,3,2,1,0:T(8,128)(2,1)}, bf16[2,2,2,4,16,128]{5,4,3,2,1,0:T(8,128)(2,1)S(1)}, u32[]{:S(2)}, u32[]{:S(2)}) collective-permute-start(bf16[2,2,2,4,16,128]{5,4,3,2,1,0:T(8,128)(2,1)} %copy-done.15), channel_id=1, source_target_pairs={{0,48},{8,56},{16,32},{24,40},{32,80},{40,88},{48,64},{56,72},{64,... | collective-permute-start | bytes 393224 | tf_op jit(solution)/shard_map/ppermute | solution.py:346
  38.4 13.4 %collective-permute-start.6 = (bf16[2,2,2,4,16,128]{5,4,3,2,1,0:T(8,128)(2,1)}, bf16[2,2,2,4,16,128]{5,4,3,2,1,0:T(8,128)(2,1)S(1)}, u32[]{:S(2)}, u32[]{:S(2)}) collective-permute-start(bf16[2,2,2,4,16,128]{5,4,3,2,1,0:T(8,128)(2,1)} %copy-done.14), channel_id=1, source_target_pairs={{0,80},{8,88},{16,64},{24,72},{32,112},{40,120},{48,96},{56,104},{... | collective-permute-start | bytes 393224 | tf_op jit(solution)/shard_map/ppermute | solution.py:346
  39.4 12.4 %collective-permute-start.7 = (bf16[2,2,2,4,16,128]{5,4,3,2,1,0:T(8,128)(2,1)}, bf16[2,2,2,4,16,128]{5,4,3,2,1,0:T(8,128)(2,1)S(1)}, u32[]{:S(2)}, u32[]{:S(2)}) collective-permute-start(bf16[2,2,2,4,16,128]{5,4,3,2,1,0:T(8,128)(2,1)} %copy-done.13), channel_id=1, source_target_pairs={{0,112},{8,120},{16,96},{24,104},{32,16},{40,24},{48,0},{56,8},{64... | collective-permute-start | bytes 393224 | tf_op jit(solution)/shard_map/ppermute | solution.py:346
  43.2 8.6 %collective-permute-start.1 = (bf16[2,2,2,4,16,128]{5,4,3,2,1,0:T(8,128)(2,1)S(1)}, bf16[2,2,2,4,16,128]{5,4,3,2,1,0:T(8,128)(2,1)S(1)}, u32[]{:S(2)}, u32[]{:S(2)}) collective-permute-start(bf16[2,2,2,4,16,128]{5,4,3,2,1,0:T(8,128)(2,1)S(1)} %get-tuple-element.20.after_ref), channel_id=1, source_target_pairs={{0,32},{8,40},{16,48},{24,56},{32,64},{40,72},{48,80},{56,88},{64,... | collective-permute-start | bytes 393224 | tf_op jit(solution)/shard_map/ppermute | solution.py:346
  53.5 3.8 %copy-start = (bf16[4,2,256,512]{3,2,1,0:T(8,128)(2,1)S(1)}, bf16[4,2,256,512]{3,2,1,0:T(8,128)(2,1)}, u32[]{:S(2)}) copy-start(bf16[4,2,256,512]{3,2,1,0:T(8,128)(2,1)} %constant.20.clone.third_ref) | copy-start | bytes 6291460
  53.5 1.7 %copy-start.3 = (bf16[4,256,1024]{2,1,0:T(8,128)(2,1)S(1)}, bf16[4,256,1024]{2,1,0:T(8,128)(2,1)}, u32[]{:S(2)}) copy-start(bf16[4,256,1024]{2,1,0:T(8,128)(2,1)} %constant.19.clone.table_ref) | copy-start | bytes 6291460
  55.3 2.0 %copy-start.2 = (f32[4,256,128]{2,1,0:T(8,128)S(1)}, f32[4,256,128]{2,1,0:T(8,128)}, u32[]{:S(2)}) copy-start(f32[4,256,128]{2,1,0:T(8,128)} %copy-done.1) | copy-start | bytes 1572868
  55.3 2.0 %copy-start.7 = (f32[2,1024,128]{2,1,0:T(8,128)S(1)}, f32[2,1024,128]{2,1,0:T(8,128)}, u32[]{:S(2)}) copy-start(f32[2,1024,128]{2,1,0:T(8,128)} %copy-done.6) | copy-start | bytes 3145732
  57.2 2.7 %collective-permute-start.8 = (f32[2,1024,128]{2,1,0:T(8,128)S(1)}, f32[2,1024,128]{2,1,0:T(8,128)S(1)}, u32[]{:S(2)}, u32[]{:S(2)}) collective-permute-start(f32[2,1024,128]{2,1,0:T(8,128)S(1)} %shard_map.141.spec), channel_id=1, source_target_pairs={{0,8},{8,0},{16,24},{24,16},{32,40},{40,32},{48,56},{56,48},{64,72... | collective-permute-start | bytes 3145736 | tf_op jit(solution)/shard_map/ppermute | solution.py:363
  61.1 35.4 %copy-start.19 = (bf16[4,2,256,256]{3,2,1,0:T(8,128)(2,1)S(1)}, bf16[4,2,256,256]{3,2,1,0:T(8,128)(2,1)}, u32[]{:S(2)}) copy-start(bf16[4,2,256,256]{3,2,1,0:T(8,128)(2,1)} %constant.23.clone.table_ref) | copy-start | bytes 3145732

commit v2 on v1

--- a/solution.py
+++ b/solution.py
@@ -16,7 +16,7 @@
 SMEM = pl.BlockSpec(memory_space=pltpu.SMEM)
 ANY = pl.BlockSpec(memory_space=pl.ANY)
 MIB = 1 << 20
-OFFSETS = [(rz, rx) for rz in range(2) for rx in range(4)][1:]
+OFFSETS = [(rz, rx) for rz in range(2) for rx in range(4)]
 
 
 def phases(product, count):
@@ -38,12 +38,10 @@
     for r in range(4):
         c, s = phases((4 * q[:, None] + r) * q[None, :], 1024)
         first.append(np.stack([np.stack(split_hi_lo(c)), np.stack(split_hi_lo(-s))]))
-    rows = np.array([4 * (i % 32) + i // 32 for i in range(128)])
     k2 = np.arange(1024)
+    rows = np.concatenate([4 * np.arange(32), 128 * np.arange(8), np.arange(8)])
     c, s = phases(rows[:, None] * k2[None, :], NSAMP)
-    fine = np.stack([c, -s]).astype(np.float32)
-    c, s = phases(128 * np.arange(8)[:, None] * k2[None, :], NSAMP)
-    base = np.stack([c, -s]).astype(np.float32)
+    turn = np.stack([c, -s]).astype(np.float32)
     second = []
     for r in range(4):
         c, s = phases(q[:, None] * (4 * q[None, :] + r), 1024)
@@ -65,8 +63,7 @@
         last.append(np.stack([c, s]).astype(np.float32))
     return dict(
         first=np.stack(first),
-        fine=fine,
-        base=base,
+        turn=turn,
         second=np.stack(second),
         third=np.stack(third).astype(jnp.bfloat16),
         back=back,
@@ -89,9 +86,11 @@
 
 
 def gate_kernel(
-    strain_ref, start_any, span_any, assign_any, bank_any, out_ref, near_ref, cross_ref,
-    strain, bank_ref, start_ref, span_ref, assign_ref, sems,
+    strain_ref, start_any, span_any, assign_any, bank_any, asd_any, back_any, shift_any,
+    out_ref, weight_ref, twist_ref, *rest
 ):
+    pick_refs, rest = rest[:8], rest[8:]
+    strain, bank_ref, start_ref, span_ref, assign_ref, asd_ref, back_ref, shift_ref, sems = rest
     x, z, core = place()
     copies = [
         pltpu.make_async_copy(start_any, start_ref, sems.at[0]),
@@ -99,6 +98,9 @@
         pltpu.make_async_copy(strain_ref.at[core], strain, sems.at[2]),
         pltpu.make_async_copy(assign_any, assign_ref, sems.at[3]),
         pltpu.make_async_copy(bank_any, bank_ref, sems.at[4]),
+        pltpu.make_async_copy(asd_any, asd_ref, sems.at[5]),
+        pltpu.make_async_copy(back_any, back_ref, sems.at[6]),
+        pltpu.make_async_copy(shift_any, shift_ref, sems.at[7]),
     ]
     for copy in copies:
         copy.start()
@@ -123,25 +125,24 @@
     for dest in range(8):
         out_ref[dest] = ordered[:, 128 * dest : 128 * dest + 128]
 
-    for copy in copies[3:]:
+    for copy in copies[3:5]:
         copy.wait()
     for i in range(16):
-        rc, rz, rx = i // 8, i // 4 % 2, i % 4
+        rz, rx, rc = i // 8, i // 2 % 4, i % 2
         dest = ((x + rx) % 4) * 4 + (z + rz) % 2 * 2 + (core + rc) % 2
         for slot in range(2):
             chosen = assign_ref[2 * dest + slot]
             for part in range(2):
                 for p in range(4):
                     value = bank_ref[part, chosen, pl.ds(p, 16, stride=4), :].astype(BF)
-                    (near_ref, cross_ref)[rc][rz, rx, slot, part, p] = value
-
-
-def prepare_kernel(asd_ref, back_ref, shift_ref, weight_ref, twist_ref):
+                    pick_refs[i // 2][rc, slot, part, p] = value
+
+    for copy in copies[5:]:
+        copy.wait()
     for p in range(4):
         asd = asd_ref[pl.ds(p, 256, stride=4), :]
         weight_ref[p] = 1.0 / (asd * asd)
-    seg = lax.axis_index("seg")
-    own = lax.broadcasted_iota(jnp.int32, (128, 128), 1) == seg
+    own = lane == lax.axis_index("seg")
     for i in range(8):
         rows = slice(128 * i, 128 * i + 128)
         shift = [jnp.sum(jnp.where(own, shift_ref[part, rows, :], 0.0), axis=1, keepdims=True) for part in range(2)]
@@ -150,10 +151,14 @@
         twist_ref[1, rows, :] = re * shift[1] + im * shift[0]
 
 
-def pack_kernel(near_ref, cross_ref, *out_refs):
-    for i, (rz, rx) in enumerate(OFFSETS):
-        out_refs[i][0] = near_ref[rz, rx]
-        out_refs[i][1] = cross_ref[rz, rx]
+def pack_kernel(*refs):
+    piece_refs, out_ref, token_ref, sems = refs[:8], *refs[8:]
+    token_ref[...] = jnp.zeros_like(token_ref)
+    copies = [pltpu.make_async_copy(piece_refs[i].at[1], out_ref.at[i], sems.at[i]) for i in range(8)]
+    for copy in copies:
+        copy.start()
+    for copy in copies:
+        copy.wait()
 
 
 def four_way(sign, parts):
@@ -169,28 +174,31 @@
     return ((sr + ur, si + ui), (tr + wr, ti + wi), (sr - ur, si - ui), (tr - wr, ti - wi))
 
 
-def first_kernel(cols_ref, table_ref, fine_ref, base_ref, after_ref, also_ref, out_ref, z_ref):
-    del after_ref, also_ref
-    seg = lax.axis_index("seg")
+def first_kernel(cols_ref, table_ref, turn_ref, after_ref, out_ref, z_ref):
+    del after_ref
     for r in range(4):
         turned = cols_ref[:, 32 * r : 32 * r + 32, :].reshape(256, 128).T
         for part in range(2):
             z_ref[r, part] = dot(turned, table_ref[r, part, 0]) + dot(turned, table_ref[r, part, 1])
-    base_re = base_ref[0, pl.ds(seg, 1), :]
-    base_im = base_ref[1, pl.ds(seg, 1), :]
-    for i in range(8):
-        rows = slice(16 * i, 16 * i + 16)
-        at = slice(i % 2 * 16, i % 2 * 16 + 16)
-        fr, fi = fine_ref[0, rows, :], fine_ref[1, rows, :]
-        tr = fr * base_re - fi * base_im
-        ti = fr * base_im + fi * base_re
-        outs = four_way(-1, [(z_ref[r, 0, rows, :], z_ref[r, 1, rows, :]) for r in range(4)])
-        for k, (re, im) in enumerate(outs):
-            wr, wi = tr[:, 256 * k : 256 * k + 256], ti[:, 256 * k : 256 * k + 256]
-            done = ((re * wr - im * wi).astype(BF), (re * wi + im * wr).astype(BF))
-            for half in range(2):
-                for part in range(2):
-                    out_ref[2 * k + half, part, i // 2, at] = done[part][:, 128 * half : 128 * half + 128]
+    seg = 32 + lax.axis_index("seg")
+    seg_re, seg_im = turn_ref[0, pl.ds(seg, 1), :], turn_ref[1, pl.ds(seg, 1), :]
+    for r1 in range(4):
+        low_re, low_im = turn_ref[0, 40 + r1 : 41 + r1, :], turn_ref[1, 40 + r1 : 41 + r1, :]
+        base_re = low_re * seg_re - low_im * seg_im
+        base_im = low_re * seg_im + low_im * seg_re
+        for i in range(2):
+            at = slice(16 * i, 16 * i + 16)
+            rows = slice(32 * r1 + 16 * i, 32 * r1 + 16 * i + 16)
+            fr, fi = turn_ref[0, at, :], turn_ref[1, at, :]
+            tr = fr * base_re - fi * base_im
+            ti = fr * base_im + fi * base_re
+            outs = four_way(-1, [(z_ref[r, 0, rows, :], z_ref[r, 1, rows, :]) for r in range(4)])
+            for k, (re, im) in enumerate(outs):
+                wr, wi = tr[:, 256 * k : 256 * k + 256], ti[:, 256 * k : 256 * k + 256]
+                done = ((re * wr - im * wi).astype(BF), (re * wi + im * wr).astype(BF))
+                for half in range(2):
+                    for part in range(2):
+                        out_ref[2 * k + half, part, r1, at] = done[part][:, 128 * half : 128 * half + 128]
 
 
 def second_kernel(own_ref, table_ref, after_ref, spec_ref, z_ref):
@@ -208,14 +216,14 @@
                 spec_ref[part, 256 * k + 32 * i : 256 * k + 32 * i + 32, :] = parts[part]
 
 
-def assemble_kernel(near_ref, cross_ref, *rest):
-    moved_refs, bank, sems = rest[:7], rest[7], rest[8]
+def assemble_kernel(*refs):
+    piece_refs, cross_ref, bank, sems = refs[:8], refs[8], refs[9], refs[10]
     x, z, core = place()
     copies = []
-    for i, (rz, rx) in enumerate([(0, 0)] + OFFSETS):
+    for i in range(8):
         for rc in range(2):
-            src = (near_ref, cross_ref)[rc].at[0, 0] if i == 0 else moved_refs[i - 1].at[rc]
-            origin = ((x + 4 - rx) % 4) * 4 + (z + rz) % 2 * 2 + (core + rc) % 2
+            src = piece_refs[i].at[0] if rc == 0 else cross_ref.at[i]
+            origin = ((x + 4 - i % 4) % 4) * 4 + (z + i // 4) % 2 * 2 + (core + rc) % 2
             copies.append(pltpu.make_async_copy(src, bank.at[origin], sems.at[len(copies)]))
     for copy in copies:
         copy.start()
@@ -306,12 +314,12 @@
             out_ref[seg, slot, pl.ds(p, 256, stride=4), :] = jnp.sqrt(sr * sr + si * si) * scales[slot]
 
 
-def call(kernel, ins, outs, specs, flops, moved, scratch=(), limit=16):
+def call(kernel, ins, outs, specs, flops, moved, scratch=(), limit=16, space=VMEM):
     return pl.pallas_call(
         kernel,
         out_shape=outs,
         in_specs=specs,
-        out_specs=jax.tree.map(lambda _: VMEM, outs),
+        out_specs=space if isinstance(space, tuple) else jax.tree.map(lambda _: space, outs),
         scratch_shapes=list(scratch),
         compiler_params=pltpu.CompilerParams(vmem_limit_bytes=limit * MIB),
         cost_estimate=pl.CostEstimate(flops=flops, bytes_accessed=moved, transcendentals=0),
@@ -327,33 +335,38 @@
     swap_core = [(i, i ^ 1) for i in range(16)]
 
     blk = (2, 2, 4, 16, 128)
-    gated, near, cross = call(
-        gate_kernel, (strain, gate_start, gate_span, assign, bank),
-        (shape(8, 128, 128), shape(2, 4, *blk), shape(2, 4, *blk)), [ANY] * 5, 10**8, 4 * MIB,
+    gated, weight, twist, *picked = call(
+        gate_kernel, (strain, gate_start, gate_span, assign, bank, asd, const["back"], const["shift"]),
+        (
+            shape(8, 128, 128), shape(4, 256, 128, dtype=F32), shape(2, 1024, 128, dtype=F32),
+            *[shape(2, *blk)] * 8,
+        ),
+        [ANY] * 8, 10**8, 4 * MIB,
         [
             pltpu.VMEM((128, 1024), F32), pltpu.VMEM((2, 32, 64, 128), F32), pltpu.SMEM((2, 1, 2), jnp.int32),
-            pltpu.SMEM((2, 1, 2), jnp.int32), pltpu.SMEM((32,), jnp.int32), pltpu.SemaphoreType.DMA((5,)),
+            pltpu.SMEM((2, 1, 2), jnp.int32), pltpu.SMEM((32,), jnp.int32), pltpu.VMEM((1024, 128), F32),
+            pltpu.VMEM((2, 1024, 128), F32), pltpu.VMEM((2, 1024, 128), F32), pltpu.SemaphoreType.DMA((8,)),
         ],
         limit=63,
     )
     columns = lax.all_to_all(gated, "seg", 0, 0)
 
-    cross = lax.ppermute(cross, "tmpl", swap_core)
-    sends = call(pack_kernel, (near, cross), (shape(2, *blk),) * 7, [VMEM] * 2, 10**6, 2 * MIB)
-    moved = []
-    for (rz, rx), send in zip(OFFSETS, sends):
+    pieces = picked[:1]
+    for (rz, rx), send in zip(OFFSETS[1:], picked[1:]):
         hop = [(i, (i // 4 + rx) % 4 * 4 + i % 4 ^ 2 * rz) for i in range(16)]
-        moved.append(lax.ppermute(send, "tmpl", hop))
+        pieces.append(lax.ppermute(send, "tmpl", hop))
+    cross, token = call(
+        pack_kernel, pieces, (shape(8, *blk), shape(8, 128, dtype=F32)), [ANY] * 8, 1, 10 * MIB,
+        [pltpu.SemaphoreType.DMA((8,))], limit=8, space=(ANY, VMEM),
+    )
+    crossed = lax.ppermute(cross, "tmpl", swap_core)
     ordered = call(
-        assemble_kernel, (near, cross, *moved), shape(16, *blk), [ANY] * 9, 1, 20 * MIB, [pltpu.SemaphoreType.DMA((16,))]
-    )
-    weight, twist = call(
-        prepare_kernel, (asd, const["back"], const["shift"]),
-        (shape(4, 256, 128, dtype=F32), shape(2, 1024, 128, dtype=F32)), [VMEM] * 3, 1, 40 * MIB,
+        assemble_kernel, (*pieces, crossed), shape(16, *blk), [ANY] * 9, 1, 10 * MIB, [pltpu.SemaphoreType.DMA((16,))],
+        limit=8,
     )
     turned = call(
-        first_kernel, (columns, const["first"], const["fine"], const["base"], sends[0], weight),
-        shape(8, 2, 4, 32, 128), [VMEM] * 4 + [ANY] * 2, 3 * 10**8, 4 * MIB, [pltpu.VMEM((4, 2, 128, 256), F32)],
+        first_kernel, (columns, const["first"], const["turn"], token),
+        shape(8, 2, 4, 32, 128), [VMEM] * 3 + [ANY], 3 * 10**8, 4 * MIB, [pltpu.VMEM((4, 2, 128, 256), F32)],
     )
     own = lax.all_to_all(turned, "seg", 0, 0)
     spec = call(

time: 101 us -> 101 us (level)
  waiting for transfers between devices: 9.78 us -> 21.5 us
  local copies, waits for them, and re-layouts: 12.2 us -> 4.1 us
  blocking collectives: 35.4 us -> 32.1 us
  starting transfers between devices: 27 us -> 25.6 us
    all_to_all x1, waiting for transfers between devices: 0.01 us -> 10.7 us  [per_device(): own = lax.all_to_all(turned, 'seg', 0, 0)]
    unnamed x40 -> x18, local copies, waits for them, and re-layouts: 12.2 us -> 4.1 us
    all_to_all x1, blocking collectives: 35.4 us -> 32.1 us  [per_device(): series = lax.all_to_all(inner, 'seg', 0, 0)]
    ppermute x8, waiting for transfers between devices: 8.31 us -> 9.36 us  [the longest x7 9.36 us: per_device(): pieces.append(lax.ppermute(send, 'tmpl', hop))]
    pallas_call x9 -> x8, Pallas kernels: 15.9 us -> 16.2 us  [call(): pl.pallas_call(kernel, out_shape=outs, in_specs=specs, out_specs=space if...]
  transfers between devices with their start and end apart: 11 -> 11, of which waited for: 2 -> 3; matrix products, arithmetic and copies ran while one was open for 0% -> 0% of each run, Pallas kernels for 4% -> 5%
where the time goes in v2:
time: 101 us; the launch traced here: 99.7 us
  blocking collectives  32.1 us (32%)
  starting transfers between devices  25.6 us (25%)
  waiting for transfers between devices  21.5 us (21%)
  Pallas kernels  16.2 us (16%)
  local copies, waits for them, and re-layouts  4.1 us (4%)
    all_to_all x1, blocking collectives, per_device(): series = lax.all_to_all(inner, 'seg', 0, 0)  32.1 us
    pallas_call x8, Pallas kernels, call(): pl.pallas_call(kernel, out_shape=outs, in_specs=specs, out_specs=space if...  16.2 us
    ppermute x7, starting transfers between devices, per_device(): pieces.append(lax.ppermute(send, 'tmpl', hop))  11.3 us
    all_to_all x1, waiting for transfers between devices, per_device(): own = lax.all_to_all(turned, 'seg', 0, 0)  10.7 us
    ppermute x7, waiting for transfers between devices, per_device(): pieces.append(lax.ppermute(send, 'tmpl', hop))  9.36 us
    all_to_all x1, starting transfers between devices, per_device(): columns = lax.all_to_all(gated, 'seg', 0, 0)  7.78 us
    all_to_all x1, starting transfers between devices, per_device(): own = lax.all_to_all(turned, 'seg', 0, 0)  6.36 us
    unnamed x18, local copies, waits for them, and re-layouts  4.1 us
  transfers between devices with their start and end apart: 11, of which 3 were waited for; matrix products, arithmetic and copies ran while one was open for 0% of the time, Pallas kernels for 5%

profile of v2, /device:TPU:0, one launch (start us, length us, event | category | flops | bytes accessed | tf_op | source)
XLA Modules:
  0.0 99.7 jit_solution(12634700027020695995)
XLA Ops:
  0.0 4.2 %shard_map.127 = (bf16[8,128,128]{2,1,0:T(8,128)(2,1)}, f32[4,256,128]{2,1,0:T(8,128)}, f32[2,1024,128]{2,1,0:T(8,128)}, bf16[2,2,2,4,16,128]{5,4,3,2,1,0:T(8,12...) custom-call(f32[2,128,1024]{2,1,0:T(8,128)} %strain_ref.1, ...), custom_call_target="tpu_custom_call" | custom-call | flops 100000000 | bytes 4194304 | tf_op jit(solution)/shard_map/pallas_call | solution.py:318
  4.2 1.6 %collective-permute-start = (bf16[2,2,2,4,16,128]{5,4,3,2,1,0:T(8,128)(2,1)}, bf16[2,2,2,4,16,128]{5,4,3,2,1,0:T(8,128)(2,1)S(1)}, u32[]{:S(2)}, u32[]{:S(2)}) collective-permute-start(bf16[2,2,2,4,16,128]{5,4,3,2,1,0:T(8,128)(2,1)} %get-tuple-element.20), channel_id=1, source_target_pairs={{0,32},{8,40},{16,48},{24,56},{32,64},{40,72},{48,80},{56,88},{64,... | collective-permute-start | bytes 393224 | tf_op jit(solution)/shard_map/ppermute | solution.py:357
  5.9 2.7 %collective-permute-start.1 = (bf16[2,2,2,4,16,128]{5,4,3,2,1,0:T(8,128)(2,1)}, bf16[2,2,2,4,16,128]{5,4,3,2,1,0:T(8,128)(2,1)S(1)}, u32[]{:S(2)}, u32[]{:S(2)}) collective-permute-start(bf16[2,2,2,4,16,128]{5,4,3,2,1,0:T(8,128)(2,1)} %get-tuple-element.21), channel_id=1, source_target_pairs={{0,64},{8,72},{16,80},{24,88},{32,96},{40,104},{48,112},{56,120},{... | collective-permute-start | bytes 393224 | tf_op jit(solution)/shard_map/ppermute | solution.py:357
  8.6 7.8 %all-to-all-start = ((bf16[8,128,128]{2,1,0:T(8,128)(2,1)}), bf16[8,128,128]{2,1,0:T(8,128)(2,1)S(1)}, u32[]{:S(2)}, u32[]{:S(2)}) async-start(bf16[8,128,128]{2,1,0:T(8,128)(2,1)} %get-tuple-element.18), calls=%async_computation | async-start | bytes 524288 | tf_op jit(solution)/shard_map/all_to_all | solution.py:352
  16.4 1.4 %collective-permute-start.2 = (bf16[2,2,2,4,16,128]{5,4,3,2,1,0:T(8,128)(2,1)}, bf16[2,2,2,4,16,128]{5,4,3,2,1,0:T(8,128)(2,1)S(1)}, u32[]{:S(2)}, u32[]{:S(2)}) collective-permute-start(bf16[2,2,2,4,16,128]{5,4,3,2,1,0:T(8,128)(2,1)} %get-tuple-element.22), channel_id=1, source_target_pairs={{0,96},{8,104},{16,112},{24,120},{32,0},{40,8},{48,16},{56,24},{64... | collective-permute-start | bytes 393224 | tf_op jit(solution)/shard_map/ppermute | solution.py:357
  17.8 1.0 %collective-permute-start.3 = (bf16[2,2,2,4,16,128]{5,4,3,2,1,0:T(8,128)(2,1)}, bf16[2,2,2,4,16,128]{5,4,3,2,1,0:T(8,128)(2,1)S(1)}, u32[]{:S(2)}, u32[]{:S(2)}) collective-permute-start(bf16[2,2,2,4,16,128]{5,4,3,2,1,0:T(8,128)(2,1)} %get-tuple-element.23), channel_id=1, source_target_pairs={{0,16},{8,24},{16,0},{24,8},{32,48},{40,56},{48,32},{56,40},{64,80... | collective-permute-start | bytes 393224 | tf_op jit(solution)/shard_map/ppermute | solution.py:357
  18.8 1.0 %collective-permute-start.4 = (bf16[2,2,2,4,16,128]{5,4,3,2,1,0:T(8,128)(2,1)}, bf16[2,2,2,4,16,128]{5,4,3,2,1,0:T(8,128)(2,1)S(1)}, u32[]{:S(2)}, u32[]{:S(2)}) collective-permute-start(bf16[2,2,2,4,16,128]{5,4,3,2,1,0:T(8,128)(2,1)} %get-tuple-element.24), channel_id=1, source_target_pairs={{0,48},{8,56},{16,32},{24,40},{32,80},{40,88},{48,64},{56,72},{64,... | collective-permute-start | bytes 393224 | tf_op jit(solution)/shard_map/ppermute | solution.py:357
  19.9 0.0 collective-permute-done.refs_1_
  19.9 1.4 %collective-permute-start.5 = (bf16[2,2,2,4,16,128]{5,4,3,2,1,0:T(8,128)(2,1)}, bf16[2,2,2,4,16,128]{5,4,3,2,1,0:T(8,128)(2,1)S(1)}, u32[]{:S(2)}, u32[]{:S(2)}) collective-permute-start(bf16[2,2,2,4,16,128]{5,4,3,2,1,0:T(8,128)(2,1)} %get-tuple-element.25), channel_id=1, source_target_pairs={{0,80},{8,88},{16,64},{24,72},{32,112},{40,120},{48,96},{56,104},{... | collective-permute-start | bytes 393224 | tf_op jit(solution)/shard_map/ppermute | solution.py:357
  21.3 0.0 collective-permute-done.1.refs_2_
  21.3 2.0 %collective-permute-start.6 = (bf16[2,2,2,4,16,128]{5,4,3,2,1,0:T(8,128)(2,1)}, bf16[2,2,2,4,16,128]{5,4,3,2,1,0:T(8,128)(2,1)S(1)}, u32[]{:S(2)}, u32[]{:S(2)}) collective-permute-start(bf16[2,2,2,4,16,128]{5,4,3,2,1,0:T(8,128)(2,1)} %get-tuple-element.26), channel_id=1, source_target_pairs={{0,112},{8,120},{16,96},{24,104},{32,16},{40,24},{48,0},{56,8},{64... | collective-permute-start | bytes 393224 | tf_op jit(solution)/shard_map/ppermute | solution.py:357
  23.3 0.0 collective-permute-done.2.refs_3_
  23.3 9.3 %collective-permute-done.3.refs_4_ = bf16[2,2,2,4,16,128]{5,4,3,2,1,0:T(8,128)(2,1)S(1)} collective-permute-done((bf16[2,2,2,4,16,128]{5,4,3,2,1,0:T(8,128)(2,1)}, bf16[2,2,2,4,16,128]{5,4,3,2,1,0:T(8,128)(2,1)S(1)}, u32[]{:S(2)}, u32[]{:S(2)}) %collective-permute-start.3) | collective-permute-done | bytes 131104 | tf_op jit(solution)/shard_map/ppermute | solution.py:357
  32.7 0.9 copy-done.5
  33.6 0.7 shard_map.128
  34.3 0.1 collective-permute-start.7
  34.4 0.0 copy-start.1
  34.5 1.6 %copy-done.1 = bf16[4,2,2,256,256]{4,3,2,1,0:T(8,128)(2,1)S(1)} copy-done((bf16[4,2,2,256,256]{4,3,2,1,0:T(8,128)(2,1)S(1)}, bf16[4,2,2,256,256]{4,3,2,1,0:T(8,128)(2,1)}, u32[]{:S(2)}) %copy-start.1) | copy-done | bytes 2097176
  36.0 1.5 %shard_map.129 = bf16[8,2,4,32,128]{4,3,2,1,0:T(8,128)(2,1)} custom-call(bf16[8,128,128]{2,1,0:T(8,128)(2,1)S(1)} %all-to-all-done.cols_ref, bf16[4,2,2,256,256]{4,3,2,1,0:T(8,128)(2,1)S(1)} %copy-done.1, f32[2,48,1024]{2,1,0:T(8,128)S(1)} %copy-done.7, f32[8,128]{1,0:T(8,128)S(1)} %get-tuple-element.27.after_ref), custom_call_target="tpu_custom_call" | custom-call | flops 300000000 | bytes 4194304 | tf_op jit(solution)/shard_map/pallas_call | solution.py:318
  37.5 6.4 %all-to-all-start.1 = ((bf16[8,2,4,32,128]{4,3,2,1,0:T(8,128)(2,1)}), bf16[8,2,4,32,128]{4,3,2,1,0:T(8,128)(2,1)}, u32[]{:S(2)}, u32[]{:S(2)}) async-start(bf16[8,2,4,32,128]{4,3,2,1,0:T(8,128)(2,1)} %shard_map.129), calls=%async_computation.1 | async-start | bytes 1048576 | tf_op jit(solution)/shard_map/all_to_all | solution.py:371
  43.9 1.6 %shard_map.130.after_ref.bank = bf16[16,2,2,4,16,128]{5,4,3,2,1,0:T(8,128)(2,1)S(1)} custom-call(bf16[2,2,2,4,16,128]{5,4,3,2,1,0:T(8,128)(2,1)S(1)} %copy-done.6, bf16[2,2,2,4,16,128]{5,4,3,2,1,0:T(8,128)(2,1)S(1)} %collective-permute-done.refs_1_, bf16[2,2,2,4,16,128]{5,4,3,2,1,0:T(8,128)(2,1)S(1)} %collective-permute-done.1.refs_2_, ...), custom_call_target="tpu_custom_call" | custom-call | flops 1 | bytes 10485760 | tf_op jit(solution)/shard_map/pallas_call | solution.py:318
  45.6 0.0 copy-start
  45.6 10.7 %all-to-all-done.1.own_ref = bf16[8,2,4,32,128]{4,3,2,1,0:T(8,128)(2,1)} async-done(((bf16[8,2,4,32,128]{4,3,2,1,0:T(8,128)(2,1)}), bf16[8,2,4,32,128]{4,3,2,1,0:T(8,128)(2,1)}, u32[]{:S(2)}, u32[]{:S(2)}) %all-to-all-start.1) | async-done | bytes 524320 | tf_op jit(solution)/shard_map/all_to_all | solution.py:371
  56.2 1.6 %copy-done.2 = bf16[4,256,1024]{2,1,0:T(8,128)(2,1)S(1)} copy-done((bf16[4,256,1024]{2,1,0:T(8,128)(2,1)S(1)}, bf16[4,256,1024]{2,1,0:T(8,128)(2,1)}, u32[]{:S(2)}) %copy-start.2) | copy-done | bytes 2097176
  57.8 1.9 %shard_map.131.spec = f32[2,1024,128]{2,1,0:T(8,128)S(1)} custom-call(bf16[8,2,4,32,128]{4,3,2,1,0:T(8,128)(2,1)} %all-to-all-done.1.own_ref, bf16[4,256,1024]{2,1,0:T(8,128)(2,1)S(1)} %copy-done.2, bf16[16,2,2,4,16,128]{5,4,3,2,1,0:T(8,128)(2,1)S(1)} %shard_map.130.after_ref.bank), custom_call_target="tpu_custom_call" | custom-call | flops 1 | bytes 1 | tf_op jit(solution)/shard_map/pallas_call | solution.py:318
  59.7 0.1 collective-permute-start.8
  59.9 1.1 %shard_map.132.half_ref = bf16[8,528,128]{2,1,0:T(8,128)(2,1)S(1)} custom-call(f32[2,1024,128]{2,1,0:T(8,128)S(1)} %shard_map.131.spec, f32[4,256,128]{2,1,0:T(8,128)S(1)} %copy-done.4, bf16[4,2,256,512]{3,2,1,0:T(8,128)(2,1)S(1)} %copy-done, f32[2,1024,128]{2,1,0:T(8,128)S(1)} %copy-done.3, bf16[16,2,2,4,16,128]{5,4,3,2,1,0:T(8,128)(2,1)S(1)} %shard_map.130.after_ref.bank), custom_call_target="tpu_custom_call" | custom-call | flops 2000000000 | bytes 10485760 | tf_op jit(solution)/shard_map/pallas_call | solution.py:318
  61.0 1.5 %collective-permute-done.8.spec = f32[2,1024,128]{2,1,0:T(8,128)S(1)} collective-permute-done((f32[2,1024,128]{2,1,0:T(8,128)S(1)}, f32[2,1024,128]{2,1,0:T(8,128)S(1)}, u32[]{:S(2)}, u32[]{:S(2)}) %collective-permute-start.8) | collective-permute-done | bytes 1048608 | tf_op jit(solution)/shard_map/ppermute | solution.py:376
  62.5 1.2 %shard_map.133 = bf16[8,1040,128]{2,1,0:T(8,128)(2,1)S(1)} custom-call(f32[2,1024,128]{2,1,0:T(8,128)S(1)} %collective-permute-done.8.spec, f32[4,256,128]{2,1,0:T(8,128)S(1)} %copy-done.4, bf16[4,2,256,512]{3,2,1,0:T(8,128)(2,1)S(1)} %copy-done, f32[2,1024,128]{2,1,0:T(8,128)S(1)} %copy-done.3, ...), custom_call_target="tpu_custom_call" | custom-call | flops 2000000000 | bytes 10485760 | tf_op jit(solution)/shard_map/pallas_call | solution.py:318
  63.6 0.0 copy-start.8
  63.7 32.1 %all_to_all.15.in_ref = bf16[8,1040,128]{2,1,0:T(8,128)(2,1)S(1)} all-to-all(bf16[8,1040,128]{2,1,0:T(8,128)(2,1)S(1)} %shard_map.133), channel_id=1, replica_groups=mesh['tmpl'=16,'seg'=8] {'seg'}, dimensions={0} | all-to-all | bytes 4259840 | tf_op jit(solution)/shard_map/all_to_all | solution.py:387
  95.8 3.9 %shard_map.134 = f32[2,2,1024,128]{3,2,1,0:T(8,128)} custom-call(bf16[8,1040,128]{2,1,0:T(8,128)(2,1)S(1)} %all_to_all.15.in_ref, bf16[4,2,256,256]{3,2,1,0:T(8,128)(2,1)S(1)} %copy-done.8), custom_call_target="tpu_custom_call" | custom-call | flops 3000000000 | bytes 6291456 | tf_op jit(solution)/shard_map/pallas_call | solution.py:318
  (17 shorter events, 0.0 us)
Async XLA Ops:
  0.0 34.4 %copy-start.7 = (f32[2,48,1024]{2,1,0:T(8,128)S(1)}, f32[2,48,1024]{2,1,0:T(8,128)}, u32[]{:S(2)}) copy-start(f32[2,48,1024]{2,1,0:T(8,128)} %constant.15.clone.turn_ref) | copy-start | bytes 1179652
  4.2 15.7 %collective-permute-start = (bf16[2,2,2,4,16,128]{5,4,3,2,1,0:T(8,128)(2,1)}, bf16[2,2,2,4,16,128]{5,4,3,2,1,0:T(8,128)(2,1)S(1)}, u32[]{:S(2)}, u32[]{:S(2)}) collective-permute-start(bf16[2,2,2,4,16,128]{5,4,3,2,1,0:T(8,128)(2,1)} %get-tuple-element.20), channel_id=1, source_target_pairs={{0,32},{8,40},{16,48},{24,56},{32,64},{40,72},{48,80},{56,88},{64,... | collective-permute-start | bytes 393224 | tf_op jit(solution)/shard_map/ppermute | solution.py:357
  5.9 15.4 %collective-permute-start.1 = (bf16[2,2,2,4,16,128]{5,4,3,2,1,0:T(8,128)(2,1)}, bf16[2,2,2,4,16,128]{5,4,3,2,1,0:T(8,128)(2,1)S(1)}, u32[]{:S(2)}, u32[]{:S(2)}) collective-permute-start(bf16[2,2,2,4,16,128]{5,4,3,2,1,0:T(8,128)(2,1)} %get-tuple-element.21), channel_id=1, source_target_pairs={{0,64},{8,72},{16,80},{24,88},{32,96},{40,104},{48,112},{56,120},{... | collective-permute-start | bytes 393224 | tf_op jit(solution)/shard_map/ppermute | solution.py:357
  8.6 25.8 %all-to-all-start = ((bf16[8,128,128]{2,1,0:T(8,128)(2,1)}), bf16[8,128,128]{2,1,0:T(8,128)(2,1)S(1)}, u32[]{:S(2)}, u32[]{:S(2)}) async-start(bf16[8,128,128]{2,1,0:T(8,128)(2,1)} %get-tuple-element.18), calls=%async_computation | async-start | bytes 524288 | tf_op jit(solution)/shard_map/all_to_all | solution.py:352
  16.4 6.9 %collective-permute-start.2 = (bf16[2,2,2,4,16,128]{5,4,3,2,1,0:T(8,128)(2,1)}, bf16[2,2,2,4,16,128]{5,4,3,2,1,0:T(8,128)(2,1)S(1)}, u32[]{:S(2)}, u32[]{:S(2)}) collective-permute-start(bf16[2,2,2,4,16,128]{5,4,3,2,1,0:T(8,128)(2,1)} %get-tuple-element.22), channel_id=1, source_target_pairs={{0,96},{8,104},{16,112},{24,120},{32,0},{40,8},{48,16},{56,24},{64... | collective-permute-start | bytes 393224 | tf_op jit(solution)/shard_map/ppermute | solution.py:357
  17.8 14.9 %collective-permute-start.3 = (bf16[2,2,2,4,16,128]{5,4,3,2,1,0:T(8,128)(2,1)}, bf16[2,2,2,4,16,128]{5,4,3,2,1,0:T(8,128)(2,1)S(1)}, u32[]{:S(2)}, u32[]{:S(2)}) collective-permute-start(bf16[2,2,2,4,16,128]{5,4,3,2,1,0:T(8,128)(2,1)} %get-tuple-element.23), channel_id=1, source_target_pairs={{0,16},{8,24},{16,0},{24,8},{32,48},{40,56},{48,32},{56,40},{64,80... | collective-permute-start | bytes 393224 | tf_op jit(solution)/shard_map/ppermute | solution.py:357
  18.8 13.8 %collective-permute-start.4 = (bf16[2,2,2,4,16,128]{5,4,3,2,1,0:T(8,128)(2,1)}, bf16[2,2,2,4,16,128]{5,4,3,2,1,0:T(8,128)(2,1)S(1)}, u32[]{:S(2)}, u32[]{:S(2)}) collective-permute-start(bf16[2,2,2,4,16,128]{5,4,3,2,1,0:T(8,128)(2,1)} %get-tuple-element.24), channel_id=1, source_target_pairs={{0,48},{8,56},{16,32},{24,40},{32,80},{40,88},{48,64},{56,72},{64,... | collective-permute-start | bytes 393224 | tf_op jit(solution)/shard_map/ppermute | solution.py:357
  19.9 12.8 %collective-permute-start.5 = (bf16[2,2,2,4,16,128]{5,4,3,2,1,0:T(8,128)(2,1)}, bf16[2,2,2,4,16,128]{5,4,3,2,1,0:T(8,128)(2,1)S(1)}, u32[]{:S(2)}, u32[]{:S(2)}) collective-permute-start(bf16[2,2,2,4,16,128]{5,4,3,2,1,0:T(8,128)(2,1)} %get-tuple-element.25), channel_id=1, source_target_pairs={{0,80},{8,88},{16,64},{24,72},{32,112},{40,120},{48,96},{56,104},{... | collective-permute-start | bytes 393224 | tf_op jit(solution)/shard_map/ppermute | solution.py:357
  21.3 11.4 %collective-permute-start.6 = (bf16[2,2,2,4,16,128]{5,4,3,2,1,0:T(8,128)(2,1)}, bf16[2,2,2,4,16,128]{5,4,3,2,1,0:T(8,128)(2,1)S(1)}, u32[]{:S(2)}, u32[]{:S(2)}) collective-permute-start(bf16[2,2,2,4,16,128]{5,4,3,2,1,0:T(8,128)(2,1)} %get-tuple-element.26), channel_id=1, source_target_pairs={{0,112},{8,120},{16,96},{24,104},{32,16},{40,24},{48,0},{56,8},{64... | collective-permute-start | bytes 393224 | tf_op jit(solution)/shard_map/ppermute | solution.py:357
  32.7 0.9 copy-start.5
  34.3 9.6 %collective-permute-start.7 = (bf16[8,2,2,4,16,128]{5,4,3,2,1,0:T(8,128)(2,1)S(1)}, bf16[8,2,2,4,16,128]{5,4,3,2,1,0:T(8,128)(2,1)S(1)}, u32[]{:S(2)}, u32[]{:S(2)}) collective-permute-start(bf16[8,2,2,4,16,128]{5,4,3,2,1,0:T(8,128)(2,1)S(1)} %get-tuple-element.28), channel_id=1, source_target_pairs={{0,8},{8,0},{16,24},{24,16},{32,40},{40,32},{48,56},{56,48},{64,72... | collective-permute-start | bytes 1572872 | tf_op jit(solution)/shard_map/ppermute | solution.py:362
  34.4 1.6 %copy-start.1 = (bf16[4,2,2,256,256]{4,3,2,1,0:T(8,128)(2,1)S(1)}, bf16[4,2,2,256,256]{4,3,2,1,0:T(8,128)(2,1)}, u32[]{:S(2)}) copy-start(bf16[4,2,2,256,256]{4,3,2,1,0:T(8,128)(2,1)} %constant.14.clone.table_ref) | copy-start | bytes 6291460
  36.0 7.9 %copy-start.6 = (bf16[2,2,2,4,16,128]{5,4,3,2,1,0:T(8,128)(2,1)S(1)}, bf16[2,2,2,4,16,128]{5,4,3,2,1,0:T(8,128)(2,1)}, u32[]{:S(2)}) copy-start(bf16[2,2,2,4,16,128]{5,4,3,2,1,0:T(8,128)(2,1)} %get-tuple-element.19.refs_0_) | copy-start | bytes 393220
  37.5 18.7 %all-to-all-start.1 = ((bf16[8,2,4,32,128]{4,3,2,1,0:T(8,128)(2,1)}), bf16[8,2,4,32,128]{4,3,2,1,0:T(8,128)(2,1)}, u32[]{:S(2)}, u32[]{:S(2)}) async-start(bf16[8,2,4,32,128]{4,3,2,1,0:T(8,128)(2,1)} %shard_map.129), calls=%async_computation.1 | async-start | bytes 1048576 | tf_op jit(solution)/shard_map/all_to_all | solution.py:371
  45.6 14.3 %copy-start = (bf16[4,2,256,512]{3,2,1,0:T(8,128)(2,1)S(1)}, bf16[4,2,256,512]{3,2,1,0:T(8,128)(2,1)}, u32[]{:S(2)}) copy-start(bf16[4,2,256,512]{3,2,1,0:T(8,128)(2,1)} %constant.17.clone.third_ref) | copy-start | bytes 6291460
  56.2 1.6 %copy-start.2 = (bf16[4,256,1024]{2,1,0:T(8,128)(2,1)S(1)}, bf16[4,256,1024]{2,1,0:T(8,128)(2,1)}, u32[]{:S(2)}) copy-start(bf16[4,256,1024]{2,1,0:T(8,128)(2,1)} %constant.16.clone.table_ref) | copy-start | bytes 6291460
  57.8 2.0 %copy-start.3 = (f32[2,1024,128]{2,1,0:T(8,128)S(1)}, f32[2,1024,128]{2,1,0:T(8,128)}, u32[]{:S(2)}) copy-start(f32[2,1024,128]{2,1,0:T(8,128)} %get-tuple-element.30.twist) | copy-start | bytes 3145732
  57.8 2.0 %copy-start.4 = (f32[4,256,128]{2,1,0:T(8,128)S(1)}, f32[4,256,128]{2,1,0:T(8,128)}, u32[]{:S(2)}) copy-start(f32[4,256,128]{2,1,0:T(8,128)} %get-tuple-element.29.weight_ref) | copy-start | bytes 1572868
  59.7 2.7 %collective-permute-start.8 = (f32[2,1024,128]{2,1,0:T(8,128)S(1)}, f32[2,1024,128]{2,1,0:T(8,128)S(1)}, u32[]{:S(2)}, u32[]{:S(2)}) collective-permute-start(f32[2,1024,128]{2,1,0:T(8,128)S(1)} %shard_map.131.spec), channel_id=1, source_target_pairs={{0,8},{8,0},{16,24},{24,16},{32,40},{40,32},{48,56},{56,48},{64,72... | collective-permute-start | bytes 3145736 | tf_op jit(solution)/shard_map/ppermute | solution.py:376
  63.6 32.1 %copy-start.8 = (bf16[4,2,256,256]{3,2,1,0:T(8,128)(2,1)S(1)}, bf16[4,2,256,256]{3,2,1,0:T(8,128)(2,1)}, u32[]{:S(2)}) copy-start(bf16[4,2,256,256]{3,2,1,0:T(8,128)(2,1)} %constant.20.clone.table_ref) | copy-start | bytes 3145732

commit v3 on v2

--- a/solution.py
+++ b/solution.py
@@ -16,7 +16,7 @@
 SMEM = pl.BlockSpec(memory_space=pltpu.SMEM)
 ANY = pl.BlockSpec(memory_space=pl.ANY)
 MIB = 1 << 20
-OFFSETS = [(rz, rx) for rz in range(2) for rx in range(4)]
+OFFSETS = [(0, 0), (1, 0), (1, 2), (1, 1), (1, 3), (0, 2), (0, 1), (0, 3)]
 
 
 def phases(product, count):
@@ -86,11 +86,10 @@
 
 
 def gate_kernel(
-    strain_ref, start_any, span_any, assign_any, bank_any, asd_any, back_any, shift_any,
-    out_ref, weight_ref, twist_ref, *rest
+    strain_ref, start_any, span_any, assign_any, bank_any, out_ref, *rest
 ):
     pick_refs, rest = rest[:8], rest[8:]
-    strain, bank_ref, start_ref, span_ref, assign_ref, asd_ref, back_ref, shift_ref, sems = rest
+    strain, bank_ref, start_ref, span_ref, assign_ref, sems = rest
     x, z, core = place()
     copies = [
         pltpu.make_async_copy(start_any, start_ref, sems.at[0]),
@@ -98,9 +97,6 @@
         pltpu.make_async_copy(strain_ref.at[core], strain, sems.at[2]),
         pltpu.make_async_copy(assign_any, assign_ref, sems.at[3]),
         pltpu.make_async_copy(bank_any, bank_ref, sems.at[4]),
-        pltpu.make_async_copy(asd_any, asd_ref, sems.at[5]),
-        pltpu.make_async_copy(back_any, back_ref, sems.at[6]),
-        pltpu.make_async_copy(shift_any, shift_ref, sems.at[7]),
     ]
     for copy in copies:
         copy.start()
@@ -128,7 +124,7 @@
     for copy in copies[3:5]:
         copy.wait()
     for i in range(16):
-        rz, rx, rc = i // 8, i // 2 % 4, i % 2
+        (rz, rx), rc = OFFSETS[i // 2], i % 2
         dest = ((x + rx) % 4) * 4 + (z + rz) % 2 * 2 + (core + rc) % 2
         for slot in range(2):
             chosen = assign_ref[2 * dest + slot]
@@ -136,19 +132,6 @@
                 for p in range(4):
                     value = bank_ref[part, chosen, pl.ds(p, 16, stride=4), :].astype(BF)
                     pick_refs[i // 2][rc, slot, part, p] = value
-
-    for copy in copies[5:]:
-        copy.wait()
-    for p in range(4):
-        asd = asd_ref[pl.ds(p, 256, stride=4), :]
-        weight_ref[p] = 1.0 / (asd * asd)
-    own = lane == lax.axis_index("seg")
-    for i in range(8):
-        rows = slice(128 * i, 128 * i + 128)
-        shift = [jnp.sum(jnp.where(own, shift_ref[part, rows, :], 0.0), axis=1, keepdims=True) for part in range(2)]
-        re, im = back_ref[0, rows, :], back_ref[1, rows, :]
-        twist_ref[0, rows, :] = re * shift[0] - im * shift[1]
-        twist_ref[1, rows, :] = re * shift[1] + im * shift[0]
 
 
 def pack_kernel(*refs):
@@ -174,12 +157,18 @@
     return ((sr + ur, si + ui), (tr + wr, ti + wi), (sr - ur, si - ui), (tr - wr, ti - wi))
 
 
-def first_kernel(cols_ref, table_ref, turn_ref, after_ref, out_ref, z_ref):
+def first_kernel(cols_ref, table_any, turn_any, after_ref, out_ref, table_ref, turn_ref, z_ref, sems):
     del after_ref
+    copies = [pltpu.make_async_copy(table_any.at[r], table_ref.at[r], sems.at[r]) for r in range(4)]
+    copies += [pltpu.make_async_copy(turn_any, turn_ref, sems.at[4])]
+    for copy in copies:
+        copy.start()
     for r in range(4):
+        copies[r].wait()
         turned = cols_ref[:, 32 * r : 32 * r + 32, :].reshape(256, 128).T
         for part in range(2):
             z_ref[r, part] = dot(turned, table_ref[r, part, 0]) + dot(turned, table_ref[r, part, 1])
+    copies[4].wait()
     seg = 32 + lax.axis_index("seg")
     seg_re, seg_im = turn_ref[0, pl.ds(seg, 1), :], turn_ref[1, pl.ds(seg, 1), :]
     for r1 in range(4):
@@ -217,17 +206,42 @@
 
 
 def assemble_kernel(*refs):
-    piece_refs, cross_ref, bank, sems = refs[:8], refs[8], refs[9], refs[10]
+    piece_refs, cross_ref, asd_any, back_any, shift_any = refs[:8], *refs[8:12]
+    bank, weight_any, twist_any, token_ref, weight_ref, twist_ref, asd_ref, back_ref, shift_ref, sems = refs[12:]
+    token_ref[...] = jnp.zeros_like(token_ref)
     x, z, core = place()
-    copies = []
-    for i in range(8):
+    copies = [
+        pltpu.make_async_copy(asd_any, asd_ref, sems.at[16]),
+        pltpu.make_async_copy(back_any, back_ref, sems.at[17]),
+        pltpu.make_async_copy(shift_any, shift_ref, sems.at[18]),
+    ]
+    for i, (rz, rx) in enumerate(OFFSETS):
         for rc in range(2):
             src = piece_refs[i].at[0] if rc == 0 else cross_ref.at[i]
-            origin = ((x + 4 - i % 4) % 4) * 4 + (z + i // 4) % 2 * 2 + (core + rc) % 2
-            copies.append(pltpu.make_async_copy(src, bank.at[origin], sems.at[len(copies)]))
+            origin = ((x + 4 - rx) % 4) * 4 + (z + rz) % 2 * 2 + (core + rc) % 2
+            copies.append(pltpu.make_async_copy(src, bank.at[origin], sems.at[2 * i + rc]))
     for copy in copies:
         copy.start()
-    for copy in copies:
+    copies[0].wait()
+    for p in range(4):
+        asd = asd_ref[pl.ds(p, 256, stride=4), :]
+        weight_ref[p] = 1.0 / (asd * asd)
+    copies[1].wait()
+    copies[2].wait()
+    own = lax.broadcasted_iota(jnp.int32, (128, 128), 1) == lax.axis_index("seg")
+    for i in range(8):
+        rows = slice(128 * i, 128 * i + 128)
+        shift = [jnp.sum(jnp.where(own, shift_ref[part, rows, :], 0.0), axis=1, keepdims=True) for part in range(2)]
+        re, im = back_ref[0, rows, :], back_ref[1, rows, :]
+        twist_ref[0, rows, :] = re * shift[0] - im * shift[1]
+        twist_ref[1, rows, :] = re * shift[1] + im * shift[0]
+    outs = [
+        pltpu.make_async_copy(weight_ref, weight_any, sems.at[19]),
+        pltpu.make_async_copy(twist_ref, twist_any, sems.at[20]),
+    ]
+    for copy in outs:
+        copy.start()
+    for copy in copies[3:] + outs:
         copy.wait()
 
 
@@ -335,17 +349,12 @@
     swap_core = [(i, i ^ 1) for i in range(16)]
 
     blk = (2, 2, 4, 16, 128)
-    gated, weight, twist, *picked = call(
-        gate_kernel, (strain, gate_start, gate_span, assign, bank, asd, const["back"], const["shift"]),
-        (
-            shape(8, 128, 128), shape(4, 256, 128, dtype=F32), shape(2, 1024, 128, dtype=F32),
-            *[shape(2, *blk)] * 8,
-        ),
-        [ANY] * 8, 10**8, 4 * MIB,
+    gated, *picked = call(
+        gate_kernel, (strain, gate_start, gate_span, assign, bank), (shape(8, 128, 128), *[shape(2, *blk)] * 8),
+        [ANY] * 5, 10**8, 4 * MIB,
         [
             pltpu.VMEM((128, 1024), F32), pltpu.VMEM((2, 32, 64, 128), F32), pltpu.SMEM((2, 1, 2), jnp.int32),
-            pltpu.SMEM((2, 1, 2), jnp.int32), pltpu.SMEM((32,), jnp.int32), pltpu.VMEM((1024, 128), F32),
-            pltpu.VMEM((2, 1024, 128), F32), pltpu.VMEM((2, 1024, 128), F32), pltpu.SemaphoreType.DMA((8,)),
+            pltpu.SMEM((2, 1, 2), jnp.int32), pltpu.SMEM((32,), jnp.int32), pltpu.SemaphoreType.DMA((5,)),
         ],
         limit=63,
     )
@@ -355,22 +364,35 @@
     for (rz, rx), send in zip(OFFSETS[1:], picked[1:]):
         hop = [(i, (i // 4 + rx) % 4 * 4 + i % 4 ^ 2 * rz) for i in range(16)]
         pieces.append(lax.ppermute(send, "tmpl", hop))
-    cross, token = call(
+    cross, packed = call(
         pack_kernel, pieces, (shape(8, *blk), shape(8, 128, dtype=F32)), [ANY] * 8, 1, 10 * MIB,
-        [pltpu.SemaphoreType.DMA((8,))], limit=8, space=(ANY, VMEM),
+        [pltpu.SemaphoreType.DMA((8,))], limit=63, space=(ANY, VMEM),
     )
     crossed = lax.ppermute(cross, "tmpl", swap_core)
-    ordered = call(
-        assemble_kernel, (*pieces, crossed), shape(16, *blk), [ANY] * 9, 1, 10 * MIB, [pltpu.SemaphoreType.DMA((16,))],
-        limit=8,
+    ordered, weight, twist, token = call(
+        assemble_kernel, (*pieces, crossed, asd, const["back"], const["shift"]),
+        (
+            shape(16, *blk), shape(4, 256, 128, dtype=F32), shape(2, 1024, 128, dtype=F32), shape(8, 128, dtype=F32),
+        ),
+        [ANY] * 12, 1, 10 * MIB,
+        [
+            pltpu.VMEM((4, 256, 128), F32), pltpu.VMEM((2, 1024, 128), F32), pltpu.VMEM((1024, 128), F32),
+            pltpu.VMEM((2, 1024, 128), F32), pltpu.VMEM((2, 1024, 128), F32), pltpu.SemaphoreType.DMA((21,)),
+        ],
+        limit=63, space=(ANY, ANY, ANY, VMEM),
     )
     turned = call(
-        first_kernel, (columns, const["first"], const["turn"], token),
-        shape(8, 2, 4, 32, 128), [VMEM] * 3 + [ANY], 3 * 10**8, 4 * MIB, [pltpu.VMEM((4, 2, 128, 256), F32)],
+        first_kernel, (columns, const["first"], const["turn"], packed), shape(8, 2, 4, 32, 128), [VMEM] + [ANY] * 3,
+        3 * 10**8, 4 * MIB,
+        [
+            pltpu.VMEM((4, 2, 2, 256, 256), BF), pltpu.VMEM((2, 48, 1024), F32),
+            pltpu.VMEM((4, 2, 128, 256), F32), pltpu.SemaphoreType.DMA((5,)),
+        ],
+        limit=63,
     )
     own = lax.all_to_all(turned, "seg", 0, 0)
     spec = call(
-        second_kernel, (own, const["second"], ordered), shape(2, 1024, 128, dtype=F32),
+        second_kernel, (own, const["second"], token), shape(2, 1024, 128, dtype=F32),
         [VMEM] * 2 + [ANY], 1, 1, [pltpu.VMEM((4, 256, 256), F32)],
     )
     other_spec = lax.ppermute(spec, "tmpl", swap_core)

time: 101 us -> 141 us (1.40)
  Pallas kernels: 16.2 us -> 65.4 us
  waiting for transfers between devices: 21.5 us -> 5.82 us
  blocking collectives: 32.1 us -> 36.5 us
  starting transfers between devices: 25.6 us -> 27.4 us
    pallas_call x8, Pallas kernels: 16.2 us -> 65.4 us  [call(): pl.pallas_call(kernel, out_shape=outs, in_specs=specs, out_specs=space if...]
    all_to_all x1, waiting for transfers between devices: 10.7 us -> 0.01 us  [per_device(): own = lax.all_to_all(turned, 'seg', 0, 0)]
    all_to_all x1, blocking collectives: 32.1 us -> 36.5 us  [per_device(): series = lax.all_to_all(inner, 'seg', 0, 0)]
    ppermute x7, waiting for transfers between devices: 9.36 us -> 5.81 us  [per_device(): pieces.append(lax.ppermute(send, 'tmpl', hop))]
    ppermute x1, waiting for transfers between devices: 1.46 us -> 0.01 us  [per_device(): other_spec = lax.ppermute(spec, 'tmpl', swap_core)]
    unnamed x18 -> x26, local copies, waits for them, and re-layouts: 4.1 us -> 4.69 us
  transfers between devices with their start and end apart: 11 -> 11, of which waited for: 3 -> 5; matrix products, arithmetic and copies ran while one was open for 0% -> 0% of each run, Pallas kernels for 5% -> 40%
where the time goes in v3:
time: 141 us; the launch traced here: 140 us
  Pallas kernels  65.4 us (46%)
  blocking collectives  36.5 us (26%)
  starting transfers between devices  27.4 us (19%)
  waiting for transfers between devices  5.82 us (4%)
  local copies, waits for them, and re-layouts  4.69 us (3%)
    pallas_call x8, Pallas kernels, call(): pl.pallas_call(kernel, out_shape=outs, in_specs=specs, out_specs=space if...  65.4 us
    all_to_all x1, blocking collectives, per_device(): series = lax.all_to_all(inner, 'seg', 0, 0)  36.5 us
    ppermute x7, starting transfers between devices, per_device(): pieces.append(lax.ppermute(send, 'tmpl', hop))  12.1 us
    all_to_all x1, starting transfers between devices, per_device(): columns = lax.all_to_all(gated, 'seg', 0, 0)  7.78 us
    all_to_all x1, starting transfers between devices, per_device(): own = lax.all_to_all(turned, 'seg', 0, 0)  7.13 us
    ppermute x7, waiting for transfers between devices, per_device(): pieces.append(lax.ppermute(send, 'tmpl', hop))  5.81 us
    unnamed x26, local copies, waits for them, and re-layouts  4.69 us
  transfers between devices with their start and end apart: 11, of which 5 were waited for; matrix products, arithmetic and copies ran while one was open for 0% of the time, Pallas kernels for 40%

profile of v3, /device:TPU:0, one launch (start us, length us, event | category | flops | bytes accessed | tf_op | source)
XLA Modules:
  0.0 140.0 jit_solution(13157536185518150668)
XLA Ops:
  0.0 3.0 %shard_map.127 = (bf16[8,128,128]{2,1,0:T(8,128)(2,1)}, bf16[2,2,2,4,16,128]{5,4,3,2,1,0:T(8,128)(2,1)}, bf16[2,2,2,4,16,128]{5,4,3,2,1,0:T(8,128)(2,1)}, bf16[2...) custom-call(f32[2,128,1024]{2,1,0:T(8,128)} %strain_ref.1, ...), custom_call_target="tpu_custom_call" | custom-call | flops 100000000 | bytes 4194304 | tf_op jit(solution)/shard_map/pallas_call | solution.py:332
  3.0 2.1 %collective-permute-start = (bf16[2,2,2,4,16,128]{5,4,3,2,1,0:T(8,128)(2,1)}, bf16[2,2,2,4,16,128]{5,4,3,2,1,0:T(8,128)(2,1)S(1)}, u32[]{:S(2)}, u32[]{:S(2)}) collective-permute-start(bf16[2,2,2,4,16,128]{5,4,3,2,1,0:T(8,128)(2,1)} %get-tuple-element.22), channel_id=1, source_target_pairs={{0,16},{8,24},{16,0},{24,8},{32,48},{40,56},{48,32},{56,40},{64,80... | collective-permute-start | bytes 393224 | tf_op jit(solution)/shard_map/ppermute | solution.py:366
  5.1 2.6 %collective-permute-start.1 = (bf16[2,2,2,4,16,128]{5,4,3,2,1,0:T(8,128)(2,1)}, bf16[2,2,2,4,16,128]{5,4,3,2,1,0:T(8,128)(2,1)S(1)}, u32[]{:S(2)}, u32[]{:S(2)}) collective-permute-start(bf16[2,2,2,4,16,128]{5,4,3,2,1,0:T(8,128)(2,1)} %get-tuple-element.23), channel_id=1, source_target_pairs={{0,80},{8,88},{16,64},{24,72},{32,112},{40,120},{48,96},{56,104},{... | collective-permute-start | bytes 393224 | tf_op jit(solution)/shard_map/ppermute | solution.py:366
  7.7 7.8 %all-to-all-start = ((bf16[8,128,128]{2,1,0:T(8,128)(2,1)}), bf16[8,128,128]{2,1,0:T(8,128)(2,1)S(1)}, u32[]{:S(2)}, u32[]{:S(2)}) async-start(bf16[8,128,128]{2,1,0:T(8,128)(2,1)} %get-tuple-element.20), calls=%async_computation | async-start | bytes 524288 | tf_op jit(solution)/shard_map/all_to_all | solution.py:361
  15.4 1.0 collective-permute-start.2
  16.5 3.1 %collective-permute-start.3 = (bf16[2,2,2,4,16,128]{5,4,3,2,1,0:T(8,128)(2,1)}, bf16[2,2,2,4,16,128]{5,4,3,2,1,0:T(8,128)(2,1)S(1)}, u32[]{:S(2)}, u32[]{:S(2)}) collective-permute-start(bf16[2,2,2,4,16,128]{5,4,3,2,1,0:T(8,128)(2,1)} %get-tuple-element.25), channel_id=1, source_target_pairs={{0,112},{8,120},{16,96},{24,104},{32,16},{40,24},{48,0},{56,8},{64... | collective-permute-start | bytes 393224 | tf_op jit(solution)/shard_map/ppermute | solution.py:366
  19.6 0.8 collective-permute-start.5
  20.4 2.5 %collective-permute-start.6 = (bf16[2,2,2,4,16,128]{5,4,3,2,1,0:T(8,128)(2,1)}, bf16[2,2,2,4,16,128]{5,4,3,2,1,0:T(8,128)(2,1)}, u32[]{:S(2)}, u32[]{:S(2)}) collective-permute-start(bf16[2,2,2,4,16,128]{5,4,3,2,1,0:T(8,128)(2,1)} %get-tuple-element.28), channel_id=1, source_target_pairs={{0,96},{8,104},{16,112},{24,120},{32,0},{40,8},{48,16},{56,24},{64... | collective-permute-start | bytes 393224 | tf_op jit(solution)/shard_map/ppermute | solution.py:366
  22.9 3.2 %collective-permute-done.2.refs_3_ = bf16[2,2,2,4,16,128]{5,4,3,2,1,0:T(8,128)(2,1)S(1)} collective-permute-done((bf16[2,2,2,4,16,128]{5,4,3,2,1,0:T(8,128)(2,1)}, bf16[2,2,2,4,16,128]{5,4,3,2,1,0:T(8,128)(2,1)S(1)}, u32[]{:S(2)}, u32[]{:S(2)}) %collective-permute-start.2) | collective-permute-done | bytes 131104 | tf_op jit(solution)/shard_map/ppermute | solution.py:366
  26.1 0.2 collective-permute-done.3.refs_4_
  26.3 0.4 collective-permute-done.4.refs_5_
  26.7 1.4 %collective-permute-done.5.refs_6_ = bf16[2,2,2,4,16,128]{5,4,3,2,1,0:T(8,128)(2,1)} collective-permute-done((bf16[2,2,2,4,16,128]{5,4,3,2,1,0:T(8,128)(2,1)}, bf16[2,2,2,4,16,128]{5,4,3,2,1,0:T(8,128)(2,1)}, u32[]{:S(2)}, u32[]{:S(2)}) %collective-permute-start.5) | collective-permute-done | bytes 131104 | tf_op jit(solution)/shard_map/ppermute | solution.py:366
  28.2 0.5 collective-permute-done.6.refs_7_
  28.7 17.6 %shard_map.128 = (bf16[8,2,2,4,16,128]{5,4,3,2,1,0:T(8,128)(2,1)}, f32[8,128]{1,0:T(8,128)}) custom-call(bf16[2,2,2,4,16,128]{5,4,3,2,1,0:T(8,128)(2,1)} %get-tuple-element.21.refs_0_, bf16[2,2,2,4,16,128]{5,4,3,2,1,0:T(8,128)(2,1)} %copy-done.8, bf16[2,2,2,4,16,128]{5,4,3,2,1,0:T(8,128)(2,1)} %copy-done.9, bf16[2,2,2,4,16,128]{5,4,3,2,1,0:T(8,128)(2,1)} %copy-done.10, ...), custom_call_target="tpu_custom_call" | custom-call | flops 1 | bytes 10485760 | tf_op jit(solution)/shard_map/pallas_call | solution.py:332
  46.4 0.1 collective-permute-start.7
  46.5 0.7 copy-done.7
  47.2 4.2 %shard_map.129 = bf16[8,2,4,32,128]{4,3,2,1,0:T(8,128)(2,1)} custom-call(bf16[8,128,128]{2,1,0:T(8,128)(2,1)} %copy-done.7, bf16[4,2,2,256,256]{4,3,2,1,0:T(8,128)(2,1)} %constant.14.clone.table_any, f32[2,48,1024]{2,1,0:T(8,128)} %constant.15.clone.turn_any, f32[8,128]{1,0:T(8,128)} %get-tuple-element.29.after_ref), custom_call_target="tpu_custom_call" | custom-call | flops 300000000 | bytes 4194304 | tf_op jit(solution)/shard_map/pallas_call | solution.py:332
  51.4 7.1 %all-to-all-start.1 = ((bf16[8,2,4,32,128]{4,3,2,1,0:T(8,128)(2,1)}), bf16[8,2,4,32,128]{4,3,2,1,0:T(8,128)(2,1)S(1)}, u32[]{:S(2)}, u32[]{:S(2)}) async-start(bf16[8,2,4,32,128]{4,3,2,1,0:T(8,128)(2,1)} %shard_map.129), calls=%async_computation.1 | async-start | bytes 1048576 | tf_op jit(solution)/shard_map/all_to_all | solution.py:393
  58.5 33.7 %shard_map.130 = (bf16[16,2,2,4,16,128]{5,4,3,2,1,0:T(8,128)(2,1)}, f32[4,256,128]{2,1,0:T(8,128)}, f32[2,1024,128]{2,1,0:T(8,128)}, f32[8,128]{1,0:T(8,128)}) custom-call(bf16[2,2,2,4,16,128]{5,4,3,2,1,0:T(8,128)(2,1)} %get-tuple-element.21.refs_0_, bf16[2,2,2,4,16,128]{5,4,3,2,1,0:T(8,128)(2,1)} %copy-done.8, bf16[2,2,2,4,16,128]{5,4,3,2,1,0:T(8,128)(2,1)} %copy-done.9, ...), custom_call_target="tpu_custom_call" | custom-call | flops 1 | bytes 10485760 | tf_op jit(solution)/shard_map/pallas_call | solution.py:332
  92.2 0.0 copy-start
  92.2 0.0 copy-start.1
  92.3 1.7 %copy-done.1 = bf16[4,256,1024]{2,1,0:T(8,128)(2,1)S(1)} copy-done((bf16[4,256,1024]{2,1,0:T(8,128)(2,1)S(1)}, bf16[4,256,1024]{2,1,0:T(8,128)(2,1)}, u32[]{:S(2)}) %copy-start.1) | copy-done | bytes 2097176
  94.0 0.7 copy-done.5
  94.7 0.7 shard_map.131.spec
  95.4 0.3 collective-permute-start.8
  95.7 0.2 copy-done.2
  95.9 0.1 copy-done.4
  96.0 1.2 copy-done.3
  97.2 1.1 shard_map.132.half_ref
  98.4 1.2 shard_map.133
  99.6 36.5 %all_to_all.15.in_ref = bf16[8,1040,128]{2,1,0:T(8,128)(2,1)S(1)} all-to-all(bf16[8,1040,128]{2,1,0:T(8,128)(2,1)S(1)} %shard_map.133), channel_id=1, replica_groups=mesh['tmpl'=16,'seg'=8] {'seg'}, dimensions={0} | all-to-all | bytes 4259840 | tf_op jit(solution)/shard_map/all_to_all | solution.py:409
  136.1 3.9 %shard_map.134 = f32[2,2,1024,128]{3,2,1,0:T(8,128)} custom-call(bf16[8,1040,128]{2,1,0:T(8,128)(2,1)S(1)} %all_to_all.15.in_ref, bf16[4,2,256,256]{3,2,1,0:T(8,128)(2,1)S(1)} %copy-done.6), custom_call_target="tpu_custom_call" | custom-call | flops 3000000000 | bytes 6291456 | tf_op jit(solution)/shard_map/pallas_call | solution.py:332
  (25 shorter events, 0.1 us)
Async XLA Ops:
  3.0 16.6 %collective-permute-start = (bf16[2,2,2,4,16,128]{5,4,3,2,1,0:T(8,128)(2,1)}, bf16[2,2,2,4,16,128]{5,4,3,2,1,0:T(8,128)(2,1)S(1)}, u32[]{:S(2)}, u32[]{:S(2)}) collective-permute-start(bf16[2,2,2,4,16,128]{5,4,3,2,1,0:T(8,128)(2,1)} %get-tuple-element.22), channel_id=1, source_target_pairs={{0,16},{8,24},{16,0},{24,8},{32,48},{40,56},{48,32},{56,40},{64,80... | collective-permute-start | bytes 393224 | tf_op jit(solution)/shard_map/ppermute | solution.py:366
  5.1 15.3 %collective-permute-start.1 = (bf16[2,2,2,4,16,128]{5,4,3,2,1,0:T(8,128)(2,1)}, bf16[2,2,2,4,16,128]{5,4,3,2,1,0:T(8,128)(2,1)S(1)}, u32[]{:S(2)}, u32[]{:S(2)}) collective-permute-start(bf16[2,2,2,4,16,128]{5,4,3,2,1,0:T(8,128)(2,1)} %get-tuple-element.23), channel_id=1, source_target_pairs={{0,80},{8,88},{16,64},{24,72},{32,112},{40,120},{48,96},{56,104},{... | collective-permute-start | bytes 393224 | tf_op jit(solution)/shard_map/ppermute | solution.py:366
  7.7 38.8 %all-to-all-start = ((bf16[8,128,128]{2,1,0:T(8,128)(2,1)}), bf16[8,128,128]{2,1,0:T(8,128)(2,1)S(1)}, u32[]{:S(2)}, u32[]{:S(2)}) async-start(bf16[8,128,128]{2,1,0:T(8,128)(2,1)} %get-tuple-element.20), calls=%async_computation | async-start | bytes 524288 | tf_op jit(solution)/shard_map/all_to_all | solution.py:361
  15.4 10.6 %collective-permute-start.2 = (bf16[2,2,2,4,16,128]{5,4,3,2,1,0:T(8,128)(2,1)}, bf16[2,2,2,4,16,128]{5,4,3,2,1,0:T(8,128)(2,1)S(1)}, u32[]{:S(2)}, u32[]{:S(2)}) collective-permute-start(bf16[2,2,2,4,16,128]{5,4,3,2,1,0:T(8,128)(2,1)} %get-tuple-element.24), channel_id=1, source_target_pairs={{0,48},{8,56},{16,32},{24,40},{32,80},{40,88},{48,64},{56,72},{64,... | collective-permute-start | bytes 393224 | tf_op jit(solution)/shard_map/ppermute | solution.py:366
  16.5 9.8 %collective-permute-start.3 = (bf16[2,2,2,4,16,128]{5,4,3,2,1,0:T(8,128)(2,1)}, bf16[2,2,2,4,16,128]{5,4,3,2,1,0:T(8,128)(2,1)S(1)}, u32[]{:S(2)}, u32[]{:S(2)}) collective-permute-start(bf16[2,2,2,4,16,128]{5,4,3,2,1,0:T(8,128)(2,1)} %get-tuple-element.25), channel_id=1, source_target_pairs={{0,112},{8,120},{16,96},{24,104},{32,16},{40,24},{48,0},{56,8},{64... | collective-permute-start | bytes 393224 | tf_op jit(solution)/shard_map/ppermute | solution.py:366
  19.6 7.2 %collective-permute-start.4 = (bf16[2,2,2,4,16,128]{5,4,3,2,1,0:T(8,128)(2,1)}, bf16[2,2,2,4,16,128]{5,4,3,2,1,0:T(8,128)(2,1)S(1)}, u32[]{:S(2)}, u32[]{:S(2)}) collective-permute-start(bf16[2,2,2,4,16,128]{5,4,3,2,1,0:T(8,128)(2,1)} %get-tuple-element.26), channel_id=1, source_target_pairs={{0,64},{8,72},{16,80},{24,88},{32,96},{40,104},{48,112},{56,120},{... | collective-permute-start | bytes 393224 | tf_op jit(solution)/shard_map/ppermute | solution.py:366
  19.6 9.1 %copy-start.8 = (bf16[2,2,2,4,16,128]{5,4,3,2,1,0:T(8,128)(2,1)}, bf16[2,2,2,4,16,128]{5,4,3,2,1,0:T(8,128)(2,1)S(1)}, u32[]{:S(2)}) copy-start(bf16[2,2,2,4,16,128]{5,4,3,2,1,0:T(8,128)(2,1)S(1)} %collective-permute-done.refs_1_) | copy-start | bytes 393220
  19.6 8.6 %collective-permute-start.5 = (bf16[2,2,2,4,16,128]{5,4,3,2,1,0:T(8,128)(2,1)}, bf16[2,2,2,4,16,128]{5,4,3,2,1,0:T(8,128)(2,1)}, u32[]{:S(2)}, u32[]{:S(2)}) collective-permute-start(bf16[2,2,2,4,16,128]{5,4,3,2,1,0:T(8,128)(2,1)} %get-tuple-element.27), channel_id=1, source_target_pairs={{0,32},{8,40},{16,48},{24,56},{32,64},{40,72},{48,80},{56,88},{64,... | collective-permute-start | bytes 393224 | tf_op jit(solution)/shard_map/ppermute | solution.py:366
  20.4 8.3 %copy-start.9 = (bf16[2,2,2,4,16,128]{5,4,3,2,1,0:T(8,128)(2,1)}, bf16[2,2,2,4,16,128]{5,4,3,2,1,0:T(8,128)(2,1)S(1)}, u32[]{:S(2)}) copy-start(bf16[2,2,2,4,16,128]{5,4,3,2,1,0:T(8,128)(2,1)S(1)} %collective-permute-done.1.refs_2_) | copy-start | bytes 393220
  20.4 8.3 %collective-permute-start.6 = (bf16[2,2,2,4,16,128]{5,4,3,2,1,0:T(8,128)(2,1)}, bf16[2,2,2,4,16,128]{5,4,3,2,1,0:T(8,128)(2,1)}, u32[]{:S(2)}, u32[]{:S(2)}) collective-permute-start(bf16[2,2,2,4,16,128]{5,4,3,2,1,0:T(8,128)(2,1)} %get-tuple-element.28), channel_id=1, source_target_pairs={{0,96},{8,104},{16,112},{24,120},{32,0},{40,8},{48,16},{56,24},{64... | collective-permute-start | bytes 393224 | tf_op jit(solution)/shard_map/ppermute | solution.py:366
  26.1 2.7 %copy-start.10 = (bf16[2,2,2,4,16,128]{5,4,3,2,1,0:T(8,128)(2,1)}, bf16[2,2,2,4,16,128]{5,4,3,2,1,0:T(8,128)(2,1)S(1)}, u32[]{:S(2)}) copy-start(bf16[2,2,2,4,16,128]{5,4,3,2,1,0:T(8,128)(2,1)S(1)} %collective-permute-done.2.refs_3_) | copy-start | bytes 393220
  26.3 2.4 %copy-start.11 = (bf16[2,2,2,4,16,128]{5,4,3,2,1,0:T(8,128)(2,1)}, bf16[2,2,2,4,16,128]{5,4,3,2,1,0:T(8,128)(2,1)S(1)}, u32[]{:S(2)}) copy-start(bf16[2,2,2,4,16,128]{5,4,3,2,1,0:T(8,128)(2,1)S(1)} %collective-permute-done.3.refs_4_) | copy-start | bytes 393220
  26.7 2.0 %copy-start.12 = (bf16[2,2,2,4,16,128]{5,4,3,2,1,0:T(8,128)(2,1)}, bf16[2,2,2,4,16,128]{5,4,3,2,1,0:T(8,128)(2,1)S(1)}, u32[]{:S(2)}) copy-start(bf16[2,2,2,4,16,128]{5,4,3,2,1,0:T(8,128)(2,1)S(1)} %collective-permute-done.4.refs_5_) | copy-start | bytes 393220
  46.4 12.1 %collective-permute-start.7 = (bf16[8,2,2,4,16,128]{5,4,3,2,1,0:T(8,128)(2,1)}, bf16[8,2,2,4,16,128]{5,4,3,2,1,0:T(8,128)(2,1)}, u32[]{:S(2)}, u32[]{:S(2)}) collective-permute-start(bf16[8,2,2,4,16,128]{5,4,3,2,1,0:T(8,128)(2,1)} %get-tuple-element.30), channel_id=1, source_target_pairs={{0,8},{8,0},{16,24},{24,16},{32,40},{40,32},{48,56},{56,48},{64,72... | collective-permute-start | bytes 1572872 | tf_op jit(solution)/shard_map/ppermute | solution.py:371
  46.5 0.7 copy-start.7
  51.4 40.8 %all-to-all-start.1 = ((bf16[8,2,4,32,128]{4,3,2,1,0:T(8,128)(2,1)}), bf16[8,2,4,32,128]{4,3,2,1,0:T(8,128)(2,1)S(1)}, u32[]{:S(2)}, u32[]{:S(2)}) async-start(bf16[8,2,4,32,128]{4,3,2,1,0:T(8,128)(2,1)} %shard_map.129), calls=%async_computation.1 | async-start | bytes 1048576 | tf_op jit(solution)/shard_map/all_to_all | solution.py:393
  92.2 3.5 %copy-start = (bf16[4,2,256,512]{3,2,1,0:T(8,128)(2,1)S(1)}, bf16[4,2,256,512]{3,2,1,0:T(8,128)(2,1)}, u32[]{:S(2)}) copy-start(bf16[4,2,256,512]{3,2,1,0:T(8,128)(2,1)} %constant.17.clone.third_ref) | copy-start | bytes 6291460
  92.2 1.7 %copy-start.1 = (bf16[4,256,1024]{2,1,0:T(8,128)(2,1)S(1)}, bf16[4,256,1024]{2,1,0:T(8,128)(2,1)}, u32[]{:S(2)}) copy-start(bf16[4,256,1024]{2,1,0:T(8,128)(2,1)} %constant.16.clone.table_ref) | copy-start | bytes 6291460
  94.0 0.7 copy-start.5
  94.7 1.2 copy-start.2
  94.7 1.4 copy-start.4
  95.4 3.0 %collective-permute-start.8 = (f32[2,1024,128]{2,1,0:T(8,128)S(1)}, f32[2,1024,128]{2,1,0:T(8,128)S(1)}, u32[]{:S(2)}, u32[]{:S(2)}) collective-permute-start(f32[2,1024,128]{2,1,0:T(8,128)S(1)} %shard_map.131.spec), channel_id=1, source_target_pairs={{0,8},{8,0},{16,24},{24,16},{32,40},{40,32},{48,56},{56,48},{64,72... | collective-permute-start | bytes 3145736 | tf_op jit(solution)/shard_map/ppermute | solution.py:398
  96.0 1.2 copy-start.3
  99.6 36.5 %copy-start.6 = (bf16[4,2,256,256]{3,2,1,0:T(8,128)(2,1)S(1)}, bf16[4,2,256,256]{3,2,1,0:T(8,128)(2,1)}, u32[]{:S(2)}) copy-start(bf16[4,2,256,256]{3,2,1,0:T(8,128)(2,1)} %constant.20.clone.table_ref) | copy-start | bytes 3145732

commit v4 on v2

--- a/solution.py
+++ b/solution.py
@@ -16,7 +16,7 @@
 SMEM = pl.BlockSpec(memory_space=pltpu.SMEM)
 ANY = pl.BlockSpec(memory_space=pl.ANY)
 MIB = 1 << 20
-OFFSETS = [(rz, rx) for rz in range(2) for rx in range(4)]
+OFFSETS = [(0, 0), (1, 0), (1, 2), (1, 1), (1, 3), (0, 2), (0, 1), (0, 3)]
 
 
 def phases(product, count):
@@ -34,19 +34,18 @@
 @functools.cache
 def tables():
     q = np.arange(256)
-    first = []
-    for r in range(4):
-        c, s = phases((4 * q[:, None] + r) * q[None, :], 1024)
-        first.append(np.stack([np.stack(split_hi_lo(c)), np.stack(split_hi_lo(-s))]))
+    c, s = phases(q[:, None] * q[None, :], 256)
+    first = np.stack(split_hi_lo(np.concatenate([c, -s], axis=1)))
     k2 = np.arange(1024)
-    rows = np.concatenate([4 * np.arange(32), 128 * np.arange(8), np.arange(8)])
+    rows = np.concatenate([4 * np.arange(32), 128 * np.arange(8), np.arange(8), 1024 * np.arange(8)])
     c, s = phases(rows[:, None] * k2[None, :], NSAMP)
     turn = np.stack([c, -s]).astype(np.float32)
-    second = []
-    for r in range(4):
-        c, s = phases(q[:, None] * (4 * q[None, :] + r), 1024)
-        (ch, cl), (sh, sl) = split_hi_lo(c), split_hi_lo(s)
-        second.append(np.concatenate([ch, sh, cl, sl], axis=1))
+    c, s = phases(q[:, None] * q[None, :], 256)
+    (ch, cl), (sh, sl) = split_hi_lo(c), split_hi_lo(s)
+    second = np.concatenate([ch, sh, cl, sl], axis=1)
+    c, s = phases(q[:, None] * np.arange(4)[None, :], 1024)
+    lag = np.zeros((256, 128), np.float32)
+    lag[:, 0:8:2], lag[:, 1:8:2] = c, -s
     third = []
     for p in range(4):
         c, s = phases(q[:, None] * (4 * q[None, :] + p), 1024)
@@ -62,9 +61,10 @@
         c, s = phases((4 * q[:, None] + p) * q[None, :], 1024)
         last.append(np.stack([c, s]).astype(np.float32))
     return dict(
-        first=np.stack(first),
+        first=first,
         turn=turn,
-        second=np.stack(second),
+        second=second,
+        lag=lag,
         third=np.stack(third).astype(jnp.bfloat16),
         back=back,
         shift=shift,
@@ -86,11 +86,10 @@
 
 
 def gate_kernel(
-    strain_ref, start_any, span_any, assign_any, bank_any, asd_any, back_any, shift_any,
-    out_ref, weight_ref, twist_ref, *rest
+    strain_ref, start_any, span_any, assign_any, bank_any, out_ref, *rest
 ):
     pick_refs, rest = rest[:8], rest[8:]
-    strain, bank_ref, start_ref, span_ref, assign_ref, asd_ref, back_ref, shift_ref, sems = rest
+    strain, bank_ref, start_ref, span_ref, assign_ref, sems = rest
     x, z, core = place()
     copies = [
         pltpu.make_async_copy(start_any, start_ref, sems.at[0]),
@@ -98,9 +97,6 @@
         pltpu.make_async_copy(strain_ref.at[core], strain, sems.at[2]),
         pltpu.make_async_copy(assign_any, assign_ref, sems.at[3]),
         pltpu.make_async_copy(bank_any, bank_ref, sems.at[4]),
-        pltpu.make_async_copy(asd_any, asd_ref, sems.at[5]),
-        pltpu.make_async_copy(back_any, back_ref, sems.at[6]),
-        pltpu.make_async_copy(shift_any, shift_ref, sems.at[7]),
     ]
     for copy in copies:
         copy.start()
@@ -128,7 +124,7 @@
     for copy in copies[3:5]:
         copy.wait()
     for i in range(16):
-        rz, rx, rc = i // 8, i // 2 % 4, i % 2
+        (rz, rx), rc = OFFSETS[i // 2], i % 2
         dest = ((x + rx) % 4) * 4 + (z + rz) % 2 * 2 + (core + rc) % 2
         for slot in range(2):
             chosen = assign_ref[2 * dest + slot]
@@ -137,12 +133,22 @@
                     value = bank_ref[part, chosen, pl.ds(p, 16, stride=4), :].astype(BF)
                     pick_refs[i // 2][rc, slot, part, p] = value
 
-    for copy in copies[5:]:
-        copy.wait()
+
+def prepare_kernel(asd_any, back_any, shift_any, weight_ref, twist_ref, asd_ref, back_ref, shift_ref, sems):
+    copies = [
+        pltpu.make_async_copy(asd_any, asd_ref, sems.at[0]),
+        pltpu.make_async_copy(back_any, back_ref, sems.at[1]),
+        pltpu.make_async_copy(shift_any, shift_ref, sems.at[2]),
+    ]
+    for copy in copies:
+        copy.start()
+    copies[0].wait()
     for p in range(4):
         asd = asd_ref[pl.ds(p, 256, stride=4), :]
         weight_ref[p] = 1.0 / (asd * asd)
-    own = lane == lax.axis_index("seg")
+    copies[1].wait()
+    copies[2].wait()
+    own = lax.broadcasted_iota(jnp.int32, (128, 128), 1) == lax.axis_index("seg")
     for i in range(8):
         rows = slice(128 * i, 128 * i + 128)
         shift = [jnp.sum(jnp.where(own, shift_ref[part, rows, :], 0.0), axis=1, keepdims=True) for part in range(2)]
@@ -176,10 +182,8 @@
 
 def first_kernel(cols_ref, table_ref, turn_ref, after_ref, out_ref, z_ref):
     del after_ref
-    for r in range(4):
-        turned = cols_ref[:, 32 * r : 32 * r + 32, :].reshape(256, 128).T
-        for part in range(2):
-            z_ref[r, part] = dot(turned, table_ref[r, part, 0]) + dot(turned, table_ref[r, part, 1])
+    turned = jnp.concatenate([cols_ref[:, 32 * r : 32 * r + 32, :].reshape(256, 128).T for r in range(4)], axis=0)
+    z_ref[...] = dot(turned, table_ref[0]) + dot(turned, table_ref[1])
     seg = 32 + lax.axis_index("seg")
     seg_re, seg_im = turn_ref[0, pl.ds(seg, 1), :], turn_ref[1, pl.ds(seg, 1), :]
     for r1 in range(4):
@@ -192,7 +196,15 @@
             fr, fi = turn_ref[0, at, :], turn_ref[1, at, :]
             tr = fr * base_re - fi * base_im
             ti = fr * base_im + fi * base_re
-            outs = four_way(-1, [(z_ref[r, 0, rows, :], z_ref[r, 1, rows, :]) for r in range(4)])
+            sums = []
+            for r in range(4):
+                here = slice(128 * r + rows.start, 128 * r + rows.stop)
+                re, im = z_ref[here, :256], z_ref[here, 256:]
+                if r > 0:
+                    pr, pi = turn_ref[0, 48 + r : 49 + r, :256], turn_ref[1, 48 + r : 49 + r, :256]
+                    re, im = re * pr - im * pi, re * pi + im * pr
+                sums.append((re, im))
+            outs = four_way(-1, sums)
             for k, (re, im) in enumerate(outs):
                 wr, wi = tr[:, 256 * k : 256 * k + 256], ti[:, 256 * k : 256 * k + 256]
                 done = ((re * wr - im * wi).astype(BF), (re * wi + im * wr).astype(BF))
@@ -201,29 +213,33 @@
                         out_ref[2 * k + half, part, r1, at] = done[part][:, 128 * half : 128 * half + 128]
 
 
-def second_kernel(own_ref, table_ref, after_ref, spec_ref, z_ref):
+def second_kernel(own_ref, table_ref, lag_ref, after_ref, spec_ref, z_ref):
     del after_ref
     for r in range(4):
         re = own_ref[:, 0, r].reshape(256, 128)
         im = own_ref[:, 1, r].reshape(256, 128)
         right = jnp.concatenate([jnp.concatenate([re, im], axis=1), jnp.concatenate([im, -re], axis=1)], axis=0)
-        z_ref[r] = dot(table_ref[r, :, :512], right) + dot(table_ref[r, :, 512:], right)
+        z_ref[r] = dot(table_ref[:, :512], right) + dot(table_ref[:, 512:], right)
     for i in range(8):
         rows = slice(32 * i, 32 * i + 32)
-        outs = four_way(-1, [(z_ref[r, rows, :128], z_ref[r, rows, 128:]) for r in range(4)])
-        for k, parts in enumerate(outs):
+        sums = [(z_ref[0, rows, :128], z_ref[0, rows, 128:])]
+        for r in range(1, 4):
+            pr, pi = lag_ref[rows, 2 * r : 2 * r + 1], lag_ref[rows, 2 * r + 1 : 2 * r + 2]
+            re, im = z_ref[r, rows, :128], z_ref[r, rows, 128:]
+            sums.append((re * pr - im * pi, re * pi + im * pr))
+        for k, parts in enumerate(four_way(-1, sums)):
             for part in range(2):
                 spec_ref[part, 256 * k + 32 * i : 256 * k + 32 * i + 32, :] = parts[part]
 
 
 def assemble_kernel(*refs):
-    piece_refs, cross_ref, bank, sems = refs[:8], refs[8], refs[9], refs[10]
+    piece_refs, cross_ref, _, bank, sems = refs[:8], *refs[8:]
     x, z, core = place()
     copies = []
-    for i in range(8):
+    for i, (rz, rx) in enumerate(OFFSETS):
         for rc in range(2):
             src = piece_refs[i].at[0] if rc == 0 else cross_ref.at[i]
-            origin = ((x + 4 - i % 4) % 4) * 4 + (z + i // 4) % 2 * 2 + (core + rc) % 2
+            origin = ((x + 4 - rx) % 4) * 4 + (z + rz) % 2 * 2 + (core + rc) % 2
             copies.append(pltpu.make_async_copy(src, bank.at[origin], sems.at[len(copies)]))
     for copy in copies:
         copy.start()
@@ -282,7 +298,7 @@
     filter_segment(spec, weight_ref, third_ref, twist, bank, out_ref, 528, v_ref, None)
 
 
-def last_kernel(in_ref, table_ref, out_ref):
+def last_kernel(in_ref, table_ref, out_any, out_ref, sems):
     total = jnp.zeros((16, 128), F32)
     for s in range(8):
         total = total + in_ref[s, 512:528, :].astype(F32)
@@ -293,6 +309,7 @@
         sigma2 = jnp.sum(jnp.where(mine, total, 0.0), axis=(0, 1), keepdims=True)
         scales.append(1.0 / jnp.sqrt(NSAMP * sigma2))
     _, _, core = place()
+    copies = []
     for pair in range(4):
         other, slot = pair // 2, pair % 2
         seg = (core + other) % 2
@@ -311,7 +328,11 @@
             sin = dot_nt(table_ref[p, 1], hi) + dot_nt(table_ref[p, 1], lo)
             sr = cos[:, :128] - sin[:, 128:]
             si = sin[:, :128] + cos[:, 128:]
-            out_ref[seg, slot, pl.ds(p, 256, stride=4), :] = jnp.sqrt(sr * sr + si * si) * scales[slot]
+            out_ref[pair, pl.ds(p, 256, stride=4), :] = jnp.sqrt(sr * sr + si * si) * scales[slot]
+        copies.append(pltpu.make_async_copy(out_ref.at[pair], out_any.at[seg, slot], sems.at[pair]))
+        copies[pair].start()
+    for copy in copies:
+        copy.wait()
 
 
 def call(kernel, ins, outs, specs, flops, moved, scratch=(), limit=16, space=VMEM):
@@ -335,17 +356,12 @@
     swap_core = [(i, i ^ 1) for i in range(16)]
 
     blk = (2, 2, 4, 16, 128)
-    gated, weight, twist, *picked = call(
-        gate_kernel, (strain, gate_start, gate_span, assign, bank, asd, const["back"], const["shift"]),
-        (
-            shape(8, 128, 128), shape(4, 256, 128, dtype=F32), shape(2, 1024, 128, dtype=F32),
-            *[shape(2, *blk)] * 8,
-        ),
-        [ANY] * 8, 10**8, 4 * MIB,
+    gated, *picked = call(
+        gate_kernel, (strain, gate_start, gate_span, assign, bank), (shape(8, 128, 128), *[shape(2, *blk)] * 8),
+        [ANY] * 5, 10**8, 4 * MIB,
         [
             pltpu.VMEM((128, 1024), F32), pltpu.VMEM((2, 32, 64, 128), F32), pltpu.SMEM((2, 1, 2), jnp.int32),
-            pltpu.SMEM((2, 1, 2), jnp.int32), pltpu.SMEM((32,), jnp.int32), pltpu.VMEM((1024, 128), F32),
-            pltpu.VMEM((2, 1024, 128), F32), pltpu.VMEM((2, 1024, 128), F32), pltpu.SemaphoreType.DMA((8,)),
+            pltpu.SMEM((2, 1, 2), jnp.int32), pltpu.SMEM((32,), jnp.int32), pltpu.SemaphoreType.DMA((5,)),
         ],
         limit=63,
     )
@@ -360,18 +376,27 @@
         [pltpu.SemaphoreType.DMA((8,))], limit=8, space=(ANY, VMEM),
     )
     crossed = lax.ppermute(cross, "tmpl", swap_core)
+    weight, twist = call(
+        prepare_kernel, (asd, const["back"], const["shift"]),
+        (shape(4, 256, 128, dtype=F32), shape(2, 1024, 128, dtype=F32)), [ANY] * 3, 1, 10 * MIB,
+        [
+            pltpu.VMEM((1024, 128), F32), pltpu.VMEM((2, 1024, 128), F32), pltpu.VMEM((2, 1024, 128), F32),
+            pltpu.SemaphoreType.DMA((3,)),
+        ],
+        limit=63,
+    )
     ordered = call(
-        assemble_kernel, (*pieces, crossed), shape(16, *blk), [ANY] * 9, 1, 10 * MIB, [pltpu.SemaphoreType.DMA((16,))],
-        limit=8,
+        assemble_kernel, (*pieces, crossed, weight), shape(16, *blk), [ANY] * 10, 1, 10 * MIB,
+        [pltpu.SemaphoreType.DMA((16,))], limit=8,
     )
     turned = call(
         first_kernel, (columns, const["first"], const["turn"], token),
-        shape(8, 2, 4, 32, 128), [VMEM] * 3 + [ANY], 3 * 10**8, 4 * MIB, [pltpu.VMEM((4, 2, 128, 256), F32)],
+        shape(8, 2, 4, 32, 128), [VMEM] * 3 + [ANY], 3 * 10**8, 4 * MIB, [pltpu.VMEM((512, 512), F32)],
     )
     own = lax.all_to_all(turned, "seg", 0, 0)
     spec = call(
-        second_kernel, (own, const["second"], ordered), shape(2, 1024, 128, dtype=F32),
-        [VMEM] * 2 + [ANY], 1, 1, [pltpu.VMEM((4, 256, 256), F32)],
+        second_kernel, (own, const["second"], const["lag"], ordered), shape(2, 1024, 128, dtype=F32),
+        [VMEM] * 3 + [ANY], 1, 1, [pltpu.VMEM((4, 256, 256), F32)],
     )
     other_spec = lax.ppermute(spec, "tmpl", swap_core)
     half = call(
@@ -386,7 +411,8 @@
     )
     series = lax.all_to_all(inner, "seg", 0, 0)
     return call(
-        last_kernel, (series, const["last"]), shape(2, 2, 1024, 128, dtype=F32), [VMEM] * 2, 3 * 10**9, 6 * MIB
+        last_kernel, (series, const["last"]), shape(2, 2, 1024, 128, dtype=F32), [VMEM] * 2, 3 * 10**9, 6 * MIB,
+        [pltpu.VMEM((4, 1024, 128), F32), pltpu.SemaphoreType.DMA((4,))], space=ANY,
     )
 
 

time: 101 us -> 97.5 us (0.965)
  waiting for transfers between devices: 21.5 us -> 11.5 us
  local copies, waits for them, and re-layouts: 4.1 us -> 7.12 us
  Pallas kernels: 16.2 us -> 17.9 us
  starting transfers between devices: 25.6 us -> 27.3 us
    all_to_all x1, waiting for transfers between devices: 10.7 us -> 5.51 us  [per_device(): own = lax.all_to_all(turned, 'seg', 0, 0)]
    ppermute x7, waiting for transfers between devices: 9.36 us -> 5.77 us  [per_device(): pieces.append(lax.ppermute(send, 'tmpl', hop))]
    unnamed x18 -> x38, local copies, waits for them, and re-layouts: 4.1 us -> 7.12 us
    pallas_call x8 -> x9, Pallas kernels: 16.2 us -> 17.9 us  [call(): pl.pallas_call(kernel, out_shape=outs, in_specs=specs, out_specs=space if...]
    ppermute x1, waiting for transfers between devices: 1.46 us -> 0.25 us  [per_device(): other_spec = lax.ppermute(spec, 'tmpl', swap_core)]
  transfers between devices with their start and end apart: 11 -> 11, of which waited for: 3 -> 7; matrix products, arithmetic and copies ran while one was open for 0% -> 0% of each run, Pallas kernels for 5% -> 9%
where the time goes in v4:
time: 97.5 us; the launch traced here: 96.4 us
  blocking collectives  32.2 us (33%)
  starting transfers between devices  27.3 us (28%)
  Pallas kernels  17.9 us (18%)
  waiting for transfers between devices  11.5 us (12%)
  local copies, waits for them, and re-layouts  7.12 us (7%)
    all_to_all x1, blocking collectives, per_device(): series = lax.all_to_all(inner, 'seg', 0, 0)  32.2 us
    pallas_call x9, Pallas kernels, call(): pl.pallas_call(kernel, out_shape=outs, in_specs=specs, out_specs=space if...  17.9 us
    ppermute x7, starting transfers between devices, per_device(): pieces.append(lax.ppermute(send, 'tmpl', hop))  12 us
    all_to_all x1, starting transfers between devices, per_device(): columns = lax.all_to_all(gated, 'seg', 0, 0)  7.78 us
    all_to_all x1, starting transfers between devices, per_device(): own = lax.all_to_all(turned, 'seg', 0, 0)  7.31 us
    unnamed x38, local copies, waits for them, and re-layouts  7.12 us
    ppermute x7, waiting for transfers between devices, per_device(): pieces.append(lax.ppermute(send, 'tmpl', hop))  5.77 us
    all_to_all x1, waiting for transfers between devices, per_device(): own = lax.all_to_all(turned, 'seg', 0, 0)  5.51 us
  transfers between devices with their start and end apart: 11, of which 7 were waited for; matrix products, arithmetic and copies ran while one was open for 0% of the time, Pallas kernels for 9%

profile of v4, /device:TPU:0, one launch (start us, length us, event | category | flops | bytes accessed | tf_op | source)
XLA Modules:
  0.0 96.4 jit_solution(44776934664745931)
XLA Ops:
  0.0 3.0 %shard_map.136 = (bf16[8,128,128]{2,1,0:T(8,128)(2,1)}, bf16[2,2,2,4,16,128]{5,4,3,2,1,0:T(8,128)(2,1)}, bf16[2,2,2,4,16,128]{5,4,3,2,1,0:T(8,128)(2,1)}, bf16[2...) custom-call(f32[2,128,1024]{2,1,0:T(8,128)} %strain_ref.1, ...), custom_call_target="tpu_custom_call" | custom-call | flops 100000000 | bytes 4194304 | tf_op jit(solution)/shard_map/pallas_call | solution.py:339
  3.0 2.1 %collective-permute-start = (bf16[2,2,2,4,16,128]{5,4,3,2,1,0:T(8,128)(2,1)}, bf16[2,2,2,4,16,128]{5,4,3,2,1,0:T(8,128)(2,1)S(1)}, u32[]{:S(2)}, u32[]{:S(2)}) collective-permute-start(bf16[2,2,2,4,16,128]{5,4,3,2,1,0:T(8,128)(2,1)} %get-tuple-element.20), channel_id=1, source_target_pairs={{0,16},{8,24},{16,0},{24,8},{32,48},{40,56},{48,32},{56,40},{64,80... | collective-permute-start | bytes 393224 | tf_op jit(solution)/shard_map/ppermute | solution.py:373
  5.1 2.6 %collective-permute-start.1 = (bf16[2,2,2,4,16,128]{5,4,3,2,1,0:T(8,128)(2,1)}, bf16[2,2,2,4,16,128]{5,4,3,2,1,0:T(8,128)(2,1)S(1)}, u32[]{:S(2)}, u32[]{:S(2)}) collective-permute-start(bf16[2,2,2,4,16,128]{5,4,3,2,1,0:T(8,128)(2,1)} %get-tuple-element.21), channel_id=1, source_target_pairs={{0,80},{8,88},{16,64},{24,72},{32,112},{40,120},{48,96},{56,104},{... | collective-permute-start | bytes 393224 | tf_op jit(solution)/shard_map/ppermute | solution.py:373
  7.7 7.8 %all-to-all-start = ((bf16[8,128,128]{2,1,0:T(8,128)(2,1)}), bf16[8,128,128]{2,1,0:T(8,128)(2,1)S(1)}, u32[]{:S(2)}, u32[]{:S(2)}) async-start(bf16[8,128,128]{2,1,0:T(8,128)(2,1)} %get-tuple-element.18), calls=%async_computation | async-start | bytes 524288 | tf_op jit(solution)/shard_map/all_to_all | solution.py:368
  15.5 1.0 %collective-permute-start.2 = (bf16[2,2,2,4,16,128]{5,4,3,2,1,0:T(8,128)(2,1)}, bf16[2,2,2,4,16,128]{5,4,3,2,1,0:T(8,128)(2,1)S(1)}, u32[]{:S(2)}, u32[]{:S(2)}) collective-permute-start(bf16[2,2,2,4,16,128]{5,4,3,2,1,0:T(8,128)(2,1)} %get-tuple-element.22), channel_id=1, source_target_pairs={{0,48},{8,56},{16,32},{24,40},{32,80},{40,88},{48,64},{56,72},{64,... | collective-permute-start | bytes 393224 | tf_op jit(solution)/shard_map/ppermute | solution.py:373
  16.5 3.1 %collective-permute-start.3 = (bf16[2,2,2,4,16,128]{5,4,3,2,1,0:T(8,128)(2,1)}, bf16[2,2,2,4,16,128]{5,4,3,2,1,0:T(8,128)(2,1)S(1)}, u32[]{:S(2)}, u32[]{:S(2)}) collective-permute-start(bf16[2,2,2,4,16,128]{5,4,3,2,1,0:T(8,128)(2,1)} %get-tuple-element.23), channel_id=1, source_target_pairs={{0,112},{8,120},{16,96},{24,104},{32,16},{40,24},{48,0},{56,8},{64... | collective-permute-start | bytes 393224 | tf_op jit(solution)/shard_map/ppermute | solution.py:373
  19.6 0.8 collective-permute-start.5
  20.4 2.5 %collective-permute-start.6 = (bf16[2,2,2,4,16,128]{5,4,3,2,1,0:T(8,128)(2,1)}, bf16[2,2,2,4,16,128]{5,4,3,2,1,0:T(8,128)(2,1)S(1)}, u32[]{:S(2)}, u32[]{:S(2)}) collective-permute-start(bf16[2,2,2,4,16,128]{5,4,3,2,1,0:T(8,128)(2,1)} %get-tuple-element.26), channel_id=1, source_target_pairs={{0,96},{8,104},{16,112},{24,120},{32,0},{40,8},{48,16},{56,24},{64... | collective-permute-start | bytes 393224 | tf_op jit(solution)/shard_map/ppermute | solution.py:373
  22.9 3.2 %collective-permute-done.2.refs_3_ = bf16[2,2,2,4,16,128]{5,4,3,2,1,0:T(8,128)(2,1)S(1)} collective-permute-done((bf16[2,2,2,4,16,128]{5,4,3,2,1,0:T(8,128)(2,1)}, bf16[2,2,2,4,16,128]{5,4,3,2,1,0:T(8,128)(2,1)S(1)}, u32[]{:S(2)}, u32[]{:S(2)}) %collective-permute-start.2) | collective-permute-done | bytes 131104 | tf_op jit(solution)/shard_map/ppermute | solution.py:373
  26.1 0.2 collective-permute-done.3.refs_4_
  26.3 0.4 collective-permute-done.4.refs_5_
  26.8 1.3 %collective-permute-done.5.refs_6_ = bf16[2,2,2,4,16,128]{5,4,3,2,1,0:T(8,128)(2,1)S(1)} collective-permute-done((bf16[2,2,2,4,16,128]{5,4,3,2,1,0:T(8,128)(2,1)}, bf16[2,2,2,4,16,128]{5,4,3,2,1,0:T(8,128)(2,1)S(1)}, u32[]{:S(2)}, u32[]{:S(2)}) %collective-permute-start.5) | collective-permute-done | bytes 131104 | tf_op jit(solution)/shard_map/ppermute | solution.py:373
  28.1 0.6 collective-permute-done.6.refs_7_
  28.6 0.9 copy-done.6
  29.6 0.9 shard_map.137
  30.6 1.0 %copy-done.16 = f32[2,56,1024]{2,1,0:T(8,128)S(1)} copy-done((f32[2,56,1024]{2,1,0:T(8,128)S(1)}, f32[2,56,1024]{2,1,0:T(8,128)}, u32[]{:S(2)}) %copy-start.16) | copy-done | bytes 458776
  31.7 1.6 %shard_map.138 = bf16[8,2,4,32,128]{4,3,2,1,0:T(8,128)(2,1)} custom-call(bf16[8,128,128]{2,1,0:T(8,128)(2,1)S(1)} %all-to-all-done.cols_ref, bf16[2,256,512]{2,1,0:T(8,128)(2,1)S(1)} %copy-done.5, f32[2,56,1024]{2,1,0:T(8,128)S(1)} %copy-done.16, f32[8,128]{1,0:T(8,128)S(1)} %get-tuple-element.27.after_ref), custom_call_target="tpu_custom_call" | custom-call | flops 300000000 | bytes 4194304 | tf_op jit(solution)/shard_map/pallas_call | solution.py:339
  33.3 7.3 %all-to-all-start.1 = ((bf16[8,2,4,32,128]{4,3,2,1,0:T(8,128)(2,1)}), bf16[8,2,4,32,128]{4,3,2,1,0:T(8,128)(2,1)}, u32[]{:S(2)}, u32[]{:S(2)}) async-start(bf16[8,2,4,32,128]{4,3,2,1,0:T(8,128)(2,1)} %shard_map.138), calls=%async_computation.1 | async-start | bytes 1048576 | tf_op jit(solution)/shard_map/all_to_all | solution.py:396
  40.6 3.1 %shard_map.139 = (f32[4,256,128]{2,1,0:T(8,128)}, f32[2,1024,128]{2,1,0:T(8,128)}) custom-call(f32[1024,128]{1,0:T(8,128)} %asd_any.1, f32[2,1024,128]{2,1,0:T(8,128)} %constant.21.clone.back_any, f32[2,1024,128]{2,1,0:T(8,128)} %constant.22.clone.shift_any), custom_call_target="tpu_custom_call" | custom-call | flops 1 | bytes 10485760 | tf_op jit(solution)/shard_map/pallas_call | solution.py:339
  43.7 1.0 %copy-done.1 = f32[4,256,128]{2,1,0:T(8,128)S(1)} copy-done((f32[4,256,128]{2,1,0:T(8,128)S(1)}, f32[4,256,128]{2,1,0:T(8,128)}, u32[]{:S(2)}) %copy-start.1) | copy-done | bytes 524312
  44.7 0.9 copy-done.15
  45.6 1.7 %shard_map.140.after_ref.bank = bf16[16,2,2,4,16,128]{5,4,3,2,1,0:T(8,128)(2,1)S(1)} custom-call(bf16[2,2,2,4,16,128]{5,4,3,2,1,0:T(8,128)(2,1)S(1)} %copy-done.7, bf16[2,2,2,4,16,128]{5,4,3,2,1,0:T(8,128)(2,1)S(1)} %collective-permute-done.refs_1_, bf16[2,2,2,4,16,128]{5,4,3,2,1,0:T(8,128)(2,1)S(1)} %collective-permute-done.1.refs_2_, ...), custom_call_target="tpu_custom_call" | custom-call | flops 1 | bytes 10485760 | tf_op jit(solution)/shard_map/pallas_call | solution.py:339
  47.4 5.5 %all-to-all-done.1.own_ref = bf16[8,2,4,32,128]{4,3,2,1,0:T(8,128)(2,1)} async-done(((bf16[8,2,4,32,128]{4,3,2,1,0:T(8,128)(2,1)}), bf16[8,2,4,32,128]{4,3,2,1,0:T(8,128)(2,1)}, u32[]{:S(2)}, u32[]{:S(2)}) %all-to-all-start.1) | async-done | bytes 524320 | tf_op jit(solution)/shard_map/all_to_all | solution.py:396
  52.9 1.0 %copy-done.4 = bf16[256,1024]{1,0:T(8,128)(2,1)S(1)} copy-done((bf16[256,1024]{1,0:T(8,128)(2,1)S(1)}, bf16[256,1024]{1,0:T(8,128)(2,1)}, u32[]{:S(2)}) %copy-start.4) | copy-done | bytes 524312
  54.0 0.9 copy-done.17
  54.9 1.9 %shard_map.141.spec = f32[2,1024,128]{2,1,0:T(8,128)S(1)} custom-call(bf16[8,2,4,32,128]{4,3,2,1,0:T(8,128)(2,1)} %all-to-all-done.1.own_ref, bf16[256,1024]{1,0:T(8,128)(2,1)S(1)} %copy-done.4, f32[256,128]{1,0:T(8,128)S(1)} %copy-done.17, bf16[16,2,2,4,16,128]{5,4,3,2,1,0:T(8,128)(2,1)S(1)} %shard_map.140.after_ref.bank), custom_call_target="tpu_custom_call" | custom-call | flops 1 | bytes 1 | tf_op jit(solution)/shard_map/pallas_call | solution.py:339
  56.9 1.2 %copy-done.3 = f32[2,1024,128]{2,1,0:T(8,128)S(1)} copy-done((f32[2,1024,128]{2,1,0:T(8,128)S(1)}, f32[2,1024,128]{2,1,0:T(8,128)}, u32[]{:S(2)}) %copy-start.3) | copy-done | bytes 1048600
  58.1 1.1 %shard_map.142.half_ref = bf16[8,528,128]{2,1,0:T(8,128)(2,1)S(1)} custom-call(f32[2,1024,128]{2,1,0:T(8,128)S(1)} %shard_map.141.spec, f32[4,256,128]{2,1,0:T(8,128)S(1)} %copy-done.2, bf16[4,2,256,512]{3,2,1,0:T(8,128)(2,1)S(1)} %copy-done, f32[2,1024,128]{2,1,0:T(8,128)S(1)} %copy-done.3, bf16[16,2,2,4,16,128]{5,4,3,2,1,0:T(8,128)(2,1)S(1)} %shard_map.140.after_ref.bank), custom_call_target="tpu_custom_call" | custom-call | flops 2000000000 | bytes 10485760 | tf_op jit(solution)/shard_map/pallas_call | solution.py:339
  59.2 0.3 collective-permute-done.8.spec
  59.5 1.2 %shard_map.143 = bf16[8,1040,128]{2,1,0:T(8,128)(2,1)S(1)} custom-call(f32[2,1024,128]{2,1,0:T(8,128)S(1)} %collective-permute-done.8.spec, f32[4,256,128]{2,1,0:T(8,128)S(1)} %copy-done.2, bf16[4,2,256,512]{3,2,1,0:T(8,128)(2,1)S(1)} %copy-done, f32[2,1024,128]{2,1,0:T(8,128)S(1)} %copy-done.3, ...), custom_call_target="tpu_custom_call" | custom-call | flops 2000000000 | bytes 10485760 | tf_op jit(solution)/shard_map/pallas_call | solution.py:339
  60.7 32.2 %all_to_all.15.in_ref = bf16[8,1040,128]{2,1,0:T(8,128)(2,1)S(1)} all-to-all(bf16[8,1040,128]{2,1,0:T(8,128)(2,1)S(1)} %shard_map.143), channel_id=1, replica_groups=mesh['tmpl'=16,'seg'=8] {'seg'}, dimensions={0} | all-to-all | bytes 4259840 | tf_op jit(solution)/shard_map/all_to_all | solution.py:412
  92.9 3.5 %shard_map.144 = f32[2,2,1024,128]{3,2,1,0:T(8,128)} custom-call(bf16[8,1040,128]{2,1,0:T(8,128)(2,1)S(1)} %all_to_all.15.in_ref, bf16[4,2,256,256]{3,2,1,0:T(8,128)(2,1)S(1)} %copy-done.18), custom_call_target="tpu_custom_call" | custom-call | flops 3000000000 | bytes 6291456 | tf_op jit(solution)/shard_map/pallas_call | solution.py:339
  (38 shorter events, 0.3 us)
Async XLA Ops:
  0.0 30.6 %copy-start.5 = (bf16[2,256,512]{2,1,0:T(8,128)(2,1)S(1)}, bf16[2,256,512]{2,1,0:T(8,128)(2,1)}, u32[]{:S(2)}) copy-start(bf16[2,256,512]{2,1,0:T(8,128)(2,1)} %constant.16.clone.table_ref) | copy-start | bytes 1572868
  3.0 16.6 %collective-permute-start = (bf16[2,2,2,4,16,128]{5,4,3,2,1,0:T(8,128)(2,1)}, bf16[2,2,2,4,16,128]{5,4,3,2,1,0:T(8,128)(2,1)S(1)}, u32[]{:S(2)}, u32[]{:S(2)}) collective-permute-start(bf16[2,2,2,4,16,128]{5,4,3,2,1,0:T(8,128)(2,1)} %get-tuple-element.20), channel_id=1, source_target_pairs={{0,16},{8,24},{16,0},{24,8},{32,48},{40,56},{48,32},{56,40},{64,80... | collective-permute-start | bytes 393224 | tf_op jit(solution)/shard_map/ppermute | solution.py:373
  5.1 15.3 %collective-permute-start.1 = (bf16[2,2,2,4,16,128]{5,4,3,2,1,0:T(8,128)(2,1)}, bf16[2,2,2,4,16,128]{5,4,3,2,1,0:T(8,128)(2,1)S(1)}, u32[]{:S(2)}, u32[]{:S(2)}) collective-permute-start(bf16[2,2,2,4,16,128]{5,4,3,2,1,0:T(8,128)(2,1)} %get-tuple-element.21), channel_id=1, source_target_pairs={{0,80},{8,88},{16,64},{24,72},{32,112},{40,120},{48,96},{56,104},{... | collective-permute-start | bytes 393224 | tf_op jit(solution)/shard_map/ppermute | solution.py:373
  7.7 22.9 %all-to-all-start = ((bf16[8,128,128]{2,1,0:T(8,128)(2,1)}), bf16[8,128,128]{2,1,0:T(8,128)(2,1)S(1)}, u32[]{:S(2)}, u32[]{:S(2)}) async-start(bf16[8,128,128]{2,1,0:T(8,128)(2,1)} %get-tuple-element.18), calls=%async_computation | async-start | bytes 524288 | tf_op jit(solution)/shard_map/all_to_all | solution.py:368
  15.5 10.6 %collective-permute-start.2 = (bf16[2,2,2,4,16,128]{5,4,3,2,1,0:T(8,128)(2,1)}, bf16[2,2,2,4,16,128]{5,4,3,2,1,0:T(8,128)(2,1)S(1)}, u32[]{:S(2)}, u32[]{:S(2)}) collective-permute-start(bf16[2,2,2,4,16,128]{5,4,3,2,1,0:T(8,128)(2,1)} %get-tuple-element.22), channel_id=1, source_target_pairs={{0,48},{8,56},{16,32},{24,40},{32,80},{40,88},{48,64},{56,72},{64,... | collective-permute-start | bytes 393224 | tf_op jit(solution)/shard_map/ppermute | solution.py:373
  16.5 9.8 %collective-permute-start.3 = (bf16[2,2,2,4,16,128]{5,4,3,2,1,0:T(8,128)(2,1)}, bf16[2,2,2,4,16,128]{5,4,3,2,1,0:T(8,128)(2,1)S(1)}, u32[]{:S(2)}, u32[]{:S(2)}) collective-permute-start(bf16[2,2,2,4,16,128]{5,4,3,2,1,0:T(8,128)(2,1)} %get-tuple-element.23), channel_id=1, source_target_pairs={{0,112},{8,120},{16,96},{24,104},{32,16},{40,24},{48,0},{56,8},{64... | collective-permute-start | bytes 393224 | tf_op jit(solution)/shard_map/ppermute | solution.py:373
  19.6 7.2 %collective-permute-start.4 = (bf16[2,2,2,4,16,128]{5,4,3,2,1,0:T(8,128)(2,1)}, bf16[2,2,2,4,16,128]{5,4,3,2,1,0:T(8,128)(2,1)S(1)}, u32[]{:S(2)}, u32[]{:S(2)}) collective-permute-start(bf16[2,2,2,4,16,128]{5,4,3,2,1,0:T(8,128)(2,1)} %get-tuple-element.24), channel_id=1, source_target_pairs={{0,64},{8,72},{16,80},{24,88},{32,96},{40,104},{48,112},{56,120},{... | collective-permute-start | bytes 393224 | tf_op jit(solution)/shard_map/ppermute | solution.py:373
  19.6 8.4 %collective-permute-start.5 = (bf16[2,2,2,4,16,128]{5,4,3,2,1,0:T(8,128)(2,1)}, bf16[2,2,2,4,16,128]{5,4,3,2,1,0:T(8,128)(2,1)S(1)}, u32[]{:S(2)}, u32[]{:S(2)}) collective-permute-start(bf16[2,2,2,4,16,128]{5,4,3,2,1,0:T(8,128)(2,1)} %get-tuple-element.25), channel_id=1, source_target_pairs={{0,32},{8,40},{16,48},{24,56},{32,64},{40,72},{48,80},{56,88},{64,... | collective-permute-start | bytes 393224 | tf_op jit(solution)/shard_map/ppermute | solution.py:373
  20.4 8.2 %collective-permute-start.6 = (bf16[2,2,2,4,16,128]{5,4,3,2,1,0:T(8,128)(2,1)}, bf16[2,2,2,4,16,128]{5,4,3,2,1,0:T(8,128)(2,1)S(1)}, u32[]{:S(2)}, u32[]{:S(2)}) collective-permute-start(bf16[2,2,2,4,16,128]{5,4,3,2,1,0:T(8,128)(2,1)} %get-tuple-element.26), channel_id=1, source_target_pairs={{0,96},{8,104},{16,112},{24,120},{32,0},{40,8},{48,16},{56,24},{64... | collective-permute-start | bytes 393224 | tf_op jit(solution)/shard_map/ppermute | solution.py:373
  26.3 4.2 %copy-start.8 = (bf16[2,2,2,4,16,128]{5,4,3,2,1,0:T(8,128)(2,1)}, bf16[2,2,2,4,16,128]{5,4,3,2,1,0:T(8,128)(2,1)S(1)}, u32[]{:S(2)}) copy-start(bf16[2,2,2,4,16,128]{5,4,3,2,1,0:T(8,128)(2,1)S(1)} %collective-permute-done.3.refs_4_) | copy-start | bytes 393220
  26.8 3.7 %copy-start.10 = (bf16[2,2,2,4,16,128]{5,4,3,2,1,0:T(8,128)(2,1)}, bf16[2,2,2,4,16,128]{5,4,3,2,1,0:T(8,128)(2,1)S(1)}, u32[]{:S(2)}) copy-start(bf16[2,2,2,4,16,128]{5,4,3,2,1,0:T(8,128)(2,1)S(1)} %collective-permute-done.4.refs_5_) | copy-start | bytes 393220
  28.1 2.4 %copy-start.12 = (bf16[2,2,2,4,16,128]{5,4,3,2,1,0:T(8,128)(2,1)}, bf16[2,2,2,4,16,128]{5,4,3,2,1,0:T(8,128)(2,1)S(1)}, u32[]{:S(2)}) copy-start(bf16[2,2,2,4,16,128]{5,4,3,2,1,0:T(8,128)(2,1)S(1)} %collective-permute-done.5.refs_6_) | copy-start | bytes 393220
  28.6 1.9 %copy-start.14 = (bf16[2,2,2,4,16,128]{5,4,3,2,1,0:T(8,128)(2,1)}, bf16[2,2,2,4,16,128]{5,4,3,2,1,0:T(8,128)(2,1)S(1)}, u32[]{:S(2)}) copy-start(bf16[2,2,2,4,16,128]{5,4,3,2,1,0:T(8,128)(2,1)S(1)} %collective-permute-done.6.refs_7_) | copy-start | bytes 393220
  28.6 1.0 copy-start.6
  30.5 13.1 %collective-permute-start.7 = (bf16[8,2,2,4,16,128]{5,4,3,2,1,0:T(8,128)(2,1)}, bf16[8,2,2,4,16,128]{5,4,3,2,1,0:T(8,128)(2,1)}, u32[]{:S(2)}, u32[]{:S(2)}) collective-permute-start(bf16[8,2,2,4,16,128]{5,4,3,2,1,0:T(8,128)(2,1)} %get-tuple-element.28), channel_id=1, source_target_pairs={{0,8},{8,0},{16,24},{24,16},{32,40},{40,32},{48,56},{56,48},{64,72... | collective-permute-start | bytes 1572872 | tf_op jit(solution)/shard_map/ppermute | solution.py:378
  30.6 1.0 %copy-start.16 = (f32[2,56,1024]{2,1,0:T(8,128)S(1)}, f32[2,56,1024]{2,1,0:T(8,128)}, u32[]{:S(2)}) copy-start(f32[2,56,1024]{2,1,0:T(8,128)} %constant.17.clone.turn_ref) | copy-start | bytes 1376260
  33.2 10.4 %copy-start.7 = (bf16[2,2,2,4,16,128]{5,4,3,2,1,0:T(8,128)(2,1)S(1)}, bf16[2,2,2,4,16,128]{5,4,3,2,1,0:T(8,128)(2,1)}, u32[]{:S(2)}) copy-start(bf16[2,2,2,4,16,128]{5,4,3,2,1,0:T(8,128)(2,1)} %get-tuple-element.19.refs_0_) | copy-start | bytes 393220
  33.2 10.4 %copy-start.9 = (bf16[2,2,2,4,16,128]{5,4,3,2,1,0:T(8,128)(2,1)S(1)}, bf16[2,2,2,4,16,128]{5,4,3,2,1,0:T(8,128)(2,1)}, u32[]{:S(2)}) copy-start(bf16[2,2,2,4,16,128]{5,4,3,2,1,0:T(8,128)(2,1)} %copy-done.8) | copy-start | bytes 393220
  33.2 10.4 %copy-start.11 = (bf16[2,2,2,4,16,128]{5,4,3,2,1,0:T(8,128)(2,1)S(1)}, bf16[2,2,2,4,16,128]{5,4,3,2,1,0:T(8,128)(2,1)}, u32[]{:S(2)}) copy-start(bf16[2,2,2,4,16,128]{5,4,3,2,1,0:T(8,128)(2,1)} %copy-done.10) | copy-start | bytes 393220
  33.3 10.4 %copy-start.13 = (bf16[2,2,2,4,16,128]{5,4,3,2,1,0:T(8,128)(2,1)S(1)}, bf16[2,2,2,4,16,128]{5,4,3,2,1,0:T(8,128)(2,1)}, u32[]{:S(2)}) copy-start(bf16[2,2,2,4,16,128]{5,4,3,2,1,0:T(8,128)(2,1)} %copy-done.12) | copy-start | bytes 393220
  33.3 19.7 %all-to-all-start.1 = ((bf16[8,2,4,32,128]{4,3,2,1,0:T(8,128)(2,1)}), bf16[8,2,4,32,128]{4,3,2,1,0:T(8,128)(2,1)}, u32[]{:S(2)}, u32[]{:S(2)}) async-start(bf16[8,2,4,32,128]{4,3,2,1,0:T(8,128)(2,1)} %shard_map.138), calls=%async_computation.1 | async-start | bytes 1048576 | tf_op jit(solution)/shard_map/all_to_all | solution.py:396
  43.7 1.0 %copy-start.1 = (f32[4,256,128]{2,1,0:T(8,128)S(1)}, f32[4,256,128]{2,1,0:T(8,128)}, u32[]{:S(2)}) copy-start(f32[4,256,128]{2,1,0:T(8,128)} %get-tuple-element.29.refs_9_.weight_ref) | copy-start | bytes 1572868
  44.7 0.9 copy-start.15
  47.4 9.5 %copy-start = (bf16[4,2,256,512]{3,2,1,0:T(8,128)(2,1)S(1)}, bf16[4,2,256,512]{3,2,1,0:T(8,128)(2,1)}, u32[]{:S(2)}) copy-start(bf16[4,2,256,512]{3,2,1,0:T(8,128)(2,1)} %constant.20.clone.third_ref) | copy-start | bytes 6291460
  52.9 1.0 %copy-start.4 = (bf16[256,1024]{1,0:T(8,128)(2,1)S(1)}, bf16[256,1024]{1,0:T(8,128)(2,1)}, u32[]{:S(2)}) copy-start(bf16[256,1024]{1,0:T(8,128)(2,1)} %constant.18.clone.table_ref) | copy-start | bytes 1572868
  54.0 0.9 copy-start.17
  54.9 2.0 %copy-start.2 = (f32[4,256,128]{2,1,0:T(8,128)S(1)}, f32[4,256,128]{2,1,0:T(8,128)}, u32[]{:S(2)}) copy-start(f32[4,256,128]{2,1,0:T(8,128)} %get-tuple-element.29.refs_9_.weight_ref) | copy-start | bytes 1572868
  56.8 2.7 %collective-permute-start.8 = (f32[2,1024,128]{2,1,0:T(8,128)S(1)}, f32[2,1024,128]{2,1,0:T(8,128)S(1)}, u32[]{:S(2)}, u32[]{:S(2)}) collective-permute-start(f32[2,1024,128]{2,1,0:T(8,128)S(1)} %shard_map.141.spec), channel_id=1, source_target_pairs={{0,8},{8,0},{16,24},{24,16},{32,40},{40,32},{48,56},{56,48},{64,72... | collective-permute-start | bytes 3145736 | tf_op jit(solution)/shard_map/ppermute | solution.py:401
  56.9 1.2 %copy-start.3 = (f32[2,1024,128]{2,1,0:T(8,128)S(1)}, f32[2,1024,128]{2,1,0:T(8,128)}, u32[]{:S(2)}) copy-start(f32[2,1024,128]{2,1,0:T(8,128)} %get-tuple-element.30.twist) | copy-start | bytes 3145732
  60.7 32.2 %copy-start.18 = (bf16[4,2,256,256]{3,2,1,0:T(8,128)(2,1)S(1)}, bf16[4,2,256,256]{3,2,1,0:T(8,128)(2,1)}, u32[]{:S(2)}) copy-start(bf16[4,2,256,256]{3,2,1,0:T(8,128)(2,1)} %constant.23.clone.table_ref) | copy-start | bytes 3145732

commit v5 on v4

--- a/solution.py
+++ b/solution.py
@@ -16,7 +16,7 @@
 SMEM = pl.BlockSpec(memory_space=pltpu.SMEM)
 ANY = pl.BlockSpec(memory_space=pl.ANY)
 MIB = 1 << 20
-OFFSETS = [(0, 0), (1, 0), (1, 2), (1, 1), (1, 3), (0, 2), (0, 1), (0, 3)]
+OFFSETS = [(0, 0), (1, 0), (1, 2), (0, 2), (0, 1), (1, 1), (1, 3), (0, 3)]
 
 
 def phases(product, count):
@@ -35,22 +35,25 @@
 def tables():
     q = np.arange(256)
     c, s = phases(q[:, None] * q[None, :], 256)
-    first = np.stack(split_hi_lo(np.concatenate([c, -s], axis=1)))
+    hi, lo = split_hi_lo(np.concatenate([c, -s], axis=1))
+    first = np.concatenate([hi, lo], axis=1).astype(np.float32)
     k2 = np.arange(1024)
     rows = np.concatenate([4 * np.arange(32), 128 * np.arange(8), np.arange(8), 1024 * np.arange(8)])
     c, s = phases(rows[:, None] * k2[None, :], NSAMP)
-    turn = np.stack([c, -s]).astype(np.float32)
+    turn = np.concatenate([c, -s]).astype(np.float32)
+    first = np.concatenate([first, turn], axis=0)
     c, s = phases(q[:, None] * q[None, :], 256)
     (ch, cl), (sh, sl) = split_hi_lo(c), split_hi_lo(s)
     second = np.concatenate([ch, sh, cl, sl], axis=1)
     c, s = phases(q[:, None] * np.arange(4)[None, :], 1024)
     lag = np.zeros((256, 128), np.float32)
     lag[:, 0:8:2], lag[:, 1:8:2] = c, -s
+    second = np.concatenate([second.astype(np.float32), lag], axis=1)
     third = []
     for p in range(4):
         c, s = phases(q[:, None] * (4 * q[None, :] + p), 1024)
         c, s = c.astype(np.float32), s.astype(np.float32)
-        third.append(np.stack([np.concatenate([c, -s], 1), np.concatenate([s, c], 1)]))
+        third.append(np.concatenate([c, s], 1))
     n1 = np.arange(1024)
     c, s = phases(n1[:, None] * np.arange(128)[None, :], NSAMP)
     back = np.stack([c, s]).astype(np.float32)
@@ -62,9 +65,7 @@
         last.append(np.stack([c, s]).astype(np.float32))
     return dict(
         first=first,
-        turn=turn,
         second=second,
-        lag=lag,
         third=np.stack(third).astype(jnp.bfloat16),
         back=back,
         shift=shift,
@@ -86,10 +87,11 @@
 
 
 def gate_kernel(
-    strain_ref, start_any, span_any, assign_any, bank_any, out_ref, *rest
+    strain_ref, start_any, span_any, assign_any, bank_any, asd_any, back_any, shift_any,
+    out_ref, weight_ref, twist_ref, *rest
 ):
     pick_refs, rest = rest[:8], rest[8:]
-    strain, bank_ref, start_ref, span_ref, assign_ref, sems = rest
+    strain, bank_ref, start_ref, span_ref, assign_ref, asd_ref, back_ref, shift_ref, sems = rest
     x, z, core = place()
     copies = [
         pltpu.make_async_copy(start_any, start_ref, sems.at[0]),
@@ -97,6 +99,9 @@
         pltpu.make_async_copy(strain_ref.at[core], strain, sems.at[2]),
         pltpu.make_async_copy(assign_any, assign_ref, sems.at[3]),
         pltpu.make_async_copy(bank_any, bank_ref, sems.at[4]),
+        pltpu.make_async_copy(asd_any, asd_ref, sems.at[5]),
+        pltpu.make_async_copy(back_any, back_ref, sems.at[6]),
+        pltpu.make_async_copy(shift_any, shift_ref, sems.at[7]),
     ]
     for copy in copies:
         copy.start()
@@ -133,22 +138,12 @@
                     value = bank_ref[part, chosen, pl.ds(p, 16, stride=4), :].astype(BF)
                     pick_refs[i // 2][rc, slot, part, p] = value
 
-
-def prepare_kernel(asd_any, back_any, shift_any, weight_ref, twist_ref, asd_ref, back_ref, shift_ref, sems):
-    copies = [
-        pltpu.make_async_copy(asd_any, asd_ref, sems.at[0]),
-        pltpu.make_async_copy(back_any, back_ref, sems.at[1]),
-        pltpu.make_async_copy(shift_any, shift_ref, sems.at[2]),
-    ]
-    for copy in copies:
-        copy.start()
-    copies[0].wait()
+    for copy in copies[5:]:
+        copy.wait()
     for p in range(4):
         asd = asd_ref[pl.ds(p, 256, stride=4), :]
         weight_ref[p] = 1.0 / (asd * asd)
-    copies[1].wait()
-    copies[2].wait()
-    own = lax.broadcasted_iota(jnp.int32, (128, 128), 1) == lax.axis_index("seg")
+    own = lane == lax.axis_index("seg")
     for i in range(8):
         rows = slice(128 * i, 128 * i + 128)
         shift = [jnp.sum(jnp.where(own, shift_ref[part, rows, :], 0.0), axis=1, keepdims=True) for part in range(2)]
@@ -158,9 +153,8 @@
 
 
 def pack_kernel(*refs):
-    piece_refs, out_ref, token_ref, sems = refs[:8], *refs[8:]
-    token_ref[...] = jnp.zeros_like(token_ref)
-    copies = [pltpu.make_async_copy(piece_refs[i].at[1], out_ref.at[i], sems.at[i]) for i in range(8)]
+    piece_refs, out_refs, sems = refs[:8], refs[9:13], refs[13]
+    copies = [pltpu.make_async_copy(piece_refs[i].at[1], out_refs[i // 2].at[i % 2], sems.at[i]) for i in range(8)]
     for copy in copies:
         copy.start()
     for copy in copies:
@@ -180,10 +174,12 @@
     return ((sr + ur, si + ui), (tr + wr, ti + wi), (sr - ur, si - ui), (tr - wr, ti - wi))
 
 
-def first_kernel(cols_ref, table_ref, turn_ref, after_ref, out_ref, z_ref):
-    del after_ref
+def first_kernel(cols_ref, table_ref, *refs):
+    out_ref, token_ref, z_ref = refs[-3:]
+    token_ref[...] = jnp.zeros_like(token_ref)
+    turn_ref = table_ref.at[256:368].reshape(2, 56, 1024)
     turned = jnp.concatenate([cols_ref[:, 32 * r : 32 * r + 32, :].reshape(256, 128).T for r in range(4)], axis=0)
-    z_ref[...] = dot(turned, table_ref[0]) + dot(turned, table_ref[1])
+    z_ref[...] = dot(turned, table_ref[:256, :512].astype(BF)) + dot(turned, table_ref[:256, 512:].astype(BF))
     seg = 32 + lax.axis_index("seg")
     seg_re, seg_im = turn_ref[0, pl.ds(seg, 1), :], turn_ref[1, pl.ds(seg, 1), :]
     for r1 in range(4):
@@ -213,18 +209,20 @@
                         out_ref[2 * k + half, part, r1, at] = done[part][:, 128 * half : 128 * half + 128]
 
 
-def second_kernel(own_ref, table_ref, lag_ref, after_ref, spec_ref, z_ref):
+def second_kernel(own_ref, table_ref, after_ref, spec_ref, z_ref):
     del after_ref
+    hi, lo = table_ref[:, :512].astype(BF), table_ref[:, 512:1024].astype(BF)
     for r in range(4):
         re = own_ref[:, 0, r].reshape(256, 128)
         im = own_ref[:, 1, r].reshape(256, 128)
         right = jnp.concatenate([jnp.concatenate([re, im], axis=1), jnp.concatenate([im, -re], axis=1)], axis=0)
-        z_ref[r] = dot(table_ref[:, :512], right) + dot(table_ref[:, 512:], right)
+        z_ref[r] = dot(hi, right) + dot(lo, right)
     for i in range(8):
         rows = slice(32 * i, 32 * i + 32)
         sums = [(z_ref[0, rows, :128], z_ref[0, rows, 128:])]
         for r in range(1, 4):
-            pr, pi = lag_ref[rows, 2 * r : 2 * r + 1], lag_ref[rows, 2 * r + 1 : 2 * r + 2]
+            at = 1024 + 2 * r
+            pr, pi = table_ref[rows, at : at + 1], table_ref[rows, at + 1 : at + 2]
             re, im = z_ref[r, rows, :128], z_ref[r, rows, 128:]
             sums.append((re * pr - im * pi, re * pi + im * pr))
         for k, parts in enumerate(four_way(-1, sums)):
@@ -233,12 +231,12 @@
 
 
 def assemble_kernel(*refs):
-    piece_refs, cross_ref, _, bank, sems = refs[:8], *refs[8:]
+    piece_refs, cross_refs, bank, sems = refs[:8], refs[8:12], *refs[12:]
     x, z, core = place()
     copies = []
     for i, (rz, rx) in enumerate(OFFSETS):
         for rc in range(2):
-            src = piece_refs[i].at[0] if rc == 0 else cross_ref.at[i]
+            src = piece_refs[i].at[0] if rc == 0 else cross_refs[i // 2].at[i % 2]
             origin = ((x + 4 - rx) % 4) * 4 + (z + rz) % 2 * 2 + (core + rc) % 2
             copies.append(pltpu.make_async_copy(src, bank.at[origin], sems.at[len(copies)]))
     for copy in copies:
@@ -261,9 +259,9 @@
                 norms[slot] = norms[slot] + power.reshape(32, 8, 128).sum(axis=0)
             lanes_re.append((sr * hr + si * hi).astype(BF))
             lanes_im.append((si * hr - sr * hi).astype(BF))
-        right = jnp.concatenate([jnp.concatenate(lanes_re, axis=1), jnp.concatenate(lanes_im, axis=1)], axis=0)
-        v_ref[p, 0] = dot(third_ref[p, 0], right)
-        v_ref[p, 1] = dot(third_ref[p, 1], right)
+        re, im = jnp.concatenate(lanes_re, axis=1), jnp.concatenate(lanes_im, axis=1)
+        v_ref[p, 0] = dot(third_ref[p], jnp.concatenate([re, -im], axis=0))
+        v_ref[p, 1] = dot(third_ref[p], jnp.concatenate([im, re], axis=0))
     for i in range(8):
         rows = slice(32 * i, 32 * i + 32)
         half, inside = i // 4, (i % 4) * 32
@@ -356,12 +354,17 @@
     swap_core = [(i, i ^ 1) for i in range(16)]
 
     blk = (2, 2, 4, 16, 128)
-    gated, *picked = call(
-        gate_kernel, (strain, gate_start, gate_span, assign, bank), (shape(8, 128, 128), *[shape(2, *blk)] * 8),
-        [ANY] * 5, 10**8, 4 * MIB,
+    gated, weight, twist, *picked = call(
+        gate_kernel, (strain, gate_start, gate_span, assign, bank, asd, const["back"], const["shift"]),
+        (
+            shape(8, 128, 128), shape(4, 256, 128, dtype=F32), shape(2, 1024, 128, dtype=F32),
+            *[shape(2, *blk)] * 8,
+        ),
+        [ANY] * 8, 10**8, 4 * MIB,
         [
             pltpu.VMEM((128, 1024), F32), pltpu.VMEM((2, 32, 64, 128), F32), pltpu.SMEM((2, 1, 2), jnp.int32),
-            pltpu.SMEM((2, 1, 2), jnp.int32), pltpu.SMEM((32,), jnp.int32), pltpu.SemaphoreType.DMA((5,)),
+            pltpu.SMEM((2, 1, 2), jnp.int32), pltpu.SMEM((32,), jnp.int32), pltpu.VMEM((1024, 128), F32),
+            pltpu.VMEM((2, 1024, 128), F32), pltpu.VMEM((2, 1024, 128), F32), pltpu.SemaphoreType.DMA((8,)),
         ],
         limit=63,
     )
@@ -371,32 +374,23 @@
     for (rz, rx), send in zip(OFFSETS[1:], picked[1:]):
         hop = [(i, (i // 4 + rx) % 4 * 4 + i % 4 ^ 2 * rz) for i in range(16)]
         pieces.append(lax.ppermute(send, "tmpl", hop))
-    cross, token = call(
-        pack_kernel, pieces, (shape(8, *blk), shape(8, 128, dtype=F32)), [ANY] * 8, 1, 10 * MIB,
-        [pltpu.SemaphoreType.DMA((8,))], limit=8, space=(ANY, VMEM),
-    )
-    crossed = lax.ppermute(cross, "tmpl", swap_core)
-    weight, twist = call(
-        prepare_kernel, (asd, const["back"], const["shift"]),
-        (shape(4, 256, 128, dtype=F32), shape(2, 1024, 128, dtype=F32)), [ANY] * 3, 1, 10 * MIB,
-        [
-            pltpu.VMEM((1024, 128), F32), pltpu.VMEM((2, 1024, 128), F32), pltpu.VMEM((2, 1024, 128), F32),
-            pltpu.SemaphoreType.DMA((3,)),
-        ],
-        limit=63,
-    )
+    turned, token = call(
+        first_kernel, (columns, const["first"], *pieces[1:4]), (shape(8, 2, 4, 32, 128), shape(8, 128, dtype=F32)),
+        [VMEM] * 2 + [ANY] * 3, 3 * 10**8, 4 * MIB, [pltpu.VMEM((512, 512), F32)],
+    )
+    crosses = call(
+        pack_kernel, (*pieces, token), (shape(2, *blk),) * 4, [ANY] * 9, 1, MIB, [pltpu.SemaphoreType.DMA((8,))],
+        limit=8, space=(ANY,) * 4,
+    )
+    crossed = [lax.ppermute(cross, "tmpl", swap_core) for cross in crosses]
     ordered = call(
-        assemble_kernel, (*pieces, crossed, weight), shape(16, *blk), [ANY] * 10, 1, 10 * MIB,
+        assemble_kernel, (*pieces, *crossed), shape(16, *blk), [ANY] * 12, 1, 10 * MIB,
         [pltpu.SemaphoreType.DMA((16,))], limit=8,
-    )
-    turned = call(
-        first_kernel, (columns, const["first"], const["turn"], token),
-        shape(8, 2, 4, 32, 128), [VMEM] * 3 + [ANY], 3 * 10**8, 4 * MIB, [pltpu.VMEM((512, 512), F32)],
     )
     own = lax.all_to_all(turned, "seg", 0, 0)
     spec = call(
-        second_kernel, (own, const["second"], const["lag"], ordered), shape(2, 1024, 128, dtype=F32),
-        [VMEM] * 3 + [ANY], 1, 1, [pltpu.VMEM((4, 256, 256), F32)],
+        second_kernel, (own, const["second"], ordered), shape(2, 1024, 128, dtype=F32),
+        [VMEM] * 2 + [ANY], 1, 1, [pltpu.VMEM((4, 256, 256), F32)],
     )
     other_spec = lax.ppermute(spec, "tmpl", swap_core)
     half = call(

time: 97.5 us -> 95.1 us (0.975)
  local copies, waits for them, and re-layouts: 7.12 us -> 1.86 us
  waiting for transfers between devices: 11.5 us -> 15.1 us
  Pallas kernels: 17.9 us -> 14.6 us
  blocking collectives: 32.2 us -> 34.7 us
    ppermute x7, waiting for transfers between devices: 5.77 us -> 13.3 us  [per_device(): pieces.append(lax.ppermute(send, 'tmpl', hop))]
    all_to_all x1, waiting for transfers between devices: 5.51 us -> 0.01 us  [per_device(): own = lax.all_to_all(turned, 'seg', 0, 0)]
    unnamed x38 -> x22, local copies, waits for them, and re-layouts: 7.12 us -> 1.86 us
    pallas_call x9 -> x8, Pallas kernels: 17.9 us -> 14.6 us  [call(): pl.pallas_call(kernel, out_shape=outs, in_specs=specs, out_specs=space if...]
    all_to_all x1, blocking collectives: 32.2 us -> 34.7 us  [per_device(): series = lax.all_to_all(inner, 'seg', 0, 0)]
    ppermute x1 -> x4, waiting for transfers between devices: 0.01 us -> 1.02 us  [per_device(): crossed = [lax.ppermute(cross, 'tmpl', swap_core) for cross in crosses]]
    ppermute x1 -> x4, starting transfers between devices: 0.09 us -> 1.09 us  [per_device(): crossed = [lax.ppermute(cross, 'tmpl', swap_core) for cross in crosses]]
  transfers between devices with their start and end apart: 11 -> 14, of which waited for: 7 -> 11; matrix products, arithmetic and copies ran while one was open for 0% -> 0% of each run, Pallas kernels for 9% -> 4%
where the time goes in v5:
time: 95.1 us; the launch traced here: 94.3 us
  blocking collectives  34.7 us (36%)
  starting transfers between devices  27.9 us (29%)
  waiting for transfers between devices  15.1 us (16%)
  Pallas kernels  14.6 us (15%)
  local copies, waits for them, and re-layouts  1.86 us (2%)
    all_to_all x1, blocking collectives, per_device(): series = lax.all_to_all(inner, 'seg', 0, 0)  34.7 us
    pallas_call x8, Pallas kernels, call(): pl.pallas_call(kernel, out_shape=outs, in_specs=specs, out_specs=space if...  14.6 us
    ppermute x7, waiting for transfers between devices, per_device(): pieces.append(lax.ppermute(send, 'tmpl', hop))  13.3 us
    ppermute x7, starting transfers between devices, per_device(): pieces.append(lax.ppermute(send, 'tmpl', hop))  11.2 us
    all_to_all x1, starting transfers between devices, per_device(): columns = lax.all_to_all(gated, 'seg', 0, 0)  8.01 us
    all_to_all x1, starting transfers between devices, per_device(): own = lax.all_to_all(turned, 'seg', 0, 0)  7.21 us
  transfers between devices with their start and end apart: 14, of which 11 were waited for; matrix products, arithmetic and copies ran while one was open for 0% of the time, Pallas kernels for 4%

profile of v5, /device:TPU:0, one launch (start us, length us, event | category | flops | bytes accessed | tf_op | source)
XLA Modules:
  0.0 94.3 jit_solution(13807590454300578700)
XLA Ops:
  0.0 4.2 %shard_map.118 = (bf16[8,128,128]{2,1,0:T(8,128)(2,1)}, f32[4,256,128]{2,1,0:T(8,128)}, f32[2,1024,128]{2,1,0:T(8,128)}, bf16[2,2,2,4,16,128]{5,4,3,2,1,0:T(8,12...) custom-call(f32[2,128,1024]{2,1,0:T(8,128)} %strain_ref.1, ...), custom_call_target="tpu_custom_call" | custom-call | flops 100000000 | bytes 4194304 | tf_op jit(solution)/shard_map/pallas_call | solution.py:337
  4.2 8.0 %all-to-all-start = ((bf16[8,128,128]{2,1,0:T(8,128)(2,1)}), bf16[8,128,128]{2,1,0:T(8,128)(2,1)S(1)}, u32[]{:S(2)}, u32[]{:S(2)}) async-start(bf16[8,128,128]{2,1,0:T(8,128)(2,1)} %get-tuple-element.22), calls=%async_computation | async-start | bytes 524288 | tf_op jit(solution)/shard_map/all_to_all | solution.py:371
  12.2 1.0 %collective-permute-start = (bf16[2,2,2,4,16,128]{5,4,3,2,1,0:T(8,128)(2,1)}, bf16[2,2,2,4,16,128]{5,4,3,2,1,0:T(8,128)(2,1)S(1)}, u32[]{:S(2)}, u32[]{:S(2)}) collective-permute-start(bf16[2,2,2,4,16,128]{5,4,3,2,1,0:T(8,128)(2,1)} %get-tuple-element.23), channel_id=1, source_target_pairs={{0,16},{8,24},{16,0},{24,8},{32,48},{40,56},{48,32},{56,40},{64,80... | collective-permute-start | bytes 393224 | tf_op jit(solution)/shard_map/ppermute | solution.py:376
  13.2 3.5 %collective-permute-start.1 = (bf16[2,2,2,4,16,128]{5,4,3,2,1,0:T(8,128)(2,1)}, bf16[2,2,2,4,16,128]{5,4,3,2,1,0:T(8,128)(2,1)S(1)}, u32[]{:S(2)}, u32[]{:S(2)}) collective-permute-start(bf16[2,2,2,4,16,128]{5,4,3,2,1,0:T(8,128)(2,1)} %get-tuple-element.24), channel_id=1, source_target_pairs={{0,80},{8,88},{16,64},{24,72},{32,112},{40,120},{48,96},{56,104},{... | collective-permute-start | bytes 393224 | tf_op jit(solution)/shard_map/ppermute | solution.py:376
  16.7 0.5 collective-permute-start.2
  17.2 5.4 %collective-permute-done.refs_0_.refs_1_ = bf16[2,2,2,4,16,128]{5,4,3,2,1,0:T(8,128)(2,1)S(1)} collective-permute-done((bf16[2,2,2,4,16,128]{5,4,3,2,1,0:T(8,128)(2,1)}, bf16[2,2,2,4,16,128]{5,4,3,2,1,0:T(8,128)(2,1)S(1)}, u32[]{:S(2)}, u32[]{:S(2)}) %collective-permute-start) | collective-permute-done | bytes 131104 | tf_op jit(solution)/shard_map/ppermute | solution.py:376
  22.7 0.7 collective-permute-done.2.refs_2_.refs_3_
  23.4 1.4 %copy-done = f32[368,1024]{1,0:T(8,128)S(1)} copy-done((f32[368,1024]{1,0:T(8,128)S(1)}, f32[368,1024]{1,0:T(8,128)}, u32[]{:S(2)}) %copy-start) | copy-done | bytes 1507352
  24.8 1.6 %shard_map.119 = (bf16[8,2,4,32,128]{4,3,2,1,0:T(8,128)(2,1)}, f32[8,128]{1,0:T(8,128)S(1)}) custom-call(bf16[8,128,128]{2,1,0:T(8,128)(2,1)S(1)} %all-to-all-done.cols_ref, f32[368,1024]{1,0:T(8,128)S(1)} %copy-done, bf16[2,2,2,4,16,128]{5,4,3,2,1,0:T(8,128)(2,1)S(1)} %collective-permute-done.refs_0_.refs_1_, ...), custom_call_target="tpu_custom_call" | custom-call | flops 300000000 | bytes 4194304 | tf_op jit(solution)/shard_map/pallas_call | solution.py:337
  26.4 7.2 %all-to-all-start.1 = ((bf16[8,2,4,32,128]{4,3,2,1,0:T(8,128)(2,1)}), bf16[8,2,4,32,128]{4,3,2,1,0:T(8,128)(2,1)S(1)}, u32[]{:S(2)}, u32[]{:S(2)}) async-start(bf16[8,2,4,32,128]{4,3,2,1,0:T(8,128)(2,1)} %get-tuple-element.26), calls=%async_computation.1 | async-start | bytes 1048576 | tf_op jit(solution)/shard_map/all_to_all | solution.py:390
  33.6 1.2 %collective-permute-start.3 = (bf16[2,2,2,4,16,128]{5,4,3,2,1,0:T(8,128)(2,1)S(1)}, bf16[2,2,2,4,16,128]{5,4,3,2,1,0:T(8,128)(2,1)S(1)}, u32[]{:S(2)}, u32[]{:S(2)}) collective-permute-start(bf16[2,2,2,4,16,128]{5,4,3,2,1,0:T(8,128)(2,1)S(1)} %copy-done.10), channel_id=1, source_target_pairs={{0,32},{8,40},{16,48},{24,56},{32,64},{40,72},{48,80},{56,88},{64,... | collective-permute-start | bytes 393224 | tf_op jit(solution)/shard_map/ppermute | solution.py:376
  34.8 1.6 %collective-permute-start.4 = (bf16[2,2,2,4,16,128]{5,4,3,2,1,0:T(8,128)(2,1)S(1)}, bf16[2,2,2,4,16,128]{5,4,3,2,1,0:T(8,128)(2,1)S(1)}, u32[]{:S(2)}, u32[]{:S(2)}) collective-permute-start(bf16[2,2,2,4,16,128]{5,4,3,2,1,0:T(8,128)(2,1)S(1)} %copy-done.9), channel_id=1, source_target_pairs={{0,48},{8,56},{16,32},{24,40},{32,80},{40,88},{48,64},{56,72},{64,... | collective-permute-start | bytes 393224 | tf_op jit(solution)/shard_map/ppermute | solution.py:376
  36.4 2.6 %collective-permute-start.5 = (bf16[2,2,2,4,16,128]{5,4,3,2,1,0:T(8,128)(2,1)S(1)}, bf16[2,2,2,4,16,128]{5,4,3,2,1,0:T(8,128)(2,1)S(1)}, u32[]{:S(2)}, u32[]{:S(2)}) collective-permute-start(bf16[2,2,2,4,16,128]{5,4,3,2,1,0:T(8,128)(2,1)S(1)} %copy-done.8), channel_id=1, source_target_pairs={{0,112},{8,120},{16,96},{24,104},{32,16},{40,24},{48,0},{56,8},{64... | collective-permute-start | bytes 393224 | tf_op jit(solution)/shard_map/ppermute | solution.py:376
  39.0 0.9 collective-permute-start.6
  39.8 0.5 collective-permute-done.3.refs_4_
  40.3 5.1 %collective-permute-done.4.refs_5_ = bf16[2,2,2,4,16,128]{5,4,3,2,1,0:T(8,128)(2,1)S(1)} collective-permute-done((bf16[2,2,2,4,16,128]{5,4,3,2,1,0:T(8,128)(2,1)S(1)}, bf16[2,2,2,4,16,128]{5,4,3,2,1,0:T(8,128)(2,1)S(1)}, u32[]{:S(2)}, u32[]{:S(2)}) %collective-permute-start.4) | collective-permute-done | bytes 131104 | tf_op jit(solution)/shard_map/ppermute | solution.py:376
  45.4 0.7 collective-permute-done.5.refs_6_
  46.2 0.7 collective-permute-done.6.refs_7_
  46.9 0.7 shard_map.120
  47.8 0.5 collective-permute-start.8
  48.4 0.4 collective-permute-start.10
  48.8 0.3 collective-permute-done.7.refs_8_
  49.3 0.3 collective-permute-done.9.refs_10_
  49.8 1.6 %shard_map.121.after_ref.bank = bf16[16,2,2,4,16,128]{5,4,3,2,1,0:T(8,128)(2,1)S(1)} custom-call(bf16[2,2,2,4,16,128]{5,4,3,2,1,0:T(8,128)(2,1)S(1)} %copy-done.4, bf16[2,2,2,4,16,128]{5,4,3,2,1,0:T(8,128)(2,1)S(1)} %collective-permute-done.refs_0_.refs_1_, bf16[2,2,2,4,16,128]{5,4,3,2,1,0:T(8,128)(2,1)S(1)} %collective-permute-done.1.refs_1_.refs_2_, ...), custom_call_target="tpu_custom_call" | custom-call | flops 1 | bytes 10485760 | tf_op jit(solution)/shard_map/pallas_call | solution.py:337
  51.5 0.8 shard_map.122.spec
  52.3 0.4 collective-permute-start.11
  52.7 0.3 copy-done.3
  53.1 1.1 %shard_map.123.half_ref = bf16[8,528,128]{2,1,0:T(8,128)(2,1)S(1)} custom-call(f32[2,1024,128]{2,1,0:T(8,128)S(1)} %shard_map.122.spec, f32[4,256,128]{2,1,0:T(8,128)S(1)} %copy-done.5, bf16[4,256,512]{2,1,0:T(8,128)(2,1)S(1)} %copy-done.2, f32[2,1024,128]{2,1,0:T(8,128)S(1)} %copy-done.3, bf16[16,2,2,4,16,128]{5,4,3,2,1,0:T(8,128)(2,1)S(1)} %shard_map.121.after_ref.bank), custom_call_target="tpu_custom_call" | custom-call | flops 2000000000 | bytes 10485760 | tf_op jit(solution)/shard_map/pallas_call | solution.py:337
  54.3 0.8 collective-permute-done.11.spec
  55.1 1.1 %shard_map.124 = bf16[8,1040,128]{2,1,0:T(8,128)(2,1)S(1)} custom-call(f32[2,1024,128]{2,1,0:T(8,128)S(1)} %collective-permute-done.11.spec, f32[4,256,128]{2,1,0:T(8,128)S(1)} %copy-done.5, bf16[4,256,512]{2,1,0:T(8,128)(2,1)S(1)} %copy-done.2, f32[2,1024,128]{2,1,0:T(8,128)S(1)} %copy-done.3, ...), custom_call_target="tpu_custom_call" | custom-call | flops 2000000000 | bytes 10485760 | tf_op jit(solution)/shard_map/pallas_call | solution.py:337
  56.2 34.7 %all_to_all.15.in_ref = bf16[8,1040,128]{2,1,0:T(8,128)(2,1)S(1)} all-to-all(bf16[8,1040,128]{2,1,0:T(8,128)(2,1)S(1)} %shard_map.124), channel_id=1, replica_groups=mesh['tmpl'=16,'seg'=8] {'seg'}, dimensions={0} | all-to-all | bytes 4259840 | tf_op jit(solution)/shard_map/all_to_all | solution.py:406
  90.9 3.4 %shard_map.125 = f32[2,2,1024,128]{3,2,1,0:T(8,128)} custom-call(bf16[8,1040,128]{2,1,0:T(8,128)(2,1)S(1)} %all_to_all.15.in_ref, bf16[4,2,256,256]{3,2,1,0:T(8,128)(2,1)S(1)} %copy-done.6), custom_call_target="tpu_custom_call" | custom-call | flops 3000000000 | bytes 6291456 | tf_op jit(solution)/shard_map/pallas_call | solution.py:337
  (27 shorter events, 0.7 us)
Async XLA Ops:
  4.2 30.6 %copy-start.9 = (bf16[2,2,2,4,16,128]{5,4,3,2,1,0:T(8,128)(2,1)S(1)}, bf16[2,2,2,4,16,128]{5,4,3,2,1,0:T(8,128)(2,1)}, u32[]{:S(2)}) copy-start(bf16[2,2,2,4,16,128]{5,4,3,2,1,0:T(8,128)(2,1)} %get-tuple-element.29) | copy-start | bytes 393220
  4.2 32.2 %copy-start.8 = (bf16[2,2,2,4,16,128]{5,4,3,2,1,0:T(8,128)(2,1)S(1)}, bf16[2,2,2,4,16,128]{5,4,3,2,1,0:T(8,128)(2,1)}, u32[]{:S(2)}) copy-start(bf16[2,2,2,4,16,128]{5,4,3,2,1,0:T(8,128)(2,1)} %get-tuple-element.30) | copy-start | bytes 393220
  4.2 34.8 %copy-start.7 = (bf16[2,2,2,4,16,128]{5,4,3,2,1,0:T(8,128)(2,1)S(1)}, bf16[2,2,2,4,16,128]{5,4,3,2,1,0:T(8,128)(2,1)}, u32[]{:S(2)}) copy-start(bf16[2,2,2,4,16,128]{5,4,3,2,1,0:T(8,128)(2,1)} %get-tuple-element.31) | copy-start | bytes 393220
  4.2 42.7 %copy-start.4 = (bf16[2,2,2,4,16,128]{5,4,3,2,1,0:T(8,128)(2,1)S(1)}, bf16[2,2,2,4,16,128]{5,4,3,2,1,0:T(8,128)(2,1)}, u32[]{:S(2)}) copy-start(bf16[2,2,2,4,16,128]{5,4,3,2,1,0:T(8,128)(2,1)} %get-tuple-element.27.refs_0_) | copy-start | bytes 393220
  4.2 19.2 %all-to-all-start = ((bf16[8,128,128]{2,1,0:T(8,128)(2,1)}), bf16[8,128,128]{2,1,0:T(8,128)(2,1)S(1)}, u32[]{:S(2)}, u32[]{:S(2)}) async-start(bf16[8,128,128]{2,1,0:T(8,128)(2,1)} %get-tuple-element.22), calls=%async_computation | async-start | bytes 524288 | tf_op jit(solution)/shard_map/all_to_all | solution.py:371
  12.2 10.4 %collective-permute-start = (bf16[2,2,2,4,16,128]{5,4,3,2,1,0:T(8,128)(2,1)}, bf16[2,2,2,4,16,128]{5,4,3,2,1,0:T(8,128)(2,1)S(1)}, u32[]{:S(2)}, u32[]{:S(2)}) collective-permute-start(bf16[2,2,2,4,16,128]{5,4,3,2,1,0:T(8,128)(2,1)} %get-tuple-element.23), channel_id=1, source_target_pairs={{0,16},{8,24},{16,0},{24,8},{32,48},{40,56},{48,32},{56,40},{64,80... | collective-permute-start | bytes 393224 | tf_op jit(solution)/shard_map/ppermute | solution.py:376
  13.2 9.4 %collective-permute-start.1 = (bf16[2,2,2,4,16,128]{5,4,3,2,1,0:T(8,128)(2,1)}, bf16[2,2,2,4,16,128]{5,4,3,2,1,0:T(8,128)(2,1)S(1)}, u32[]{:S(2)}, u32[]{:S(2)}) collective-permute-start(bf16[2,2,2,4,16,128]{5,4,3,2,1,0:T(8,128)(2,1)} %get-tuple-element.24), channel_id=1, source_target_pairs={{0,80},{8,88},{16,64},{24,72},{32,112},{40,120},{48,96},{56,104},{... | collective-permute-start | bytes 393224 | tf_op jit(solution)/shard_map/ppermute | solution.py:376
  16.7 6.7 %collective-permute-start.2 = (bf16[2,2,2,4,16,128]{5,4,3,2,1,0:T(8,128)(2,1)}, bf16[2,2,2,4,16,128]{5,4,3,2,1,0:T(8,128)(2,1)S(1)}, u32[]{:S(2)}, u32[]{:S(2)}) collective-permute-start(bf16[2,2,2,4,16,128]{5,4,3,2,1,0:T(8,128)(2,1)} %get-tuple-element.25), channel_id=1, source_target_pairs={{0,64},{8,72},{16,80},{24,88},{32,96},{40,104},{48,112},{56,120},{... | collective-permute-start | bytes 393224 | tf_op jit(solution)/shard_map/ppermute | solution.py:376
  23.4 1.4 %copy-start = (f32[368,1024]{1,0:T(8,128)S(1)}, f32[368,1024]{1,0:T(8,128)}, u32[]{:S(2)}) copy-start(f32[368,1024]{1,0:T(8,128)} %constant.12.clone.table_ref) | copy-start | bytes 4521988
  24.8 8.8 %copy-start.10 = (bf16[2,2,2,4,16,128]{5,4,3,2,1,0:T(8,128)(2,1)S(1)}, bf16[2,2,2,4,16,128]{5,4,3,2,1,0:T(8,128)(2,1)}, u32[]{:S(2)}) copy-start(bf16[2,2,2,4,16,128]{5,4,3,2,1,0:T(8,128)(2,1)} %get-tuple-element.28) | copy-start | bytes 393220
  26.4 25.1 %all-to-all-start.1 = ((bf16[8,2,4,32,128]{4,3,2,1,0:T(8,128)(2,1)}), bf16[8,2,4,32,128]{4,3,2,1,0:T(8,128)(2,1)S(1)}, u32[]{:S(2)}, u32[]{:S(2)}) async-start(bf16[8,2,4,32,128]{4,3,2,1,0:T(8,128)(2,1)} %get-tuple-element.26), calls=%async_computation.1 | async-start | bytes 1048576 | tf_op jit(solution)/shard_map/all_to_all | solution.py:390
  33.6 17.9 %copy-start.1 = (f32[256,1152]{1,0:T(8,128)S(1)}, f32[256,1152]{1,0:T(8,128)}, u32[]{:S(2)}) copy-start(f32[256,1152]{1,0:T(8,128)} %constant.13.clone.table_ref) | copy-start | bytes 3538948
  33.6 6.7 %collective-permute-start.3 = (bf16[2,2,2,4,16,128]{5,4,3,2,1,0:T(8,128)(2,1)S(1)}, bf16[2,2,2,4,16,128]{5,4,3,2,1,0:T(8,128)(2,1)S(1)}, u32[]{:S(2)}, u32[]{:S(2)}) collective-permute-start(bf16[2,2,2,4,16,128]{5,4,3,2,1,0:T(8,128)(2,1)S(1)} %copy-done.10), channel_id=1, source_target_pairs={{0,32},{8,40},{16,48},{24,56},{32,64},{40,72},{48,80},{56,88},{64,... | collective-permute-start | bytes 393224 | tf_op jit(solution)/shard_map/ppermute | solution.py:376
  34.8 10.6 %collective-permute-start.4 = (bf16[2,2,2,4,16,128]{5,4,3,2,1,0:T(8,128)(2,1)S(1)}, bf16[2,2,2,4,16,128]{5,4,3,2,1,0:T(8,128)(2,1)S(1)}, u32[]{:S(2)}, u32[]{:S(2)}) collective-permute-start(bf16[2,2,2,4,16,128]{5,4,3,2,1,0:T(8,128)(2,1)S(1)} %copy-done.9), channel_id=1, source_target_pairs={{0,48},{8,56},{16,32},{24,40},{32,80},{40,88},{48,64},{56,72},{64,... | collective-permute-start | bytes 393224 | tf_op jit(solution)/shard_map/ppermute | solution.py:376
  36.4 9.8 %collective-permute-start.5 = (bf16[2,2,2,4,16,128]{5,4,3,2,1,0:T(8,128)(2,1)S(1)}, bf16[2,2,2,4,16,128]{5,4,3,2,1,0:T(8,128)(2,1)S(1)}, u32[]{:S(2)}, u32[]{:S(2)}) collective-permute-start(bf16[2,2,2,4,16,128]{5,4,3,2,1,0:T(8,128)(2,1)S(1)} %copy-done.8), channel_id=1, source_target_pairs={{0,112},{8,120},{16,96},{24,104},{32,16},{40,24},{48,0},{56,8},{64... | collective-permute-start | bytes 393224 | tf_op jit(solution)/shard_map/ppermute | solution.py:376
  39.0 8.0 %collective-permute-start.6 = (bf16[2,2,2,4,16,128]{5,4,3,2,1,0:T(8,128)(2,1)S(1)}, bf16[2,2,2,4,16,128]{5,4,3,2,1,0:T(8,128)(2,1)S(1)}, u32[]{:S(2)}, u32[]{:S(2)}) collective-permute-start(bf16[2,2,2,4,16,128]{5,4,3,2,1,0:T(8,128)(2,1)S(1)} %copy-done.7), channel_id=1, source_target_pairs={{0,96},{8,104},{16,112},{24,120},{32,0},{40,8},{48,16},{56,24},{64... | collective-permute-start | bytes 393224 | tf_op jit(solution)/shard_map/ppermute | solution.py:376
  47.7 1.4 %collective-permute-start.7 = (bf16[2,2,2,4,16,128]{5,4,3,2,1,0:T(8,128)(2,1)S(1)}, bf16[2,2,2,4,16,128]{5,4,3,2,1,0:T(8,128)(2,1)S(1)}, u32[]{:S(2)}, u32[]{:S(2)}) collective-permute-start(bf16[2,2,2,4,16,128]{5,4,3,2,1,0:T(8,128)(2,1)S(1)} %get-tuple-element.33), channel_id=1, source_target_pairs={{0,8},{8,0},{16,24},{24,16},{32,40},{40,32},{48,56},{56,48},{64,72... | collective-permute-start | bytes 393224 | tf_op jit(solution)/shard_map/ppermute | solution.py:385
  47.8 1.5 %collective-permute-start.8 = (bf16[2,2,2,4,16,128]{5,4,3,2,1,0:T(8,128)(2,1)S(1)}, bf16[2,2,2,4,16,128]{5,4,3,2,1,0:T(8,128)(2,1)S(1)}, u32[]{:S(2)}, u32[]{:S(2)}) collective-permute-start(bf16[2,2,2,4,16,128]{5,4,3,2,1,0:T(8,128)(2,1)S(1)} %get-tuple-element.34), channel_id=1, source_target_pairs={{0,8},{8,0},{16,24},{24,16},{32,40},{40,32},{48,56},{56,48},{64,72... | collective-permute-start | bytes 393224 | tf_op jit(solution)/shard_map/ppermute | solution.py:385
  48.3 1.3 %collective-permute-start.9 = (bf16[2,2,2,4,16,128]{5,4,3,2,1,0:T(8,128)(2,1)S(1)}, bf16[2,2,2,4,16,128]{5,4,3,2,1,0:T(8,128)(2,1)S(1)}, u32[]{:S(2)}, u32[]{:S(2)}) collective-permute-start(bf16[2,2,2,4,16,128]{5,4,3,2,1,0:T(8,128)(2,1)S(1)} %get-tuple-element.35), channel_id=1, source_target_pairs={{0,8},{8,0},{16,24},{24,16},{32,40},{40,32},{48,56},{56,48},{64,72... | collective-permute-start | bytes 393224 | tf_op jit(solution)/shard_map/ppermute | solution.py:385
  48.4 1.4 %collective-permute-start.10 = (bf16[2,2,2,4,16,128]{5,4,3,2,1,0:T(8,128)(2,1)S(1)}, bf16[2,2,2,4,16,128]{5,4,3,2,1,0:T(8,128)(2,1)S(1)}, u32[]{:S(2)}, u32[]{:S(2)}) collective-permute-start(bf16[2,2,2,4,16,128]{5,4,3,2,1,0:T(8,128)(2,1)S(1)} %get-tuple-element.36), channel_id=1, source_target_pairs={{0,8},{8,0},{16,24},{24,16},{32,40},{40,32},{48,56},{56,48},{64,72... | collective-permute-start | bytes 393224 | tf_op jit(solution)/shard_map/ppermute | solution.py:385
  51.5 1.2 %copy-start.2 = (bf16[4,256,512]{2,1,0:T(8,128)(2,1)S(1)}, bf16[4,256,512]{2,1,0:T(8,128)(2,1)}, u32[]{:S(2)}) copy-start(bf16[4,256,512]{2,1,0:T(8,128)(2,1)} %constant.14.clone.third_ref) | copy-start | bytes 3145732
  51.5 1.5 %copy-start.3 = (f32[2,1024,128]{2,1,0:T(8,128)S(1)}, f32[2,1024,128]{2,1,0:T(8,128)}, u32[]{:S(2)}) copy-start(f32[2,1024,128]{2,1,0:T(8,128)} %get-tuple-element.38.twist) | copy-start | bytes 3145732
  51.5 1.7 %copy-start.5 = (f32[4,256,128]{2,1,0:T(8,128)S(1)}, f32[4,256,128]{2,1,0:T(8,128)}, u32[]{:S(2)}) copy-start(f32[4,256,128]{2,1,0:T(8,128)} %get-tuple-element.37.weight_ref) | copy-start | bytes 1572868
  52.3 2.7 %collective-permute-start.11 = (f32[2,1024,128]{2,1,0:T(8,128)S(1)}, f32[2,1024,128]{2,1,0:T(8,128)S(1)}, u32[]{:S(2)}, u32[]{:S(2)}) collective-permute-start(f32[2,1024,128]{2,1,0:T(8,128)S(1)} %shard_map.122.spec), channel_id=1, source_target_pairs={{0,8},{8,0},{16,24},{24,16},{32,40},{40,32},{48,56},{56,48},{64,72... | collective-permute-start | bytes 3145736 | tf_op jit(solution)/shard_map/ppermute | solution.py:395
  56.2 34.7 %copy-start.6 = (bf16[4,2,256,256]{3,2,1,0:T(8,128)(2,1)S(1)}, bf16[4,2,256,256]{3,2,1,0:T(8,128)(2,1)}, u32[]{:S(2)}) copy-start(bf16[4,2,256,256]{3,2,1,0:T(8,128)(2,1)} %constant.17.clone.table_ref) | copy-start | bytes 3145732

commit v6 on v5

--- a/solution.py
+++ b/solution.py
@@ -16,7 +16,7 @@
 SMEM = pl.BlockSpec(memory_space=pltpu.SMEM)
 ANY = pl.BlockSpec(memory_space=pl.ANY)
 MIB = 1 << 20
-OFFSETS = [(0, 0), (1, 0), (1, 2), (0, 2), (0, 1), (1, 1), (1, 3), (0, 3)]
+OFFSETS = [(0, 0), (1, 0), (1, 2), (0, 2), (1, 1), (1, 3), (0, 1), (0, 3)]
 
 
 def phases(product, count):
@@ -153,8 +153,8 @@
 
 
 def pack_kernel(*refs):
-    piece_refs, out_refs, sems = refs[:8], refs[9:13], refs[13]
-    copies = [pltpu.make_async_copy(piece_refs[i].at[1], out_refs[i // 2].at[i % 2], sems.at[i]) for i in range(8)]
+    piece_refs, out_refs, sems = refs[:8], refs[9:11], refs[11]
+    copies = [pltpu.make_async_copy(piece_refs[i].at[1], out_refs[i // 4].at[i % 4], sems.at[i]) for i in range(8)]
     for copy in copies:
         copy.start()
     for copy in copies:
@@ -231,12 +231,12 @@
 
 
 def assemble_kernel(*refs):
-    piece_refs, cross_refs, bank, sems = refs[:8], refs[8:12], *refs[12:]
+    piece_refs, cross_refs, bank, sems = refs[:8], refs[8:10], *refs[10:]
     x, z, core = place()
     copies = []
     for i, (rz, rx) in enumerate(OFFSETS):
         for rc in range(2):
-            src = piece_refs[i].at[0] if rc == 0 else cross_refs[i // 2].at[i % 2]
+            src = piece_refs[i].at[0] if rc == 0 else cross_refs[i // 4].at[i % 4]
             origin = ((x + 4 - rx) % 4) * 4 + (z + rz) % 2 * 2 + (core + rc) % 2
             copies.append(pltpu.make_async_copy(src, bank.at[origin], sems.at[len(copies)]))
     for copy in copies:
@@ -319,11 +319,9 @@
             parts.append((both[:128], both[128:]))
         outs = four_way(1, parts)
         for p, (re, im) in enumerate(outs):
-            right = jnp.concatenate([re, im], axis=0)
-            hi = right.astype(BF)
-            lo = (right - hi.astype(F32)).astype(BF)
-            cos = dot_nt(table_ref[p, 0], hi) + dot_nt(table_ref[p, 0], lo)
-            sin = dot_nt(table_ref[p, 1], hi) + dot_nt(table_ref[p, 1], lo)
+            right = jnp.concatenate([re, im], axis=0).astype(BF)
+            cos = dot_nt(table_ref[p, 0], right)
+            sin = dot_nt(table_ref[p, 1], right)
             sr = cos[:, :128] - sin[:, 128:]
             si = sin[:, :128] + cos[:, 128:]
             out_ref[pair, pl.ds(p, 256, stride=4), :] = jnp.sqrt(sr * sr + si * si) * scales[slot]
@@ -379,12 +377,12 @@
         [VMEM] * 2 + [ANY] * 3, 3 * 10**8, 4 * MIB, [pltpu.VMEM((512, 512), F32)],
     )
     crosses = call(
-        pack_kernel, (*pieces, token), (shape(2, *blk),) * 4, [ANY] * 9, 1, MIB, [pltpu.SemaphoreType.DMA((8,))],
-        limit=8, space=(ANY,) * 4,
+        pack_kernel, (*pieces, token), (shape(4, *blk),) * 2, [ANY] * 9, 1, MIB, [pltpu.SemaphoreType.DMA((8,))],
+        limit=8, space=(ANY,) * 2,
     )
     crossed = [lax.ppermute(cross, "tmpl", swap_core) for cross in crosses]
     ordered = call(
-        assemble_kernel, (*pieces, *crossed), shape(16, *blk), [ANY] * 12, 1, 10 * MIB,
+        assemble_kernel, (*pieces, *crossed), shape(16, *blk), [ANY] * 10, 1, 10 * MIB,
         [pltpu.SemaphoreType.DMA((16,))], limit=8,
     )
     own = lax.all_to_all(turned, "seg", 0, 0)

time: 95.1 us -> 93.5 us (0.983)
  waiting for transfers between devices: 15.1 us -> 13.3 us
    ppermute x7, waiting for transfers between devices: 13.3 us -> 11.1 us  [per_device(): pieces.append(lax.ppermute(send, 'tmpl', hop))]
    ppermute x7, starting transfers between devices: 11.2 us -> 12.4 us  [per_device(): pieces.append(lax.ppermute(send, 'tmpl', hop))]
  transfers between devices with their start and end apart: 14 -> 12, of which waited for: 11 -> 7; matrix products, arithmetic and copies ran while one was open for 0% -> 0% of each run, Pallas kernels for 4% -> 4%
where the time goes in v6:
time: 93.5 us; the launch traced here: 92.9 us
  blocking collectives  35 us (37%)
  starting transfers between devices  28.4 us (30%)
  Pallas kernels  13.9 us (15%)
  waiting for transfers between devices  13.3 us (14%)
  local copies, waits for them, and re-layouts  2.05 us (2%)
    all_to_all x1, blocking collectives, per_device(): series = lax.all_to_all(inner, 'seg', 0, 0)  35 us
    pallas_call x8, Pallas kernels, call(): pl.pallas_call(kernel, out_shape=outs, in_specs=specs, out_specs=space if...  13.9 us
    ppermute x7, starting transfers between devices, per_device(): pieces.append(lax.ppermute(send, 'tmpl', hop))  12.4 us
    ppermute x7, waiting for transfers between devices, per_device(): pieces.append(lax.ppermute(send, 'tmpl', hop))  11.1 us
    all_to_all x1, starting transfers between devices, per_device(): columns = lax.all_to_all(gated, 'seg', 0, 0)  8.01 us
    all_to_all x1, starting transfers between devices, per_device(): own = lax.all_to_all(turned, 'seg', 0, 0)  7.21 us
    unnamed x22, local copies, waits for them, and re-layouts  2.05 us
  transfers between devices with their start and end apart: 12, of which 7 were waited for; matrix products, arithmetic and copies ran while one was open for 0% of the time, Pallas kernels for 4%

profile of v6, /device:TPU:0, one launch (start us, length us, event | category | flops | bytes accessed | tf_op | source)
XLA Modules:
  0.0 92.9 jit_solution(14106763512328152550)
XLA Ops:
  0.0 4.2 %shard_map.118 = (bf16[8,128,128]{2,1,0:T(8,128)(2,1)}, f32[4,256,128]{2,1,0:T(8,128)}, f32[2,1024,128]{2,1,0:T(8,128)}, bf16[2,2,2,4,16,128]{5,4,3,2,1,0:T(8,12...) custom-call(f32[2,128,1024]{2,1,0:T(8,128)} %strain_ref.1, ...), custom_call_target="tpu_custom_call" | custom-call | flops 100000000 | bytes 4194304 | tf_op jit(solution)/shard_map/pallas_call | solution.py:335
  4.2 8.0 %all-to-all-start = ((bf16[8,128,128]{2,1,0:T(8,128)(2,1)}), bf16[8,128,128]{2,1,0:T(8,128)(2,1)S(1)}, u32[]{:S(2)}, u32[]{:S(2)}) async-start(bf16[8,128,128]{2,1,0:T(8,128)(2,1)} %get-tuple-element.20), calls=%async_computation | async-start | bytes 524288 | tf_op jit(solution)/shard_map/all_to_all | solution.py:369
  12.2 1.0 %collective-permute-start = (bf16[2,2,2,4,16,128]{5,4,3,2,1,0:T(8,128)(2,1)}, bf16[2,2,2,4,16,128]{5,4,3,2,1,0:T(8,128)(2,1)S(1)}, u32[]{:S(2)}, u32[]{:S(2)}) collective-permute-start(bf16[2,2,2,4,16,128]{5,4,3,2,1,0:T(8,128)(2,1)} %get-tuple-element.21), channel_id=1, source_target_pairs={{0,16},{8,24},{16,0},{24,8},{32,48},{40,56},{48,32},{56,40},{64,80... | collective-permute-start | bytes 393224 | tf_op jit(solution)/shard_map/ppermute | solution.py:374
  13.2 3.5 %collective-permute-start.1 = (bf16[2,2,2,4,16,128]{5,4,3,2,1,0:T(8,128)(2,1)}, bf16[2,2,2,4,16,128]{5,4,3,2,1,0:T(8,128)(2,1)S(1)}, u32[]{:S(2)}, u32[]{:S(2)}) collective-permute-start(bf16[2,2,2,4,16,128]{5,4,3,2,1,0:T(8,128)(2,1)} %get-tuple-element.22), channel_id=1, source_target_pairs={{0,80},{8,88},{16,64},{24,72},{32,112},{40,120},{48,96},{56,104},{... | collective-permute-start | bytes 393224 | tf_op jit(solution)/shard_map/ppermute | solution.py:374
  16.7 0.5 collective-permute-start.2
  17.2 5.4 %collective-permute-done.refs_0_.refs_1_ = bf16[2,2,2,4,16,128]{5,4,3,2,1,0:T(8,128)(2,1)S(1)} collective-permute-done((bf16[2,2,2,4,16,128]{5,4,3,2,1,0:T(8,128)(2,1)}, bf16[2,2,2,4,16,128]{5,4,3,2,1,0:T(8,128)(2,1)S(1)}, u32[]{:S(2)}, u32[]{:S(2)}) %collective-permute-start) | collective-permute-done | bytes 131104 | tf_op jit(solution)/shard_map/ppermute | solution.py:374
  22.7 0.7 collective-permute-done.2.refs_2_.refs_3_
  23.4 1.4 %copy-done = f32[368,1024]{1,0:T(8,128)S(1)} copy-done((f32[368,1024]{1,0:T(8,128)S(1)}, f32[368,1024]{1,0:T(8,128)}, u32[]{:S(2)}) %copy-start) | copy-done | bytes 1507352
  24.8 1.6 %shard_map.119 = (bf16[8,2,4,32,128]{4,3,2,1,0:T(8,128)(2,1)}, f32[8,128]{1,0:T(8,128)S(1)}) custom-call(bf16[8,128,128]{2,1,0:T(8,128)(2,1)S(1)} %all-to-all-done.cols_ref, f32[368,1024]{1,0:T(8,128)S(1)} %copy-done, bf16[2,2,2,4,16,128]{5,4,3,2,1,0:T(8,128)(2,1)S(1)} %collective-permute-done.refs_0_.refs_1_, ...), custom_call_target="tpu_custom_call" | custom-call | flops 300000000 | bytes 4194304 | tf_op jit(solution)/shard_map/pallas_call | solution.py:335
  26.4 7.2 %all-to-all-start.1 = ((bf16[8,2,4,32,128]{4,3,2,1,0:T(8,128)(2,1)}), bf16[8,2,4,32,128]{4,3,2,1,0:T(8,128)(2,1)S(1)}, u32[]{:S(2)}, u32[]{:S(2)}) async-start(bf16[8,2,4,32,128]{4,3,2,1,0:T(8,128)(2,1)} %get-tuple-element.24), calls=%async_computation.1 | async-start | bytes 1048576 | tf_op jit(solution)/shard_map/all_to_all | solution.py:388
  33.6 1.7 %collective-permute-start.3 = (bf16[2,2,2,4,16,128]{5,4,3,2,1,0:T(8,128)(2,1)S(1)}, bf16[2,2,2,4,16,128]{5,4,3,2,1,0:T(8,128)(2,1)S(1)}, u32[]{:S(2)}, u32[]{:S(2)}) collective-permute-start(bf16[2,2,2,4,16,128]{5,4,3,2,1,0:T(8,128)(2,1)S(1)} %copy-done.10), channel_id=1, source_target_pairs={{0,48},{8,56},{16,32},{24,40},{32,80},{40,88},{48,64},{56,72},{64,... | collective-permute-start | bytes 393224 | tf_op jit(solution)/shard_map/ppermute | solution.py:374
  35.3 2.5 %collective-permute-start.4 = (bf16[2,2,2,4,16,128]{5,4,3,2,1,0:T(8,128)(2,1)S(1)}, bf16[2,2,2,4,16,128]{5,4,3,2,1,0:T(8,128)(2,1)S(1)}, u32[]{:S(2)}, u32[]{:S(2)}) collective-permute-start(bf16[2,2,2,4,16,128]{5,4,3,2,1,0:T(8,128)(2,1)S(1)} %copy-done.9), channel_id=1, source_target_pairs={{0,112},{8,120},{16,96},{24,104},{32,16},{40,24},{48,0},{56,8},{64... | collective-permute-start | bytes 393224 | tf_op jit(solution)/shard_map/ppermute | solution.py:374
  37.8 3.2 %collective-permute-start.6 = (bf16[2,2,2,4,16,128]{5,4,3,2,1,0:T(8,128)(2,1)S(1)}, bf16[2,2,2,4,16,128]{5,4,3,2,1,0:T(8,128)(2,1)S(1)}, u32[]{:S(2)}, u32[]{:S(2)}) collective-permute-start(bf16[2,2,2,4,16,128]{5,4,3,2,1,0:T(8,128)(2,1)S(1)} %copy-done.7), channel_id=1, source_target_pairs={{0,96},{8,104},{16,112},{24,120},{32,0},{40,8},{48,16},{56,24},{64... | collective-permute-start | bytes 393224 | tf_op jit(solution)/shard_map/ppermute | solution.py:374
  41.0 4.5 %collective-permute-done.3.refs_4_ = bf16[2,2,2,4,16,128]{5,4,3,2,1,0:T(8,128)(2,1)S(1)} collective-permute-done((bf16[2,2,2,4,16,128]{5,4,3,2,1,0:T(8,128)(2,1)S(1)}, bf16[2,2,2,4,16,128]{5,4,3,2,1,0:T(8,128)(2,1)S(1)}, u32[]{:S(2)}, u32[]{:S(2)}) %collective-permute-start.3) | collective-permute-done | bytes 131104 | tf_op jit(solution)/shard_map/ppermute | solution.py:374
  45.5 0.4 collective-permute-done.4.refs_5_
  46.0 0.8 shard_map.120
  46.8 0.1 collective-permute-start.7
  46.9 0.5 collective-permute-start.8
  47.4 1.0 %collective-permute-done.7.refs_8_ = bf16[4,2,2,4,16,128]{5,4,3,2,1,0:T(8,128)(2,1)S(1)} collective-permute-done((bf16[4,2,2,4,16,128]{5,4,3,2,1,0:T(8,128)(2,1)S(1)}, bf16[4,2,2,4,16,128]{5,4,3,2,1,0:T(8,128)(2,1)S(1)}, u32[]{:S(2)}, u32[]{:S(2)}) %collective-permute-start.7) | collective-permute-done | bytes 262176 | tf_op jit(solution)/shard_map/ppermute | solution.py:383
  48.4 0.4 collective-permute-done.8.refs_9_
  48.8 1.6 %shard_map.121.after_ref.bank = bf16[16,2,2,4,16,128]{5,4,3,2,1,0:T(8,128)(2,1)S(1)} custom-call(bf16[2,2,2,4,16,128]{5,4,3,2,1,0:T(8,128)(2,1)S(1)} %copy-done.4, bf16[2,2,2,4,16,128]{5,4,3,2,1,0:T(8,128)(2,1)S(1)} %collective-permute-done.refs_0_.refs_1_, bf16[2,2,2,4,16,128]{5,4,3,2,1,0:T(8,128)(2,1)S(1)} %collective-permute-done.1.refs_1_.refs_2_, ...), custom_call_target="tpu_custom_call" | custom-call | flops 1 | bytes 10485760 | tf_op jit(solution)/shard_map/pallas_call | solution.py:335
  50.4 0.0 copy-start.2
  50.4 0.8 shard_map.122.spec
  51.2 0.2 collective-permute-start.9
  51.5 0.2 copy-done.2
  51.6 0.3 copy-done.3
  52.0 0.1 copy-done.5
  52.1 1.1 %shard_map.123.half_ref = bf16[8,528,128]{2,1,0:T(8,128)(2,1)S(1)} custom-call(f32[2,1024,128]{2,1,0:T(8,128)S(1)} %shard_map.122.spec, f32[4,256,128]{2,1,0:T(8,128)S(1)} %copy-done.5, bf16[4,256,512]{2,1,0:T(8,128)(2,1)S(1)} %copy-done.2, f32[2,1024,128]{2,1,0:T(8,128)S(1)} %copy-done.3, bf16[16,2,2,4,16,128]{5,4,3,2,1,0:T(8,128)(2,1)S(1)} %shard_map.121.after_ref.bank), custom_call_target="tpu_custom_call" | custom-call | flops 2000000000 | bytes 10485760 | tf_op jit(solution)/shard_map/pallas_call | solution.py:335
  53.2 0.8 collective-permute-done.9.spec
  54.0 1.1 %shard_map.124 = bf16[8,1040,128]{2,1,0:T(8,128)(2,1)S(1)} custom-call(f32[2,1024,128]{2,1,0:T(8,128)S(1)} %collective-permute-done.9.spec, f32[4,256,128]{2,1,0:T(8,128)S(1)} %copy-done.5, bf16[4,256,512]{2,1,0:T(8,128)(2,1)S(1)} %copy-done.2, f32[2,1024,128]{2,1,0:T(8,128)S(1)} %copy-done.3, ...), custom_call_target="tpu_custom_call" | custom-call | flops 2000000000 | bytes 10485760 | tf_op jit(solution)/shard_map/pallas_call | solution.py:335
  55.1 35.0 %all_to_all.15.in_ref = bf16[8,1040,128]{2,1,0:T(8,128)(2,1)S(1)} all-to-all(bf16[8,1040,128]{2,1,0:T(8,128)(2,1)S(1)} %shard_map.124), channel_id=1, replica_groups=mesh['tmpl'=16,'seg'=8] {'seg'}, dimensions={0} | all-to-all | bytes 4259840 | tf_op jit(solution)/shard_map/all_to_all | solution.py:404
  90.2 2.7 %shard_map.125 = f32[2,2,1024,128]{3,2,1,0:T(8,128)} custom-call(bf16[8,1040,128]{2,1,0:T(8,128)(2,1)S(1)} %all_to_all.15.in_ref, bf16[4,2,256,256]{3,2,1,0:T(8,128)(2,1)S(1)} %copy-done.6), custom_call_target="tpu_custom_call" | custom-call | flops 3000000000 | bytes 6291456 | tf_op jit(solution)/shard_map/pallas_call | solution.py:335
  (23 shorter events, 0.1 us)
Async XLA Ops:
  4.2 31.1 %copy-start.9 = (bf16[2,2,2,4,16,128]{5,4,3,2,1,0:T(8,128)(2,1)S(1)}, bf16[2,2,2,4,16,128]{5,4,3,2,1,0:T(8,128)(2,1)}, u32[]{:S(2)}) copy-start(bf16[2,2,2,4,16,128]{5,4,3,2,1,0:T(8,128)(2,1)} %get-tuple-element.27) | copy-start | bytes 393220
  4.2 33.6 %copy-start.8 = (bf16[2,2,2,4,16,128]{5,4,3,2,1,0:T(8,128)(2,1)S(1)}, bf16[2,2,2,4,16,128]{5,4,3,2,1,0:T(8,128)(2,1)}, u32[]{:S(2)}) copy-start(bf16[2,2,2,4,16,128]{5,4,3,2,1,0:T(8,128)(2,1)} %get-tuple-element.28) | copy-start | bytes 393220
  4.2 33.6 %copy-start.7 = (bf16[2,2,2,4,16,128]{5,4,3,2,1,0:T(8,128)(2,1)S(1)}, bf16[2,2,2,4,16,128]{5,4,3,2,1,0:T(8,128)(2,1)}, u32[]{:S(2)}) copy-start(bf16[2,2,2,4,16,128]{5,4,3,2,1,0:T(8,128)(2,1)} %get-tuple-element.29) | copy-start | bytes 393220
  4.2 41.8 %copy-start.4 = (bf16[2,2,2,4,16,128]{5,4,3,2,1,0:T(8,128)(2,1)S(1)}, bf16[2,2,2,4,16,128]{5,4,3,2,1,0:T(8,128)(2,1)}, u32[]{:S(2)}) copy-start(bf16[2,2,2,4,16,128]{5,4,3,2,1,0:T(8,128)(2,1)} %get-tuple-element.25.refs_0_) | copy-start | bytes 393220
  4.2 19.2 %all-to-all-start = ((bf16[8,128,128]{2,1,0:T(8,128)(2,1)}), bf16[8,128,128]{2,1,0:T(8,128)(2,1)S(1)}, u32[]{:S(2)}, u32[]{:S(2)}) async-start(bf16[8,128,128]{2,1,0:T(8,128)(2,1)} %get-tuple-element.20), calls=%async_computation | async-start | bytes 524288 | tf_op jit(solution)/shard_map/all_to_all | solution.py:369
  12.2 10.4 %collective-permute-start = (bf16[2,2,2,4,16,128]{5,4,3,2,1,0:T(8,128)(2,1)}, bf16[2,2,2,4,16,128]{5,4,3,2,1,0:T(8,128)(2,1)S(1)}, u32[]{:S(2)}, u32[]{:S(2)}) collective-permute-start(bf16[2,2,2,4,16,128]{5,4,3,2,1,0:T(8,128)(2,1)} %get-tuple-element.21), channel_id=1, source_target_pairs={{0,16},{8,24},{16,0},{24,8},{32,48},{40,56},{48,32},{56,40},{64,80... | collective-permute-start | bytes 393224 | tf_op jit(solution)/shard_map/ppermute | solution.py:374
  13.2 9.4 %collective-permute-start.1 = (bf16[2,2,2,4,16,128]{5,4,3,2,1,0:T(8,128)(2,1)}, bf16[2,2,2,4,16,128]{5,4,3,2,1,0:T(8,128)(2,1)S(1)}, u32[]{:S(2)}, u32[]{:S(2)}) collective-permute-start(bf16[2,2,2,4,16,128]{5,4,3,2,1,0:T(8,128)(2,1)} %get-tuple-element.22), channel_id=1, source_target_pairs={{0,80},{8,88},{16,64},{24,72},{32,112},{40,120},{48,96},{56,104},{... | collective-permute-start | bytes 393224 | tf_op jit(solution)/shard_map/ppermute | solution.py:374
  16.7 6.7 %collective-permute-start.2 = (bf16[2,2,2,4,16,128]{5,4,3,2,1,0:T(8,128)(2,1)}, bf16[2,2,2,4,16,128]{5,4,3,2,1,0:T(8,128)(2,1)S(1)}, u32[]{:S(2)}, u32[]{:S(2)}) collective-permute-start(bf16[2,2,2,4,16,128]{5,4,3,2,1,0:T(8,128)(2,1)} %get-tuple-element.23), channel_id=1, source_target_pairs={{0,64},{8,72},{16,80},{24,88},{32,96},{40,104},{48,112},{56,120},{... | collective-permute-start | bytes 393224 | tf_op jit(solution)/shard_map/ppermute | solution.py:374
  23.4 1.4 %copy-start = (f32[368,1024]{1,0:T(8,128)S(1)}, f32[368,1024]{1,0:T(8,128)}, u32[]{:S(2)}) copy-start(f32[368,1024]{1,0:T(8,128)} %constant.12.clone.table_ref) | copy-start | bytes 4521988
  24.8 8.8 %copy-start.10 = (bf16[2,2,2,4,16,128]{5,4,3,2,1,0:T(8,128)(2,1)S(1)}, bf16[2,2,2,4,16,128]{5,4,3,2,1,0:T(8,128)(2,1)}, u32[]{:S(2)}) copy-start(bf16[2,2,2,4,16,128]{5,4,3,2,1,0:T(8,128)(2,1)} %get-tuple-element.26) | copy-start | bytes 393220
  26.4 24.0 %all-to-all-start.1 = ((bf16[8,2,4,32,128]{4,3,2,1,0:T(8,128)(2,1)}), bf16[8,2,4,32,128]{4,3,2,1,0:T(8,128)(2,1)S(1)}, u32[]{:S(2)}, u32[]{:S(2)}) async-start(bf16[8,2,4,32,128]{4,3,2,1,0:T(8,128)(2,1)} %get-tuple-element.24), calls=%async_computation.1 | async-start | bytes 1048576 | tf_op jit(solution)/shard_map/all_to_all | solution.py:388
  33.6 16.8 %copy-start.1 = (f32[256,1152]{1,0:T(8,128)S(1)}, f32[256,1152]{1,0:T(8,128)}, u32[]{:S(2)}) copy-start(f32[256,1152]{1,0:T(8,128)} %constant.13.clone.table_ref) | copy-start | bytes 3538948
  33.6 11.9 %collective-permute-start.3 = (bf16[2,2,2,4,16,128]{5,4,3,2,1,0:T(8,128)(2,1)S(1)}, bf16[2,2,2,4,16,128]{5,4,3,2,1,0:T(8,128)(2,1)S(1)}, u32[]{:S(2)}, u32[]{:S(2)}) collective-permute-start(bf16[2,2,2,4,16,128]{5,4,3,2,1,0:T(8,128)(2,1)S(1)} %copy-done.10), channel_id=1, source_target_pairs={{0,48},{8,56},{16,32},{24,40},{32,80},{40,88},{48,64},{56,72},{64,... | collective-permute-start | bytes 393224 | tf_op jit(solution)/shard_map/ppermute | solution.py:374
  35.3 10.7 %collective-permute-start.4 = (bf16[2,2,2,4,16,128]{5,4,3,2,1,0:T(8,128)(2,1)S(1)}, bf16[2,2,2,4,16,128]{5,4,3,2,1,0:T(8,128)(2,1)S(1)}, u32[]{:S(2)}, u32[]{:S(2)}) collective-permute-start(bf16[2,2,2,4,16,128]{5,4,3,2,1,0:T(8,128)(2,1)S(1)} %copy-done.9), channel_id=1, source_target_pairs={{0,112},{8,120},{16,96},{24,104},{32,16},{40,24},{48,0},{56,8},{64... | collective-permute-start | bytes 393224 | tf_op jit(solution)/shard_map/ppermute | solution.py:374
  37.8 8.2 %collective-permute-start.5 = (bf16[2,2,2,4,16,128]{5,4,3,2,1,0:T(8,128)(2,1)S(1)}, bf16[2,2,2,4,16,128]{5,4,3,2,1,0:T(8,128)(2,1)S(1)}, u32[]{:S(2)}, u32[]{:S(2)}) collective-permute-start(bf16[2,2,2,4,16,128]{5,4,3,2,1,0:T(8,128)(2,1)S(1)} %copy-done.8), channel_id=1, source_target_pairs={{0,32},{8,40},{16,48},{24,56},{32,64},{40,72},{48,80},{56,88},{64,... | collective-permute-start | bytes 393224 | tf_op jit(solution)/shard_map/ppermute | solution.py:374
  37.8 8.2 %collective-permute-start.6 = (bf16[2,2,2,4,16,128]{5,4,3,2,1,0:T(8,128)(2,1)S(1)}, bf16[2,2,2,4,16,128]{5,4,3,2,1,0:T(8,128)(2,1)S(1)}, u32[]{:S(2)}, u32[]{:S(2)}) collective-permute-start(bf16[2,2,2,4,16,128]{5,4,3,2,1,0:T(8,128)(2,1)S(1)} %copy-done.7), channel_id=1, source_target_pairs={{0,96},{8,104},{16,112},{24,120},{32,0},{40,8},{48,16},{56,24},{64... | collective-permute-start | bytes 393224 | tf_op jit(solution)/shard_map/ppermute | solution.py:374
  46.8 1.6 %collective-permute-start.7 = (bf16[4,2,2,4,16,128]{5,4,3,2,1,0:T(8,128)(2,1)S(1)}, bf16[4,2,2,4,16,128]{5,4,3,2,1,0:T(8,128)(2,1)S(1)}, u32[]{:S(2)}, u32[]{:S(2)}) collective-permute-start(bf16[4,2,2,4,16,128]{5,4,3,2,1,0:T(8,128)(2,1)S(1)} %get-tuple-element.31), channel_id=1, source_target_pairs={{0,8},{8,0},{16,24},{24,16},{32,40},{40,32},{48,56},{56,48},{64,72... | collective-permute-start | bytes 786440 | tf_op jit(solution)/shard_map/ppermute | solution.py:383
  46.9 1.9 %collective-permute-start.8 = (bf16[4,2,2,4,16,128]{5,4,3,2,1,0:T(8,128)(2,1)S(1)}, bf16[4,2,2,4,16,128]{5,4,3,2,1,0:T(8,128)(2,1)S(1)}, u32[]{:S(2)}, u32[]{:S(2)}) collective-permute-start(bf16[4,2,2,4,16,128]{5,4,3,2,1,0:T(8,128)(2,1)S(1)} %get-tuple-element.32), channel_id=1, source_target_pairs={{0,8},{8,0},{16,24},{24,16},{32,40},{40,32},{48,56},{56,48},{64,72... | collective-permute-start | bytes 786440 | tf_op jit(solution)/shard_map/ppermute | solution.py:383
  50.4 1.2 %copy-start.2 = (bf16[4,256,512]{2,1,0:T(8,128)(2,1)S(1)}, bf16[4,256,512]{2,1,0:T(8,128)(2,1)}, u32[]{:S(2)}) copy-start(bf16[4,256,512]{2,1,0:T(8,128)(2,1)} %constant.14.clone.third_ref) | copy-start | bytes 3145732
  50.4 1.5 %copy-start.3 = (f32[2,1024,128]{2,1,0:T(8,128)S(1)}, f32[2,1024,128]{2,1,0:T(8,128)}, u32[]{:S(2)}) copy-start(f32[2,1024,128]{2,1,0:T(8,128)} %get-tuple-element.34.twist) | copy-start | bytes 3145732
  50.4 1.7 %copy-start.5 = (f32[4,256,128]{2,1,0:T(8,128)S(1)}, f32[4,256,128]{2,1,0:T(8,128)}, u32[]{:S(2)}) copy-start(f32[4,256,128]{2,1,0:T(8,128)} %get-tuple-element.33.weight_ref) | copy-start | bytes 1572868
  51.2 2.7 %collective-permute-start.9 = (f32[2,1024,128]{2,1,0:T(8,128)S(1)}, f32[2,1024,128]{2,1,0:T(8,128)S(1)}, u32[]{:S(2)}, u32[]{:S(2)}) collective-permute-start(f32[2,1024,128]{2,1,0:T(8,128)S(1)} %shard_map.122.spec), channel_id=1, source_target_pairs={{0,8},{8,0},{16,24},{24,16},{32,40},{40,32},{48,56},{56,48},{64,72... | collective-permute-start | bytes 3145736 | tf_op jit(solution)/shard_map/ppermute | solution.py:393
  55.1 35.0 %copy-start.6 = (bf16[4,2,256,256]{3,2,1,0:T(8,128)(2,1)S(1)}, bf16[4,2,256,256]{3,2,1,0:T(8,128)(2,1)}, u32[]{:S(2)}) copy-start(bf16[4,2,256,256]{3,2,1,0:T(8,128)(2,1)} %constant.17.clone.table_ref) | copy-start | bytes 3145732

commit v7 on v6

--- a/solution.py
+++ b/solution.py
@@ -209,8 +209,8 @@
                         out_ref[2 * k + half, part, r1, at] = done[part][:, 128 * half : 128 * half + 128]
 
 
-def second_kernel(own_ref, table_ref, after_ref, spec_ref, z_ref):
-    del after_ref
+def second_kernel(own_ref, table_ref, after_ref, also_ref, spec_ref, z_ref):
+    del after_ref, also_ref
     hi, lo = table_ref[:, :512].astype(BF), table_ref[:, 512:1024].astype(BF)
     for r in range(4):
         re = own_ref[:, 0, r].reshape(256, 128)
@@ -387,8 +387,8 @@
     )
     own = lax.all_to_all(turned, "seg", 0, 0)
     spec = call(
-        second_kernel, (own, const["second"], ordered), shape(2, 1024, 128, dtype=F32),
-        [VMEM] * 2 + [ANY], 1, 1, [pltpu.VMEM((4, 256, 256), F32)],
+        second_kernel, (own, const["second"], *crossed), shape(2, 1024, 128, dtype=F32),
+        [VMEM] * 2 + [ANY] * 2, 1, 1, [pltpu.VMEM((4, 256, 256), F32)],
     )
     other_spec = lax.ppermute(spec, "tmpl", swap_core)
     half = call(

time: 93.5 us -> 92.5 us (0.989)
  transfers between devices with their start and end apart: 12 -> 12, of which waited for: 7 -> 6; matrix products, arithmetic and copies ran while one was open for 0% -> 0% of each run, Pallas kernels for 4% -> 4%
where the time goes in v7:
time: 92.5 us; the launch traced here: 91.8 us
  blocking collectives  35.3 us (38%)
  starting transfers between devices  28.4 us (31%)
  Pallas kernels  13.9 us (15%)
  waiting for transfers between devices  12.5 us (14%)
  local copies, waits for them, and re-layouts  1.43 us (2%)
    all_to_all x1, blocking collectives, per_device(): series = lax.all_to_all(inner, 'seg', 0, 0)  35.3 us
    pallas_call x8, Pallas kernels, call(): pl.pallas_call(kernel, out_shape=outs, in_specs=specs, out_specs=space if...  13.9 us
    ppermute x7, starting transfers between devices, per_device(): pieces.append(lax.ppermute(send, 'tmpl', hop))  12.4 us
    ppermute x7, waiting for transfers between devices, per_device(): pieces.append(lax.ppermute(send, 'tmpl', hop))  11.1 us
    all_to_all x1, starting transfers between devices, per_device(): columns = lax.all_to_all(gated, 'seg', 0, 0)  8.01 us
    all_to_all x1, starting transfers between devices, per_device(): own = lax.all_to_all(turned, 'seg', 0, 0)  7.21 us
  transfers between devices with their start and end apart: 12, of which 6 were waited for; matrix products, arithmetic and copies ran while one was open for 0% of the time, Pallas kernels for 4%

profile of v7, /device:TPU:0, one launch (start us, length us, event | category | flops | bytes accessed | tf_op | source)
XLA Modules:
  0.0 91.8 jit_solution(16543315664939214086)
XLA Ops:
  0.0 4.2 %shard_map.118 = (bf16[8,128,128]{2,1,0:T(8,128)(2,1)}, f32[4,256,128]{2,1,0:T(8,128)}, f32[2,1024,128]{2,1,0:T(8,128)}, bf16[2,2,2,4,16,128]{5,4,3,2,1,0:T(8,12...) custom-call(f32[2,128,1024]{2,1,0:T(8,128)} %strain_ref.1, ...), custom_call_target="tpu_custom_call" | custom-call | flops 100000000 | bytes 4194304 | tf_op jit(solution)/shard_map/pallas_call | solution.py:335
  4.2 8.0 %all-to-all-start = ((bf16[8,128,128]{2,1,0:T(8,128)(2,1)}), bf16[8,128,128]{2,1,0:T(8,128)(2,1)S(1)}, u32[]{:S(2)}, u32[]{:S(2)}) async-start(bf16[8,128,128]{2,1,0:T(8,128)(2,1)} %get-tuple-element.20), calls=%async_computation | async-start | bytes 524288 | tf_op jit(solution)/shard_map/all_to_all | solution.py:369
  12.2 1.0 %collective-permute-start = (bf16[2,2,2,4,16,128]{5,4,3,2,1,0:T(8,128)(2,1)}, bf16[2,2,2,4,16,128]{5,4,3,2,1,0:T(8,128)(2,1)S(1)}, u32[]{:S(2)}, u32[]{:S(2)}) collective-permute-start(bf16[2,2,2,4,16,128]{5,4,3,2,1,0:T(8,128)(2,1)} %get-tuple-element.21), channel_id=1, source_target_pairs={{0,16},{8,24},{16,0},{24,8},{32,48},{40,56},{48,32},{56,40},{64,80... | collective-permute-start | bytes 393224 | tf_op jit(solution)/shard_map/ppermute | solution.py:374
  13.2 3.5 %collective-permute-start.1 = (bf16[2,2,2,4,16,128]{5,4,3,2,1,0:T(8,128)(2,1)}, bf16[2,2,2,4,16,128]{5,4,3,2,1,0:T(8,128)(2,1)S(1)}, u32[]{:S(2)}, u32[]{:S(2)}) collective-permute-start(bf16[2,2,2,4,16,128]{5,4,3,2,1,0:T(8,128)(2,1)} %get-tuple-element.22), channel_id=1, source_target_pairs={{0,80},{8,88},{16,64},{24,72},{32,112},{40,120},{48,96},{56,104},{... | collective-permute-start | bytes 393224 | tf_op jit(solution)/shard_map/ppermute | solution.py:374
  16.7 0.5 collective-permute-start.2
  17.2 5.4 %collective-permute-done.refs_0_.refs_1_ = bf16[2,2,2,4,16,128]{5,4,3,2,1,0:T(8,128)(2,1)S(1)} collective-permute-done((bf16[2,2,2,4,16,128]{5,4,3,2,1,0:T(8,128)(2,1)}, bf16[2,2,2,4,16,128]{5,4,3,2,1,0:T(8,128)(2,1)S(1)}, u32[]{:S(2)}, u32[]{:S(2)}) %collective-permute-start) | collective-permute-done | bytes 131104 | tf_op jit(solution)/shard_map/ppermute | solution.py:374
  22.7 0.0 collective-permute-done.1.refs_1_.refs_2_
  22.7 0.7 collective-permute-done.2.refs_2_.refs_3_
  23.4 0.0 all-to-all-done.cols_ref
  23.4 1.4 %copy-done = f32[368,1024]{1,0:T(8,128)S(1)} copy-done((f32[368,1024]{1,0:T(8,128)S(1)}, f32[368,1024]{1,0:T(8,128)}, u32[]{:S(2)}) %copy-start) | copy-done | bytes 1507352
  24.8 1.6 %shard_map.119 = (bf16[8,2,4,32,128]{4,3,2,1,0:T(8,128)(2,1)}, f32[8,128]{1,0:T(8,128)S(1)}) custom-call(bf16[8,128,128]{2,1,0:T(8,128)(2,1)S(1)} %all-to-all-done.cols_ref, f32[368,1024]{1,0:T(8,128)S(1)} %copy-done, bf16[2,2,2,4,16,128]{5,4,3,2,1,0:T(8,128)(2,1)S(1)} %collective-permute-done.refs_0_.refs_1_, ...), custom_call_target="tpu_custom_call" | custom-call | flops 300000000 | bytes 4194304 | tf_op jit(solution)/shard_map/pallas_call | solution.py:335
  26.4 7.2 %all-to-all-start.1 = ((bf16[8,2,4,32,128]{4,3,2,1,0:T(8,128)(2,1)}), bf16[8,2,4,32,128]{4,3,2,1,0:T(8,128)(2,1)S(1)}, u32[]{:S(2)}, u32[]{:S(2)}) async-start(bf16[8,2,4,32,128]{4,3,2,1,0:T(8,128)(2,1)} %get-tuple-element.24), calls=%async_computation.1 | async-start | bytes 1048576 | tf_op jit(solution)/shard_map/all_to_all | solution.py:388
  33.6 1.7 %collective-permute-start.3 = (bf16[2,2,2,4,16,128]{5,4,3,2,1,0:T(8,128)(2,1)S(1)}, bf16[2,2,2,4,16,128]{5,4,3,2,1,0:T(8,128)(2,1)S(1)}, u32[]{:S(2)}, u32[]{:S(2)}) collective-permute-start(bf16[2,2,2,4,16,128]{5,4,3,2,1,0:T(8,128)(2,1)S(1)} %copy-done.10), channel_id=1, source_target_pairs={{0,48},{8,56},{16,32},{24,40},{32,80},{40,88},{48,64},{56,72},{64,... | collective-permute-start | bytes 393224 | tf_op jit(solution)/shard_map/ppermute | solution.py:374
  35.3 2.5 %collective-permute-start.4 = (bf16[2,2,2,4,16,128]{5,4,3,2,1,0:T(8,128)(2,1)S(1)}, bf16[2,2,2,4,16,128]{5,4,3,2,1,0:T(8,128)(2,1)S(1)}, u32[]{:S(2)}, u32[]{:S(2)}) collective-permute-start(bf16[2,2,2,4,16,128]{5,4,3,2,1,0:T(8,128)(2,1)S(1)} %copy-done.9), channel_id=1, source_target_pairs={{0,112},{8,120},{16,96},{24,104},{32,16},{40,24},{48,0},{56,8},{64... | collective-permute-start | bytes 393224 | tf_op jit(solution)/shard_map/ppermute | solution.py:374
  37.8 3.2 %collective-permute-start.6 = (bf16[2,2,2,4,16,128]{5,4,3,2,1,0:T(8,128)(2,1)S(1)}, bf16[2,2,2,4,16,128]{5,4,3,2,1,0:T(8,128)(2,1)S(1)}, u32[]{:S(2)}, u32[]{:S(2)}) collective-permute-start(bf16[2,2,2,4,16,128]{5,4,3,2,1,0:T(8,128)(2,1)S(1)} %copy-done.7), channel_id=1, source_target_pairs={{0,96},{8,104},{16,112},{24,120},{32,0},{40,8},{48,16},{56,24},{64... | collective-permute-start | bytes 393224 | tf_op jit(solution)/shard_map/ppermute | solution.py:374
  41.0 4.5 %collective-permute-done.3.refs_4_ = bf16[2,2,2,4,16,128]{5,4,3,2,1,0:T(8,128)(2,1)S(1)} collective-permute-done((bf16[2,2,2,4,16,128]{5,4,3,2,1,0:T(8,128)(2,1)S(1)}, bf16[2,2,2,4,16,128]{5,4,3,2,1,0:T(8,128)(2,1)S(1)}, u32[]{:S(2)}, u32[]{:S(2)}) %collective-permute-start.3) | collective-permute-done | bytes 131104 | tf_op jit(solution)/shard_map/ppermute | solution.py:374
  45.5 0.4 collective-permute-done.4.refs_5_
  46.0 0.8 shard_map.120
  46.8 0.1 collective-permute-start.7
  46.8 0.5 collective-permute-start.8
  47.3 1.0 %collective-permute-done.7.after_ref.refs_8_ = bf16[4,2,2,4,16,128]{5,4,3,2,1,0:T(8,128)(2,1)S(1)} collective-permute-done((bf16[4,2,2,4,16,128]{5,4,3,2,1,0:T(8,128)(2,1)S(1)}, bf16[4,2,2,4,16,128]{5,4,3,2,1,0:T(8,128)(2,1)S(1)}, u32[]{:S(2)}, u32[]{:S(2)}) %collective-permute-start.7) | collective-permute-done | bytes 262176 | tf_op jit(solution)/shard_map/ppermute | solution.py:383
  48.4 0.4 collective-permute-done.8.also_ref.refs_9_
  48.8 0.8 shard_map.121.spec
  49.6 0.0 copy-start.2
  49.6 0.0 copy-start.3
  49.6 0.2 collective-permute-start.9
  49.8 1.6 %shard_map.122.bank = bf16[16,2,2,4,16,128]{5,4,3,2,1,0:T(8,128)(2,1)S(1)} custom-call(bf16[2,2,2,4,16,128]{5,4,3,2,1,0:T(8,128)(2,1)S(1)} %copy-done.4, bf16[2,2,2,4,16,128]{5,4,3,2,1,0:T(8,128)(2,1)S(1)} %collective-permute-done.refs_0_.refs_1_, bf16[2,2,2,4,16,128]{5,4,3,2,1,0:T(8,128)(2,1)S(1)} %collective-permute-done.1.refs_1_.refs_2_, ...), custom_call_target="tpu_custom_call" | custom-call | flops 1 | bytes 10485760 | tf_op jit(solution)/shard_map/pallas_call | solution.py:335
  51.5 1.1 %shard_map.123.half_ref = bf16[8,528,128]{2,1,0:T(8,128)(2,1)S(1)} custom-call(f32[2,1024,128]{2,1,0:T(8,128)S(1)} %shard_map.121.spec, f32[4,256,128]{2,1,0:T(8,128)S(1)} %copy-done.5, bf16[4,256,512]{2,1,0:T(8,128)(2,1)S(1)} %copy-done.2, f32[2,1024,128]{2,1,0:T(8,128)S(1)} %copy-done.3, bf16[16,2,2,4,16,128]{5,4,3,2,1,0:T(8,128)(2,1)S(1)} %shard_map.122.bank), custom_call_target="tpu_custom_call" | custom-call | flops 2000000000 | bytes 10485760 | tf_op jit(solution)/shard_map/pallas_call | solution.py:335
  52.6 1.1 %shard_map.124 = bf16[8,1040,128]{2,1,0:T(8,128)(2,1)S(1)} custom-call(f32[2,1024,128]{2,1,0:T(8,128)S(1)} %collective-permute-done.9.spec, f32[4,256,128]{2,1,0:T(8,128)S(1)} %copy-done.5, bf16[4,256,512]{2,1,0:T(8,128)(2,1)S(1)} %copy-done.2, f32[2,1024,128]{2,1,0:T(8,128)S(1)} %copy-done.3, bf16[16,2,2,4,16,128]{5,4,3,2,1,0:T(8,128)(2,1)S(1)} %shard_map.122.bank, ...), custom_call_target="tpu_custom_call" | custom-call | flops 2000000000 | bytes 10485760 | tf_op jit(solution)/shard_map/pallas_call | solution.py:335
  53.8 0.0 copy-start.6
  53.8 35.3 %all_to_all.15.in_ref = bf16[8,1040,128]{2,1,0:T(8,128)(2,1)S(1)} all-to-all(bf16[8,1040,128]{2,1,0:T(8,128)(2,1)S(1)} %shard_map.124), channel_id=1, replica_groups=mesh['tmpl'=16,'seg'=8] {'seg'}, dimensions={0} | all-to-all | bytes 4259840 | tf_op jit(solution)/shard_map/all_to_all | solution.py:404
  89.1 2.7 %shard_map.125 = f32[2,2,1024,128]{3,2,1,0:T(8,128)} custom-call(bf16[8,1040,128]{2,1,0:T(8,128)(2,1)S(1)} %all_to_all.15.in_ref, bf16[4,2,256,256]{3,2,1,0:T(8,128)(2,1)S(1)} %copy-done.6), custom_call_target="tpu_custom_call" | custom-call | flops 3000000000 | bytes 6291456 | tf_op jit(solution)/shard_map/pallas_call | solution.py:335
  (23 shorter events, 0.0 us)
Async XLA Ops:
  4.2 31.1 %copy-start.9 = (bf16[2,2,2,4,16,128]{5,4,3,2,1,0:T(8,128)(2,1)S(1)}, bf16[2,2,2,4,16,128]{5,4,3,2,1,0:T(8,128)(2,1)}, u32[]{:S(2)}) copy-start(bf16[2,2,2,4,16,128]{5,4,3,2,1,0:T(8,128)(2,1)} %get-tuple-element.27) | copy-start | bytes 393220
  4.2 33.6 %copy-start.8 = (bf16[2,2,2,4,16,128]{5,4,3,2,1,0:T(8,128)(2,1)S(1)}, bf16[2,2,2,4,16,128]{5,4,3,2,1,0:T(8,128)(2,1)}, u32[]{:S(2)}) copy-start(bf16[2,2,2,4,16,128]{5,4,3,2,1,0:T(8,128)(2,1)} %get-tuple-element.28) | copy-start | bytes 393220
  4.2 33.6 %copy-start.7 = (bf16[2,2,2,4,16,128]{5,4,3,2,1,0:T(8,128)(2,1)S(1)}, bf16[2,2,2,4,16,128]{5,4,3,2,1,0:T(8,128)(2,1)}, u32[]{:S(2)}) copy-start(bf16[2,2,2,4,16,128]{5,4,3,2,1,0:T(8,128)(2,1)} %get-tuple-element.29) | copy-start | bytes 393220
  4.2 41.8 %copy-start.4 = (bf16[2,2,2,4,16,128]{5,4,3,2,1,0:T(8,128)(2,1)S(1)}, bf16[2,2,2,4,16,128]{5,4,3,2,1,0:T(8,128)(2,1)}, u32[]{:S(2)}) copy-start(bf16[2,2,2,4,16,128]{5,4,3,2,1,0:T(8,128)(2,1)} %get-tuple-element.25.refs_0_) | copy-start | bytes 393220
  4.2 19.2 %all-to-all-start = ((bf16[8,128,128]{2,1,0:T(8,128)(2,1)}), bf16[8,128,128]{2,1,0:T(8,128)(2,1)S(1)}, u32[]{:S(2)}, u32[]{:S(2)}) async-start(bf16[8,128,128]{2,1,0:T(8,128)(2,1)} %get-tuple-element.20), calls=%async_computation | async-start | bytes 524288 | tf_op jit(solution)/shard_map/all_to_all | solution.py:369
  12.2 10.4 %collective-permute-start = (bf16[2,2,2,4,16,128]{5,4,3,2,1,0:T(8,128)(2,1)}, bf16[2,2,2,4,16,128]{5,4,3,2,1,0:T(8,128)(2,1)S(1)}, u32[]{:S(2)}, u32[]{:S(2)}) collective-permute-start(bf16[2,2,2,4,16,128]{5,4,3,2,1,0:T(8,128)(2,1)} %get-tuple-element.21), channel_id=1, source_target_pairs={{0,16},{8,24},{16,0},{24,8},{32,48},{40,56},{48,32},{56,40},{64,80... | collective-permute-start | bytes 393224 | tf_op jit(solution)/shard_map/ppermute | solution.py:374
  13.2 9.4 %collective-permute-start.1 = (bf16[2,2,2,4,16,128]{5,4,3,2,1,0:T(8,128)(2,1)}, bf16[2,2,2,4,16,128]{5,4,3,2,1,0:T(8,128)(2,1)S(1)}, u32[]{:S(2)}, u32[]{:S(2)}) collective-permute-start(bf16[2,2,2,4,16,128]{5,4,3,2,1,0:T(8,128)(2,1)} %get-tuple-element.22), channel_id=1, source_target_pairs={{0,80},{8,88},{16,64},{24,72},{32,112},{40,120},{48,96},{56,104},{... | collective-permute-start | bytes 393224 | tf_op jit(solution)/shard_map/ppermute | solution.py:374
  16.7 6.7 %collective-permute-start.2 = (bf16[2,2,2,4,16,128]{5,4,3,2,1,0:T(8,128)(2,1)}, bf16[2,2,2,4,16,128]{5,4,3,2,1,0:T(8,128)(2,1)S(1)}, u32[]{:S(2)}, u32[]{:S(2)}) collective-permute-start(bf16[2,2,2,4,16,128]{5,4,3,2,1,0:T(8,128)(2,1)} %get-tuple-element.23), channel_id=1, source_target_pairs={{0,64},{8,72},{16,80},{24,88},{32,96},{40,104},{48,112},{56,120},{... | collective-permute-start | bytes 393224 | tf_op jit(solution)/shard_map/ppermute | solution.py:374
  23.4 1.4 %copy-start = (f32[368,1024]{1,0:T(8,128)S(1)}, f32[368,1024]{1,0:T(8,128)}, u32[]{:S(2)}) copy-start(f32[368,1024]{1,0:T(8,128)} %constant.12.clone.table_ref) | copy-start | bytes 4521988
  24.8 8.8 %copy-start.10 = (bf16[2,2,2,4,16,128]{5,4,3,2,1,0:T(8,128)(2,1)S(1)}, bf16[2,2,2,4,16,128]{5,4,3,2,1,0:T(8,128)(2,1)}, u32[]{:S(2)}) copy-start(bf16[2,2,2,4,16,128]{5,4,3,2,1,0:T(8,128)(2,1)} %get-tuple-element.26) | copy-start | bytes 393220
  24.8 24.0 %copy-start.1 = (f32[256,1152]{1,0:T(8,128)S(1)}, f32[256,1152]{1,0:T(8,128)}, u32[]{:S(2)}) copy-start(f32[256,1152]{1,0:T(8,128)} %constant.13.clone.table_ref) | copy-start | bytes 3538948
  26.4 22.4 %all-to-all-start.1 = ((bf16[8,2,4,32,128]{4,3,2,1,0:T(8,128)(2,1)}), bf16[8,2,4,32,128]{4,3,2,1,0:T(8,128)(2,1)S(1)}, u32[]{:S(2)}, u32[]{:S(2)}) async-start(bf16[8,2,4,32,128]{4,3,2,1,0:T(8,128)(2,1)} %get-tuple-element.24), calls=%async_computation.1 | async-start | bytes 1048576 | tf_op jit(solution)/shard_map/all_to_all | solution.py:388
  33.6 11.9 %collective-permute-start.3 = (bf16[2,2,2,4,16,128]{5,4,3,2,1,0:T(8,128)(2,1)S(1)}, bf16[2,2,2,4,16,128]{5,4,3,2,1,0:T(8,128)(2,1)S(1)}, u32[]{:S(2)}, u32[]{:S(2)}) collective-permute-start(bf16[2,2,2,4,16,128]{5,4,3,2,1,0:T(8,128)(2,1)S(1)} %copy-done.10), channel_id=1, source_target_pairs={{0,48},{8,56},{16,32},{24,40},{32,80},{40,88},{48,64},{56,72},{64,... | collective-permute-start | bytes 393224 | tf_op jit(solution)/shard_map/ppermute | solution.py:374
  35.3 10.7 %collective-permute-start.4 = (bf16[2,2,2,4,16,128]{5,4,3,2,1,0:T(8,128)(2,1)S(1)}, bf16[2,2,2,4,16,128]{5,4,3,2,1,0:T(8,128)(2,1)S(1)}, u32[]{:S(2)}, u32[]{:S(2)}) collective-permute-start(bf16[2,2,2,4,16,128]{5,4,3,2,1,0:T(8,128)(2,1)S(1)} %copy-done.9), channel_id=1, source_target_pairs={{0,112},{8,120},{16,96},{24,104},{32,16},{40,24},{48,0},{56,8},{64... | collective-permute-start | bytes 393224 | tf_op jit(solution)/shard_map/ppermute | solution.py:374
  37.8 8.2 %collective-permute-start.5 = (bf16[2,2,2,4,16,128]{5,4,3,2,1,0:T(8,128)(2,1)S(1)}, bf16[2,2,2,4,16,128]{5,4,3,2,1,0:T(8,128)(2,1)S(1)}, u32[]{:S(2)}, u32[]{:S(2)}) collective-permute-start(bf16[2,2,2,4,16,128]{5,4,3,2,1,0:T(8,128)(2,1)S(1)} %copy-done.8), channel_id=1, source_target_pairs={{0,32},{8,40},{16,48},{24,56},{32,64},{40,72},{48,80},{56,88},{64,... | collective-permute-start | bytes 393224 | tf_op jit(solution)/shard_map/ppermute | solution.py:374
  37.8 8.2 %collective-permute-start.6 = (bf16[2,2,2,4,16,128]{5,4,3,2,1,0:T(8,128)(2,1)S(1)}, bf16[2,2,2,4,16,128]{5,4,3,2,1,0:T(8,128)(2,1)S(1)}, u32[]{:S(2)}, u32[]{:S(2)}) collective-permute-start(bf16[2,2,2,4,16,128]{5,4,3,2,1,0:T(8,128)(2,1)S(1)} %copy-done.7), channel_id=1, source_target_pairs={{0,96},{8,104},{16,112},{24,120},{32,0},{40,8},{48,16},{56,24},{64... | collective-permute-start | bytes 393224 | tf_op jit(solution)/shard_map/ppermute | solution.py:374
  46.8 1.6 %collective-permute-start.7 = (bf16[4,2,2,4,16,128]{5,4,3,2,1,0:T(8,128)(2,1)S(1)}, bf16[4,2,2,4,16,128]{5,4,3,2,1,0:T(8,128)(2,1)S(1)}, u32[]{:S(2)}, u32[]{:S(2)}) collective-permute-start(bf16[4,2,2,4,16,128]{5,4,3,2,1,0:T(8,128)(2,1)S(1)} %get-tuple-element.31), channel_id=1, source_target_pairs={{0,8},{8,0},{16,24},{24,16},{32,40},{40,32},{48,56},{56,48},{64,72... | collective-permute-start | bytes 786440 | tf_op jit(solution)/shard_map/ppermute | solution.py:383
  46.8 1.9 %collective-permute-start.8 = (bf16[4,2,2,4,16,128]{5,4,3,2,1,0:T(8,128)(2,1)S(1)}, bf16[4,2,2,4,16,128]{5,4,3,2,1,0:T(8,128)(2,1)S(1)}, u32[]{:S(2)}, u32[]{:S(2)}) collective-permute-start(bf16[4,2,2,4,16,128]{5,4,3,2,1,0:T(8,128)(2,1)S(1)} %get-tuple-element.32), channel_id=1, source_target_pairs={{0,8},{8,0},{16,24},{24,16},{32,40},{40,32},{48,56},{56,48},{64,72... | collective-permute-start | bytes 786440 | tf_op jit(solution)/shard_map/ppermute | solution.py:383
  49.6 1.9 %copy-start.2 = (bf16[4,256,512]{2,1,0:T(8,128)(2,1)S(1)}, bf16[4,256,512]{2,1,0:T(8,128)(2,1)}, u32[]{:S(2)}) copy-start(bf16[4,256,512]{2,1,0:T(8,128)(2,1)} %constant.14.clone.third_ref) | copy-start | bytes 3145732
  49.6 1.9 %copy-start.3 = (f32[2,1024,128]{2,1,0:T(8,128)S(1)}, f32[2,1024,128]{2,1,0:T(8,128)}, u32[]{:S(2)}) copy-start(f32[2,1024,128]{2,1,0:T(8,128)} %get-tuple-element.34.twist) | copy-start | bytes 3145732
  49.6 1.9 %copy-start.5 = (f32[4,256,128]{2,1,0:T(8,128)S(1)}, f32[4,256,128]{2,1,0:T(8,128)}, u32[]{:S(2)}) copy-start(f32[4,256,128]{2,1,0:T(8,128)} %get-tuple-element.33.weight_ref) | copy-start | bytes 1572868
  49.6 3.0 %collective-permute-start.9 = (f32[2,1024,128]{2,1,0:T(8,128)S(1)}, f32[2,1024,128]{2,1,0:T(8,128)S(1)}, u32[]{:S(2)}, u32[]{:S(2)}) collective-permute-start(f32[2,1024,128]{2,1,0:T(8,128)S(1)} %shard_map.121.spec), channel_id=1, source_target_pairs={{0,8},{8,0},{16,24},{24,16},{32,40},{40,32},{48,56},{56,48},{64,72... | collective-permute-start | bytes 3145736 | tf_op jit(solution)/shard_map/ppermute | solution.py:393
  53.8 35.3 %copy-start.6 = (bf16[4,2,256,256]{3,2,1,0:T(8,128)(2,1)S(1)}, bf16[4,2,256,256]{3,2,1,0:T(8,128)(2,1)}, u32[]{:S(2)}) copy-start(bf16[4,2,256,256]{3,2,1,0:T(8,128)(2,1)} %constant.17.clone.table_ref) | copy-start | bytes 3145732

commit v8 on v7

--- a/solution.py
+++ b/solution.py
@@ -153,8 +153,8 @@
 
 
 def pack_kernel(*refs):
-    piece_refs, out_refs, sems = refs[:8], refs[9:11], refs[11]
-    copies = [pltpu.make_async_copy(piece_refs[i].at[1], out_refs[i // 4].at[i % 4], sems.at[i]) for i in range(8)]
+    piece_refs, _, out_ref, sems = refs[:4], *refs[4:]
+    copies = [pltpu.make_async_copy(piece_refs[i].at[1], out_ref.at[i], sems.at[i]) for i in range(4)]
     for copy in copies:
         copy.start()
     for copy in copies:
@@ -376,10 +376,13 @@
         first_kernel, (columns, const["first"], *pieces[1:4]), (shape(8, 2, 4, 32, 128), shape(8, 128, dtype=F32)),
         [VMEM] * 2 + [ANY] * 3, 3 * 10**8, 4 * MIB, [pltpu.VMEM((512, 512), F32)],
     )
-    crosses = call(
-        pack_kernel, (*pieces, token), (shape(4, *blk),) * 2, [ANY] * 9, 1, MIB, [pltpu.SemaphoreType.DMA((8,))],
-        limit=8, space=(ANY,) * 2,
-    )
+    crosses = [
+        call(
+            pack_kernel, (*pieces[i : i + 4], token), shape(4, *blk), [ANY] * 5, 1, MIB,
+            [pltpu.SemaphoreType.DMA((4,))], limit=8, space=ANY,
+        )
+        for i in (0, 4)
+    ]
     crossed = [lax.ppermute(cross, "tmpl", swap_core) for cross in crosses]
     ordered = call(
         assemble_kernel, (*pieces, *crossed), shape(16, *blk), [ANY] * 10, 1, 10 * MIB,

time: 92.5 us -> 91.7 us (level)
    pallas_call x8 -> x9, Pallas kernels: 13.9 us -> 13.9 us  [call(): pl.pallas_call(kernel, out_shape=outs, in_specs=specs, out_specs=space if...]
where the time goes in v8:
time: 91.7 us; the launch traced here: 91 us
  blocking collectives  34.6 us (38%)
  starting transfers between devices  27.9 us (30%)
  Pallas kernels  13.9 us (15%)
  waiting for transfers between devices  12.9 us (14%)
  local copies, waits for them, and re-layouts  1.43 us (2%)
    all_to_all x1, blocking collectives, per_device(): series = lax.all_to_all(inner, 'seg', 0, 0)  34.6 us
    pallas_call x9, Pallas kernels, call(): pl.pallas_call(kernel, out_shape=outs, in_specs=specs, out_specs=space if...  13.9 us
    ppermute x7, starting transfers between devices, per_device(): pieces.append(lax.ppermute(send, 'tmpl', hop))  12.4 us
    ppermute x7, waiting for transfers between devices, per_device(): pieces.append(lax.ppermute(send, 'tmpl', hop))  10.7 us
    all_to_all x1, starting transfers between devices, per_device(): columns = lax.all_to_all(gated, 'seg', 0, 0)  8.01 us
    all_to_all x1, starting transfers between devices, per_device(): own = lax.all_to_all(turned, 'seg', 0, 0)  7.21 us
  transfers between devices with their start and end apart: 12, of which 6 were waited for; matrix products, arithmetic and copies ran while one was open for 0% of the time, Pallas kernels for 4%

profile of v8, /device:TPU:0, one launch (start us, length us, event | category | flops | bytes accessed | tf_op | source)
XLA Modules:
  0.0 91.0 jit_solution(1163838775021465050)
XLA Ops:
  0.0 4.2 %shard_map.118 = (bf16[8,128,128]{2,1,0:T(8,128)(2,1)}, f32[4,256,128]{2,1,0:T(8,128)}, f32[2,1024,128]{2,1,0:T(8,128)}, bf16[2,2,2,4,16,128]{5,4,3,2,1,0:T(8,12...) custom-call(f32[2,128,1024]{2,1,0:T(8,128)} %strain_ref.1, ...), custom_call_target="tpu_custom_call" | custom-call | flops 100000000 | bytes 4194304 | tf_op jit(solution)/shard_map/pallas_call | solution.py:335
  4.2 8.0 %all-to-all-start = ((bf16[8,128,128]{2,1,0:T(8,128)(2,1)}), bf16[8,128,128]{2,1,0:T(8,128)(2,1)S(1)}, u32[]{:S(2)}, u32[]{:S(2)}) async-start(bf16[8,128,128]{2,1,0:T(8,128)(2,1)} %get-tuple-element.18), calls=%async_computation | async-start | bytes 524288 | tf_op jit(solution)/shard_map/all_to_all | solution.py:369
  12.2 1.0 %collective-permute-start = (bf16[2,2,2,4,16,128]{5,4,3,2,1,0:T(8,128)(2,1)}, bf16[2,2,2,4,16,128]{5,4,3,2,1,0:T(8,128)(2,1)S(1)}, u32[]{:S(2)}, u32[]{:S(2)}) collective-permute-start(bf16[2,2,2,4,16,128]{5,4,3,2,1,0:T(8,128)(2,1)} %get-tuple-element.19), channel_id=1, source_target_pairs={{0,16},{8,24},{16,0},{24,8},{32,48},{40,56},{48,32},{56,40},{64,80... | collective-permute-start | bytes 393224 | tf_op jit(solution)/shard_map/ppermute | solution.py:374
  13.2 3.5 %collective-permute-start.1 = (bf16[2,2,2,4,16,128]{5,4,3,2,1,0:T(8,128)(2,1)}, bf16[2,2,2,4,16,128]{5,4,3,2,1,0:T(8,128)(2,1)S(1)}, u32[]{:S(2)}, u32[]{:S(2)}) collective-permute-start(bf16[2,2,2,4,16,128]{5,4,3,2,1,0:T(8,128)(2,1)} %get-tuple-element.20), channel_id=1, source_target_pairs={{0,80},{8,88},{16,64},{24,72},{32,112},{40,120},{48,96},{56,104},{... | collective-permute-start | bytes 393224 | tf_op jit(solution)/shard_map/ppermute | solution.py:374
  16.7 0.5 collective-permute-start.2
  17.2 5.4 %collective-permute-done.refs_0_.refs_1_ = bf16[2,2,2,4,16,128]{5,4,3,2,1,0:T(8,128)(2,1)S(1)} collective-permute-done((bf16[2,2,2,4,16,128]{5,4,3,2,1,0:T(8,128)(2,1)}, bf16[2,2,2,4,16,128]{5,4,3,2,1,0:T(8,128)(2,1)S(1)}, u32[]{:S(2)}, u32[]{:S(2)}) %collective-permute-start) | collective-permute-done | bytes 131104 | tf_op jit(solution)/shard_map/ppermute | solution.py:374
  22.7 0.0 collective-permute-done.1.refs_1_.refs_2_
  22.7 0.7 collective-permute-done.2.refs_2_.refs_3_
  23.4 1.4 %copy-done = f32[368,1024]{1,0:T(8,128)S(1)} copy-done((f32[368,1024]{1,0:T(8,128)S(1)}, f32[368,1024]{1,0:T(8,128)}, u32[]{:S(2)}) %copy-start) | copy-done | bytes 1507352
  24.8 1.6 %shard_map.119 = (bf16[8,2,4,32,128]{4,3,2,1,0:T(8,128)(2,1)}, f32[8,128]{1,0:T(8,128)S(1)}) custom-call(bf16[8,128,128]{2,1,0:T(8,128)(2,1)S(1)} %all-to-all-done.cols_ref, f32[368,1024]{1,0:T(8,128)S(1)} %copy-done, bf16[2,2,2,4,16,128]{5,4,3,2,1,0:T(8,128)(2,1)S(1)} %collective-permute-done.refs_0_.refs_1_, ...), custom_call_target="tpu_custom_call" | custom-call | flops 300000000 | bytes 4194304 | tf_op jit(solution)/shard_map/pallas_call | solution.py:335
  26.4 7.2 %all-to-all-start.1 = ((bf16[8,2,4,32,128]{4,3,2,1,0:T(8,128)(2,1)}), bf16[8,2,4,32,128]{4,3,2,1,0:T(8,128)(2,1)S(1)}, u32[]{:S(2)}, u32[]{:S(2)}) async-start(bf16[8,2,4,32,128]{4,3,2,1,0:T(8,128)(2,1)} %get-tuple-element.22), calls=%async_computation.1 | async-start | bytes 1048576 | tf_op jit(solution)/shard_map/all_to_all | solution.py:391
  33.6 1.7 %collective-permute-start.4 = (bf16[2,2,2,4,16,128]{5,4,3,2,1,0:T(8,128)(2,1)S(1)}, bf16[2,2,2,4,16,128]{5,4,3,2,1,0:T(8,128)(2,1)S(1)}, u32[]{:S(2)}, u32[]{:S(2)}) collective-permute-start(bf16[2,2,2,4,16,128]{5,4,3,2,1,0:T(8,128)(2,1)S(1)} %copy-done.10), channel_id=1, source_target_pairs={{0,48},{8,56},{16,32},{24,40},{32,80},{40,88},{48,64},{56,72},{64,... | collective-permute-start | bytes 393224 | tf_op jit(solution)/shard_map/ppermute | solution.py:374
  35.3 2.5 %collective-permute-start.5 = (bf16[2,2,2,4,16,128]{5,4,3,2,1,0:T(8,128)(2,1)S(1)}, bf16[2,2,2,4,16,128]{5,4,3,2,1,0:T(8,128)(2,1)S(1)}, u32[]{:S(2)}, u32[]{:S(2)}) collective-permute-start(bf16[2,2,2,4,16,128]{5,4,3,2,1,0:T(8,128)(2,1)S(1)} %copy-done.9), channel_id=1, source_target_pairs={{0,112},{8,120},{16,96},{24,104},{32,16},{40,24},{48,0},{56,8},{64... | collective-permute-start | bytes 393224 | tf_op jit(solution)/shard_map/ppermute | solution.py:374
  37.8 3.2 %collective-permute-start.7 = (bf16[2,2,2,4,16,128]{5,4,3,2,1,0:T(8,128)(2,1)S(1)}, bf16[2,2,2,4,16,128]{5,4,3,2,1,0:T(8,128)(2,1)S(1)}, u32[]{:S(2)}, u32[]{:S(2)}) collective-permute-start(bf16[2,2,2,4,16,128]{5,4,3,2,1,0:T(8,128)(2,1)S(1)} %copy-done.7), channel_id=1, source_target_pairs={{0,96},{8,104},{16,112},{24,120},{32,0},{40,8},{48,16},{56,24},{64... | collective-permute-start | bytes 393224 | tf_op jit(solution)/shard_map/ppermute | solution.py:374
  41.0 0.4 shard_map.120
  41.4 0.1 collective-permute-start.3
  41.5 4.0 %collective-permute-done.4.refs_0_.refs_4_ = bf16[2,2,2,4,16,128]{5,4,3,2,1,0:T(8,128)(2,1)S(1)} collective-permute-done((bf16[2,2,2,4,16,128]{5,4,3,2,1,0:T(8,128)(2,1)S(1)}, bf16[2,2,2,4,16,128]{5,4,3,2,1,0:T(8,128)(2,1)S(1)}, u32[]{:S(2)}, u32[]{:S(2)}) %collective-permute-start.4) | collective-permute-done | bytes 131104 | tf_op jit(solution)/shard_map/ppermute | solution.py:374
  45.5 0.4 collective-permute-done.5.refs_1_.refs_5_
  46.0 0.4 shard_map.121
  46.4 0.1 collective-permute-start.8
  46.5 1.5 %collective-permute-done.8.also_ref.refs_9_ = bf16[4,2,2,4,16,128]{5,4,3,2,1,0:T(8,128)(2,1)S(1)} collective-permute-done((bf16[4,2,2,4,16,128]{5,4,3,2,1,0:T(8,128)(2,1)S(1)}, bf16[4,2,2,4,16,128]{5,4,3,2,1,0:T(8,128)(2,1)S(1)}, u32[]{:S(2)}, u32[]{:S(2)}) %collective-permute-start.8) | collective-permute-done | bytes 262176 | tf_op jit(solution)/shard_map/ppermute | solution.py:386
  48.0 0.7 all-to-all-done.1.own_ref
  48.7 0.8 shard_map.122.spec
  49.5 0.0 copy-start.2
  49.5 0.0 copy-start.3
  49.5 0.1 collective-permute-start.9
  49.6 1.7 %shard_map.123.bank = bf16[16,2,2,4,16,128]{5,4,3,2,1,0:T(8,128)(2,1)S(1)} custom-call(bf16[2,2,2,4,16,128]{5,4,3,2,1,0:T(8,128)(2,1)S(1)} %copy-done.4, bf16[2,2,2,4,16,128]{5,4,3,2,1,0:T(8,128)(2,1)S(1)} %collective-permute-done.refs_0_.refs_1_, bf16[2,2,2,4,16,128]{5,4,3,2,1,0:T(8,128)(2,1)S(1)} %collective-permute-done.1.refs_1_.refs_2_, ...), custom_call_target="tpu_custom_call" | custom-call | flops 1 | bytes 10485760 | tf_op jit(solution)/shard_map/pallas_call | solution.py:335
  51.4 1.1 %shard_map.124.half_ref = bf16[8,528,128]{2,1,0:T(8,128)(2,1)S(1)} custom-call(f32[2,1024,128]{2,1,0:T(8,128)S(1)} %shard_map.122.spec, f32[4,256,128]{2,1,0:T(8,128)S(1)} %copy-done.5, bf16[4,256,512]{2,1,0:T(8,128)(2,1)S(1)} %copy-done.2, f32[2,1024,128]{2,1,0:T(8,128)S(1)} %copy-done.3, bf16[16,2,2,4,16,128]{5,4,3,2,1,0:T(8,128)(2,1)S(1)} %shard_map.123.bank), custom_call_target="tpu_custom_call" | custom-call | flops 2000000000 | bytes 10485760 | tf_op jit(solution)/shard_map/pallas_call | solution.py:335
  52.5 1.1 %shard_map.125 = bf16[8,1040,128]{2,1,0:T(8,128)(2,1)S(1)} custom-call(f32[2,1024,128]{2,1,0:T(8,128)S(1)} %collective-permute-done.9.spec, f32[4,256,128]{2,1,0:T(8,128)S(1)} %copy-done.5, bf16[4,256,512]{2,1,0:T(8,128)(2,1)S(1)} %copy-done.2, f32[2,1024,128]{2,1,0:T(8,128)S(1)} %copy-done.3, bf16[16,2,2,4,16,128]{5,4,3,2,1,0:T(8,128)(2,1)S(1)} %shard_map.123.bank, ...), custom_call_target="tpu_custom_call" | custom-call | flops 2000000000 | bytes 10485760 | tf_op jit(solution)/shard_map/pallas_call | solution.py:335
  53.7 0.0 copy-start.6
  53.7 34.6 %all_to_all.15.in_ref = bf16[8,1040,128]{2,1,0:T(8,128)(2,1)S(1)} all-to-all(bf16[8,1040,128]{2,1,0:T(8,128)(2,1)S(1)} %shard_map.125), channel_id=1, replica_groups=mesh['tmpl'=16,'seg'=8] {'seg'}, dimensions={0} | all-to-all | bytes 4259840 | tf_op jit(solution)/shard_map/all_to_all | solution.py:407
  88.3 2.7 %shard_map.126 = f32[2,2,1024,128]{3,2,1,0:T(8,128)} custom-call(bf16[8,1040,128]{2,1,0:T(8,128)(2,1)S(1)} %all_to_all.15.in_ref, bf16[4,2,256,256]{3,2,1,0:T(8,128)(2,1)S(1)} %copy-done.6), custom_call_target="tpu_custom_call" | custom-call | flops 3000000000 | bytes 6291456 | tf_op jit(solution)/shard_map/pallas_call | solution.py:335
  (24 shorter events, 0.1 us)
Async XLA Ops:
  4.2 31.1 %copy-start.9 = (bf16[2,2,2,4,16,128]{5,4,3,2,1,0:T(8,128)(2,1)S(1)}, bf16[2,2,2,4,16,128]{5,4,3,2,1,0:T(8,128)(2,1)}, u32[]{:S(2)}) copy-start(bf16[2,2,2,4,16,128]{5,4,3,2,1,0:T(8,128)(2,1)} %get-tuple-element.26) | copy-start | bytes 393220
  4.2 33.6 %copy-start.8 = (bf16[2,2,2,4,16,128]{5,4,3,2,1,0:T(8,128)(2,1)S(1)}, bf16[2,2,2,4,16,128]{5,4,3,2,1,0:T(8,128)(2,1)}, u32[]{:S(2)}) copy-start(bf16[2,2,2,4,16,128]{5,4,3,2,1,0:T(8,128)(2,1)} %get-tuple-element.27) | copy-start | bytes 393220
  4.2 33.6 %copy-start.7 = (bf16[2,2,2,4,16,128]{5,4,3,2,1,0:T(8,128)(2,1)S(1)}, bf16[2,2,2,4,16,128]{5,4,3,2,1,0:T(8,128)(2,1)}, u32[]{:S(2)}) copy-start(bf16[2,2,2,4,16,128]{5,4,3,2,1,0:T(8,128)(2,1)} %get-tuple-element.28) | copy-start | bytes 393220
  4.2 36.8 %copy-start.4 = (bf16[2,2,2,4,16,128]{5,4,3,2,1,0:T(8,128)(2,1)S(1)}, bf16[2,2,2,4,16,128]{5,4,3,2,1,0:T(8,128)(2,1)}, u32[]{:S(2)}) copy-start(bf16[2,2,2,4,16,128]{5,4,3,2,1,0:T(8,128)(2,1)} %get-tuple-element.23.refs_0_) | copy-start | bytes 393220
  4.2 19.2 %all-to-all-start = ((bf16[8,128,128]{2,1,0:T(8,128)(2,1)}), bf16[8,128,128]{2,1,0:T(8,128)(2,1)S(1)}, u32[]{:S(2)}, u32[]{:S(2)}) async-start(bf16[8,128,128]{2,1,0:T(8,128)(2,1)} %get-tuple-element.18), calls=%async_computation | async-start | bytes 524288 | tf_op jit(solution)/shard_map/all_to_all | solution.py:369
  12.2 10.4 %collective-permute-start = (bf16[2,2,2,4,16,128]{5,4,3,2,1,0:T(8,128)(2,1)}, bf16[2,2,2,4,16,128]{5,4,3,2,1,0:T(8,128)(2,1)S(1)}, u32[]{:S(2)}, u32[]{:S(2)}) collective-permute-start(bf16[2,2,2,4,16,128]{5,4,3,2,1,0:T(8,128)(2,1)} %get-tuple-element.19), channel_id=1, source_target_pairs={{0,16},{8,24},{16,0},{24,8},{32,48},{40,56},{48,32},{56,40},{64,80... | collective-permute-start | bytes 393224 | tf_op jit(solution)/shard_map/ppermute | solution.py:374
  13.2 9.4 %collective-permute-start.1 = (bf16[2,2,2,4,16,128]{5,4,3,2,1,0:T(8,128)(2,1)}, bf16[2,2,2,4,16,128]{5,4,3,2,1,0:T(8,128)(2,1)S(1)}, u32[]{:S(2)}, u32[]{:S(2)}) collective-permute-start(bf16[2,2,2,4,16,128]{5,4,3,2,1,0:T(8,128)(2,1)} %get-tuple-element.20), channel_id=1, source_target_pairs={{0,80},{8,88},{16,64},{24,72},{32,112},{40,120},{48,96},{56,104},{... | collective-permute-start | bytes 393224 | tf_op jit(solution)/shard_map/ppermute | solution.py:374
  16.7 6.7 %collective-permute-start.2 = (bf16[2,2,2,4,16,128]{5,4,3,2,1,0:T(8,128)(2,1)}, bf16[2,2,2,4,16,128]{5,4,3,2,1,0:T(8,128)(2,1)S(1)}, u32[]{:S(2)}, u32[]{:S(2)}) collective-permute-start(bf16[2,2,2,4,16,128]{5,4,3,2,1,0:T(8,128)(2,1)} %get-tuple-element.21), channel_id=1, source_target_pairs={{0,64},{8,72},{16,80},{24,88},{32,96},{40,104},{48,112},{56,120},{... | collective-permute-start | bytes 393224 | tf_op jit(solution)/shard_map/ppermute | solution.py:374
  23.4 1.4 %copy-start = (f32[368,1024]{1,0:T(8,128)S(1)}, f32[368,1024]{1,0:T(8,128)}, u32[]{:S(2)}) copy-start(f32[368,1024]{1,0:T(8,128)} %constant.12.clone.table_ref) | copy-start | bytes 4521988
  24.8 8.8 %copy-start.10 = (bf16[2,2,2,4,16,128]{5,4,3,2,1,0:T(8,128)(2,1)S(1)}, bf16[2,2,2,4,16,128]{5,4,3,2,1,0:T(8,128)(2,1)}, u32[]{:S(2)}) copy-start(bf16[2,2,2,4,16,128]{5,4,3,2,1,0:T(8,128)(2,1)} %get-tuple-element.25) | copy-start | bytes 393220
  24.8 23.9 %copy-start.1 = (f32[256,1152]{1,0:T(8,128)S(1)}, f32[256,1152]{1,0:T(8,128)}, u32[]{:S(2)}) copy-start(f32[256,1152]{1,0:T(8,128)} %constant.13.clone.table_ref) | copy-start | bytes 3538948
  26.4 22.3 %all-to-all-start.1 = ((bf16[8,2,4,32,128]{4,3,2,1,0:T(8,128)(2,1)}), bf16[8,2,4,32,128]{4,3,2,1,0:T(8,128)(2,1)S(1)}, u32[]{:S(2)}, u32[]{:S(2)}) async-start(bf16[8,2,4,32,128]{4,3,2,1,0:T(8,128)(2,1)} %get-tuple-element.22), calls=%async_computation.1 | async-start | bytes 1048576 | tf_op jit(solution)/shard_map/all_to_all | solution.py:391
  33.6 11.9 %collective-permute-start.4 = (bf16[2,2,2,4,16,128]{5,4,3,2,1,0:T(8,128)(2,1)S(1)}, bf16[2,2,2,4,16,128]{5,4,3,2,1,0:T(8,128)(2,1)S(1)}, u32[]{:S(2)}, u32[]{:S(2)}) collective-permute-start(bf16[2,2,2,4,16,128]{5,4,3,2,1,0:T(8,128)(2,1)S(1)} %copy-done.10), channel_id=1, source_target_pairs={{0,48},{8,56},{16,32},{24,40},{32,80},{40,88},{48,64},{56,72},{64,... | collective-permute-start | bytes 393224 | tf_op jit(solution)/shard_map/ppermute | solution.py:374
  35.3 10.7 %collective-permute-start.5 = (bf16[2,2,2,4,16,128]{5,4,3,2,1,0:T(8,128)(2,1)S(1)}, bf16[2,2,2,4,16,128]{5,4,3,2,1,0:T(8,128)(2,1)S(1)}, u32[]{:S(2)}, u32[]{:S(2)}) collective-permute-start(bf16[2,2,2,4,16,128]{5,4,3,2,1,0:T(8,128)(2,1)S(1)} %copy-done.9), channel_id=1, source_target_pairs={{0,112},{8,120},{16,96},{24,104},{32,16},{40,24},{48,0},{56,8},{64... | collective-permute-start | bytes 393224 | tf_op jit(solution)/shard_map/ppermute | solution.py:374
  37.8 8.2 %collective-permute-start.6 = (bf16[2,2,2,4,16,128]{5,4,3,2,1,0:T(8,128)(2,1)S(1)}, bf16[2,2,2,4,16,128]{5,4,3,2,1,0:T(8,128)(2,1)S(1)}, u32[]{:S(2)}, u32[]{:S(2)}) collective-permute-start(bf16[2,2,2,4,16,128]{5,4,3,2,1,0:T(8,128)(2,1)S(1)} %copy-done.8), channel_id=1, source_target_pairs={{0,32},{8,40},{16,48},{24,56},{32,64},{40,72},{48,80},{56,88},{64,... | collective-permute-start | bytes 393224 | tf_op jit(solution)/shard_map/ppermute | solution.py:374
  37.8 8.2 %collective-permute-start.7 = (bf16[2,2,2,4,16,128]{5,4,3,2,1,0:T(8,128)(2,1)S(1)}, bf16[2,2,2,4,16,128]{5,4,3,2,1,0:T(8,128)(2,1)S(1)}, u32[]{:S(2)}, u32[]{:S(2)}) collective-permute-start(bf16[2,2,2,4,16,128]{5,4,3,2,1,0:T(8,128)(2,1)S(1)} %copy-done.7), channel_id=1, source_target_pairs={{0,96},{8,104},{16,112},{24,120},{32,0},{40,8},{48,16},{56,24},{64... | collective-permute-start | bytes 393224 | tf_op jit(solution)/shard_map/ppermute | solution.py:374
  41.4 5.1 %collective-permute-start.3 = (bf16[4,2,2,4,16,128]{5,4,3,2,1,0:T(8,128)(2,1)S(1)}, bf16[4,2,2,4,16,128]{5,4,3,2,1,0:T(8,128)(2,1)S(1)}, u32[]{:S(2)}, u32[]{:S(2)}) collective-permute-start(bf16[4,2,2,4,16,128]{5,4,3,2,1,0:T(8,128)(2,1)S(1)} %shard_map.120), channel_id=1, source_target_pairs={{0,8},{8,0},{16,24},{24,16},{32,40},{40,32},{48,56},{56,48},{64,72... | collective-permute-start | bytes 786440 | tf_op jit(solution)/shard_map/ppermute | solution.py:386
  46.4 1.6 %collective-permute-start.8 = (bf16[4,2,2,4,16,128]{5,4,3,2,1,0:T(8,128)(2,1)S(1)}, bf16[4,2,2,4,16,128]{5,4,3,2,1,0:T(8,128)(2,1)S(1)}, u32[]{:S(2)}, u32[]{:S(2)}) collective-permute-start(bf16[4,2,2,4,16,128]{5,4,3,2,1,0:T(8,128)(2,1)S(1)} %shard_map.121), channel_id=1, source_target_pairs={{0,8},{8,0},{16,24},{24,16},{32,40},{40,32},{48,56},{56,48},{64,72... | collective-permute-start | bytes 786440 | tf_op jit(solution)/shard_map/ppermute | solution.py:386
  49.5 1.8 %copy-start.2 = (bf16[4,256,512]{2,1,0:T(8,128)(2,1)S(1)}, bf16[4,256,512]{2,1,0:T(8,128)(2,1)}, u32[]{:S(2)}) copy-start(bf16[4,256,512]{2,1,0:T(8,128)(2,1)} %constant.14.clone.third_ref) | copy-start | bytes 3145732
  49.5 1.8 %copy-start.3 = (f32[2,1024,128]{2,1,0:T(8,128)S(1)}, f32[2,1024,128]{2,1,0:T(8,128)}, u32[]{:S(2)}) copy-start(f32[2,1024,128]{2,1,0:T(8,128)} %get-tuple-element.30.twist) | copy-start | bytes 3145732
  49.5 1.8 %copy-start.5 = (f32[4,256,128]{2,1,0:T(8,128)S(1)}, f32[4,256,128]{2,1,0:T(8,128)}, u32[]{:S(2)}) copy-start(f32[4,256,128]{2,1,0:T(8,128)} %get-tuple-element.29.weight_ref) | copy-start | bytes 1572868
  49.5 3.0 %collective-permute-start.9 = (f32[2,1024,128]{2,1,0:T(8,128)S(1)}, f32[2,1024,128]{2,1,0:T(8,128)S(1)}, u32[]{:S(2)}, u32[]{:S(2)}) collective-permute-start(f32[2,1024,128]{2,1,0:T(8,128)S(1)} %shard_map.122.spec), channel_id=1, source_target_pairs={{0,8},{8,0},{16,24},{24,16},{32,40},{40,32},{48,56},{56,48},{64,72... | collective-permute-start | bytes 3145736 | tf_op jit(solution)/shard_map/ppermute | solution.py:396
  53.7 34.6 %copy-start.6 = (bf16[4,2,256,256]{3,2,1,0:T(8,128)(2,1)S(1)}, bf16[4,2,256,256]{3,2,1,0:T(8,128)(2,1)}, u32[]{:S(2)}) copy-start(bf16[4,2,256,256]{3,2,1,0:T(8,128)(2,1)} %constant.17.clone.table_ref) | copy-start | bytes 3145732
